TPU v7x, 32 devices: a whole 2x2x4 slice. The times are simulated.
32 devices in a mesh: dp: 8 (over y, x, core), mp: 4 (over z).
Axes of the slice: x: 2, y: 2, z: 4, core: 2. Of those that a mesh axis runs over, the one named last changes fastest.
Arguments:
- inputs: bfloat16 [8, 1024, 1024], P('dp'), may hold values from -6 to 6
- encoder: bfloat16 [8, 2048, 1024], P('dp'), may hold values from -6 to 6
- prefix: int32 [8], P('dp'), may hold values from 102 to 512, as said below
- cotangent: bfloat16 [8, 1024, 1024], P('dp'), may hold values from -6 to 6
- inner_weights: float32 [2, 3, 1024, 1024], P(None, None, 'dp', 'mp')
- inner_first: float32 [2, 3, 1024, 1024], P(None, None, 'dp', 'mp')
- inner_second: float32 [2, 3, 1024, 1024], P(None, None, 'dp', 'mp'), may hold values from 4423.68 to 17694.72
- outer_weights: float32 [2, 1024, 1024], P(None, 'mp', 'dp')
- outer_first: float32 [2, 1024, 1024], P(None, 'mp', 'dp')
- outer_second: float32 [2, 1024, 1024], P(None, 'mp', 'dp')
- expand_weights: float32 [1024, 4096], P('dp', 'mp')
- expand_first: float32 [1024, 4096], P('dp', 'mp')
- expand_second: float32 [1024, 4096], P('dp', 'mp'), may hold values from 630.784 to 2539.52
- shrink_weights: float32 [4096, 1024], P('mp', 'dp')
- shrink_first: float32 [4096, 1024], P('mp', 'dp')
- shrink_second: float32 [4096, 1024], P('mp', 'dp'), may hold values from 3522.56 to 13926.4
- norm_params: float32 [2, 3, 1024], P(None, None, 'dp')
- norm_first: float32 [2, 3, 1024], P(None, None, 'dp')
- norm_second: float32 [2, 3, 1024], P(None, None, 'dp'), may hold values from 5464.064 to 21848.064
Outputs:
- layer_out: float32 [8, 1024, 1024], P('dp')
- input_grad: float32 [8, 1024, 1024], P('dp')
- encoder_grad: float32 [8, 2048, 1024], P('dp')
- inner_new: float32 [2, 3, 1024, 1024], P(None, None, 'dp', 'mp')
- outer_new: float32 [2, 1024, 1024], P(None, 'mp', 'dp')
- expand_new: float32 [1024, 4096], P('dp', 'mp')
- shrink_new: float32 [4096, 1024], P('mp', 'dp')
- norm_new: float32 [2, 3, 1024], P(None, None, 'dp')
- inner_first_new: float32 [2, 3, 1024, 1024], P(None, None, 'dp', 'mp')
- outer_first_new: float32 [2, 1024, 1024], P(None, 'mp', 'dp')
- expand_first_new: float32 [1024, 4096], P('dp', 'mp')
- shrink_first_new: float32 [4096, 1024], P('mp', 'dp')
- norm_first_new: float32 [2, 3, 1024], P(None, None, 'dp')
- inner_second_new: float32 [2, 3, 1024, 1024], P(None, None, 'dp', 'mp')
- outer_second_new: float32 [2, 1024, 1024], P(None, 'mp', 'dp')
- expand_second_new: float32 [1024, 4096], P('dp', 'mp')
- shrink_second_new: float32 [4096, 1024], P('mp', 'dp')
- norm_second_new: float32 [2, 3, 1024], P(None, None, 'dp')
- trust_table: float32 [3, 16], replicated
Inputs may be any that keep to these rules, and one draw needn't show every extreme that they name: `prefix`: prefix lengths; in every draw one sequence has exactly 102 and one exactly 512.
All inputs are finite; a program needn't handle non-finite values.
Results may differ from a plain program's by a relative error of at most 0.034.
Values may be sent and summed in bfloat16 or wider, within the bound.
A program may use at most 192 MiB of HBM per device.

v0:
```python
from functools import partial

import jax
import jax.numpy as jnp
from jax import lax
from jax.sharding import PartitionSpec as P

D = 1024
HEAD = 64
FF = 4096
STEP = 5


first_decay = 0.5
second_decay = 0.6
learn_rate = 0.5
weight_decay = 0.01
epsilon = 1e-06
norm_eps = 1e-05
mask_fill = -1000000000.0


def contract_rows(left, right):
    return lax.dot_general(
        left, right, (((0,), (0,)), ((), ())), preferred_element_type=jnp.float32
    )


def contract_cols(left, right):
    return lax.dot_general(
        left, right, (((1,), (1,)), ((), ())), preferred_element_type=jnp.float32
    )


def layer_norm(values, gain_row, bias_row):
    center = values - jnp.mean(values, axis=-1, keepdims=True)
    spread = jnp.mean(center * center, axis=-1, keepdims=True)
    inverse = lax.rsqrt(spread + norm_eps)
    normed = center * inverse
    return (normed * gain_row + bias_row, normed, inverse)


def norm_back(upstream, normed, inverse, gain_row):
    scaled = upstream * gain_row
    inner = (
        scaled
        - jnp.mean(scaled, axis=-1, keepdims=True)
        - normed * jnp.mean(scaled * normed, axis=-1, keepdims=True)
    )
    return (inner * inverse, jnp.sum(upstream * normed, axis=0), jnp.sum(upstream, axis=0))


def score_block(query_rows, key_rows, row_start, prefix_len, masked):
    scores = jnp.einsum(
        "qhd,khd->hqk", query_rows, key_rows, preferred_element_type=jnp.float32
    ) * HEAD ** (-0.5)
    if masked:
        row_ids = row_start + lax.broadcasted_iota(jnp.int32, scores.shape[1:], 0)
        col_ids = lax.broadcasted_iota(jnp.int32, scores.shape[1:], 1)
        allowed = (col_ids <= row_ids) | (col_ids < prefix_len)
        scores = jnp.where(allowed[None], scores, mask_fill)
    return scores


def attend_forward(query, key_rows, value_rows, prefix_len, masked):
    row_total, local_width = query.shape
    head_count = local_width // HEAD
    query_heads = query.reshape(row_total, head_count, HEAD)
    key_heads = key_rows.reshape(-1, head_count, HEAD)
    value_heads = value_rows.reshape(-1, head_count, HEAD)
    block_rows = min(512, row_total)

    def one_block(block_index):
        row_start = block_index * block_rows
        query_rows = lax.dynamic_slice_in_dim(query_heads, row_start, block_rows, 0)
        scores = score_block(query_rows, key_heads, row_start, prefix_len, masked)
        row_max = jnp.max(scores, axis=-1, keepdims=True)
        powered = jnp.exp(scores - row_max)
        totals = jnp.sum(powered, axis=-1, keepdims=True)
        attn_probs = (powered / totals).astype(jnp.bfloat16)
        mixed_out = jnp.einsum(
            "hqk,khd->qhd", attn_probs, value_heads, preferred_element_type=jnp.float32
        )
        return (
            mixed_out.astype(jnp.bfloat16).reshape(block_rows, local_width),
            (row_max + jnp.log(totals))[..., 0],
        )

    mixed_out, log_sums = lax.map(one_block, jnp.arange(row_total // block_rows))
    return (mixed_out.reshape(row_total, local_width), log_sums)


def attend_backward(query, key_rows, value_rows, grad_out, log_sums, prefix_len, masked):
    row_total, local_width = query.shape
    head_count = local_width // HEAD
    factor = HEAD ** (-0.5)
    query_heads = query.reshape(row_total, head_count, HEAD)
    grad_heads = grad_out.reshape(row_total, head_count, HEAD)
    key_heads = key_rows.reshape(-1, head_count, HEAD)
    value_heads = value_rows.reshape(-1, head_count, HEAD)
    block_rows = min(512, row_total)

    def one_block(running, block_index):
        key_grad, value_grad = running
        row_start = block_index * block_rows
        query_rows = lax.dynamic_slice_in_dim(query_heads, row_start, block_rows, 0)
        grad_rows = lax.dynamic_slice_in_dim(grad_heads, row_start, block_rows, 0)
        scores = score_block(query_rows, key_heads, row_start, prefix_len, masked)
        attn_probs = jnp.exp(scores - log_sums[block_index][..., None])
        prob_low = attn_probs.astype(jnp.bfloat16)
        prob_grad = jnp.einsum(
            "qhd,khd->hqk", grad_rows, value_heads, preferred_element_type=jnp.float32
        )
        row_delta = jnp.sum(attn_probs * prob_grad, axis=-1, keepdims=True)
        score_grad = (attn_probs * (prob_grad - row_delta)).astype(jnp.bfloat16)
        query_grad = (
            jnp.einsum("hqk,khd->qhd", score_grad, key_heads, preferred_element_type=jnp.float32)
            * factor
        )
        key_grad = (
            key_grad
            + jnp.einsum("hqk,qhd->khd", score_grad, query_rows, preferred_element_type=jnp.float32)
            * factor
        )
        value_grad = value_grad + jnp.einsum(
            "hqk,qhd->khd", prob_low, grad_rows, preferred_element_type=jnp.float32
        )
        return (
            (key_grad, value_grad),
            query_grad.astype(jnp.bfloat16).reshape(block_rows, local_width),
        )

    zero_grad = jnp.zeros(key_heads.shape, jnp.float32)
    (key_grad, value_grad), query_grad = lax.scan(
        one_block, (zero_grad, zero_grad), jnp.arange(row_total // block_rows)
    )
    return (
        query_grad.reshape(row_total, local_width),
        key_grad.astype(jnp.bfloat16).reshape(-1, local_width),
        value_grad.astype(jnp.bfloat16).reshape(-1, local_width),
    )


def moments(upstream, first_moment, second_moment, master, decay):
    first_new = first_decay * first_moment + (1.0 - first_decay) * upstream
    second_new = second_decay * second_moment + (1.0 - second_decay) * upstream * upstream
    direction = (
        first_new
        / (1.0 - first_decay**STEP)
        / (jnp.sqrt(second_new / (1.0 - second_decay**STEP)) + epsilon)
        + decay * master
    )
    return (first_new, second_new, direction)


def squares(inner, outer, expand, shrink, norms, norm_share):
    return jnp.concatenate(
        [
            jnp.sum(inner * inner, axis=(2, 3)).reshape(6),
            jnp.sum(outer * outer, axis=(1, 2)),
            jnp.sum(expand * expand)[None],
            jnp.sum(shrink * shrink)[None],
            jnp.sum(norms * norms, axis=2).reshape(6) * norm_share,
        ]
    )


def entry_counts():
    return jnp.array([D * D] * 8 + [D * FF] * 2 + [D] * 6, dtype=jnp.float32)


def on_device(
    inputs,
    encoder,
    prefix,
    cotangent,
    inner_weights,
    inner_first,
    inner_second,
    outer_weights,
    outer_first,
    outer_second,
    expand_weights,
    expand_first,
    expand_second,
    shrink_weights,
    shrink_first,
    shrink_second,
    norm_params,
    norm_first,
    norm_second,
):
    seq_count, seq_len, model_width = inputs.shape
    enc_len = encoder.shape[1]
    inner_all, outer_all, expand_all, shrink_all, norm_all = (
        lax.all_gather(inner_weights.astype(jnp.bfloat16), "dp", axis=2, tiled=True),
        lax.all_gather(outer_weights.astype(jnp.bfloat16), "dp", axis=2, tiled=True),
        lax.all_gather(expand_weights.astype(jnp.bfloat16), "dp", axis=0, tiled=True),
        lax.all_gather(shrink_weights.astype(jnp.bfloat16), "dp", axis=1, tiled=True),
        lax.all_gather(norm_params.astype(jnp.bfloat16), "dp", axis=2, tiled=True),
    )
    gains = norm_all[0].astype(jnp.float32)
    biases = norm_all[1].astype(jnp.float32)
    local_width = inner_all.shape[3]
    tokens = inputs.reshape(seq_count * seq_len, model_width)
    states = encoder.reshape(seq_count * enc_len, model_width)

    def run_forward(query, key_rows, value_rows, masked):

        def one_seq(member):
            return attend_forward(member[0], member[1], member[2], member[3], masked)

        mixed_out, log_sums = lax.map(
            one_seq,
            (
                query.reshape(seq_count, seq_len, local_width),
                key_rows.reshape(seq_count, -1, local_width),
                value_rows.reshape(seq_count, -1, local_width),
                prefix,
            ),
        )
        return (mixed_out.reshape(-1, local_width), log_sums)

    def run_backward(query, key_rows, value_rows, grad_out, log_sums, masked):

        def one_seq(member):
            return attend_backward(
                member[0], member[1], member[2], member[3], member[4], member[5], masked
            )

        results = lax.map(
            one_seq,
            (
                query.reshape(seq_count, seq_len, local_width),
                key_rows.reshape(seq_count, -1, local_width),
                value_rows.reshape(seq_count, -1, local_width),
                grad_out.reshape(seq_count, seq_len, local_width),
                log_sums,
                prefix,
            ),
        )
        return tuple((piece.reshape(-1, local_width) for piece in results))

    self_proj = jnp.einsum(
        "td,cdm->ctm", tokens, inner_all[0], preferred_element_type=jnp.float32
    ).astype(jnp.bfloat16)
    self_mixed, self_sums = run_forward(self_proj[0], self_proj[1], self_proj[2], True)
    self_branch = lax.psum(
        jnp.dot(self_mixed, outer_all[0], preferred_element_type=jnp.float32), "mp"
    )
    hidden_one, normed_one, inverse_one = layer_norm(
        tokens.astype(jnp.float32) + self_branch, gains[0], biases[0]
    )
    hidden_one_low = hidden_one.astype(jnp.bfloat16)
    cross_query = jnp.dot(
        hidden_one_low, inner_all[1, 0], preferred_element_type=jnp.float32
    ).astype(jnp.bfloat16)
    cross_source = jnp.einsum(
        "td,cdm->ctm", states, inner_all[1, 1:], preferred_element_type=jnp.float32
    ).astype(jnp.bfloat16)
    cross_mixed, cross_sums = run_forward(cross_query, cross_source[0], cross_source[1], False)
    cross_branch = lax.psum(
        jnp.dot(cross_mixed, outer_all[1], preferred_element_type=jnp.float32).astype(jnp.bfloat16),
        "mp",
    ).astype(jnp.float32)
    hidden_two, normed_two, inverse_two = layer_norm(hidden_one + cross_branch, gains[1], biases[1])
    hidden_two_low = hidden_two.astype(jnp.bfloat16)
    pre_act = jnp.dot(hidden_two_low, expand_all, preferred_element_type=jnp.float32)
    activation = jax.nn.gelu(pre_act, approximate=False).astype(jnp.bfloat16)
    mlp_branch = lax.psum(
        jnp.dot(activation, shrink_all, preferred_element_type=jnp.float32).astype(jnp.bfloat16),
        "mp",
    ).astype(jnp.float32)
    output, normed_three, inverse_three = layer_norm(hidden_two + mlp_branch, gains[2], biases[2])
    grad_third, gain_three, bias_three = norm_back(
        cotangent.reshape(-1, model_width).astype(jnp.float32),
        normed_three,
        inverse_three,
        gains[2],
    )
    grad_mlp = grad_third.astype(jnp.bfloat16)
    shrink_grad = contract_rows(activation, grad_mlp)
    gelu_out, gelu_pull = jax.vjp(partial(jax.nn.gelu, approximate=False), pre_act)
    pre_grad = gelu_pull(contract_cols(grad_mlp, shrink_all))[0].astype(jnp.bfloat16)
    expand_grad = contract_rows(hidden_two_low, pre_grad)
    grad_two = grad_third + lax.psum(
        contract_cols(pre_grad, expand_all).astype(jnp.bfloat16), "mp"
    ).astype(jnp.float32)
    grad_second, gain_two, bias_two = norm_back(grad_two, normed_two, inverse_two, gains[1])
    cross_grad = grad_second.astype(jnp.bfloat16)
    cross_outer_grad = contract_rows(cross_mixed, cross_grad)
    cross_mixed_grad = contract_cols(cross_grad, outer_all[1]).astype(jnp.bfloat16)
    cross_query_grad, cross_key_grad, cross_value_grad = run_backward(
        cross_query, cross_source[0], cross_source[1], cross_mixed_grad, cross_sums, False
    )
    cross_inner_grad = jnp.stack(
        [
            contract_rows(hidden_one_low, cross_query_grad),
            contract_rows(states, cross_key_grad),
            contract_rows(states, cross_value_grad),
        ]
    )
    hidden_part = contract_cols(cross_query_grad, inner_all[1, 0])
    state_part = contract_cols(cross_key_grad, inner_all[1, 1]) + contract_cols(
        cross_value_grad, inner_all[1, 2]
    )
    hidden_sum, encoder_grad = (
        lax.psum(hidden_part.astype(jnp.bfloat16), "mp").astype(jnp.float32),
        lax.psum(state_part.astype(jnp.bfloat16), "mp").astype(jnp.float32),
    )
    grad_one = grad_second + hidden_sum
    grad_first, gain_one, bias_one = norm_back(grad_one, normed_one, inverse_one, gains[0])
    self_grad = grad_first.astype(jnp.bfloat16)
    self_outer_grad = contract_rows(self_mixed, self_grad)
    self_mixed_grad = contract_cols(self_grad, outer_all[0]).astype(jnp.bfloat16)
    self_grads = jnp.stack(
        run_backward(self_proj[0], self_proj[1], self_proj[2], self_mixed_grad, self_sums, True)
    )
    self_inner_grad = jnp.einsum(
        "td,ctm->cdm", tokens, self_grads, preferred_element_type=jnp.float32
    )
    input_part = jnp.einsum(
        "ctm,cdm->td", self_grads, inner_all[0], preferred_element_type=jnp.float32
    )
    norm_grad = jnp.stack(
        [jnp.stack([gain_one, gain_two, gain_three]), jnp.stack([bias_one, bias_two, bias_three])]
    )
    input_grad = grad_first + lax.psum(input_part.astype(jnp.bfloat16), "mp").astype(jnp.float32)
    inner_grad = jnp.stack([self_inner_grad, cross_inner_grad])
    outer_grad = jnp.stack([self_outer_grad, cross_outer_grad])
    inner_grad, outer_grad, expand_grad, shrink_grad, norm_grad = (
        lax.psum_scatter(
            inner_grad.astype(jnp.bfloat16), "dp", scatter_dimension=2, tiled=True
        ).astype(jnp.float32),
        lax.psum_scatter(
            outer_grad.astype(jnp.bfloat16), "dp", scatter_dimension=2, tiled=True
        ).astype(jnp.float32),
        lax.psum_scatter(
            expand_grad.astype(jnp.bfloat16), "dp", scatter_dimension=0, tiled=True
        ).astype(jnp.float32),
        lax.psum_scatter(
            shrink_grad.astype(jnp.bfloat16), "dp", scatter_dimension=1, tiled=True
        ).astype(jnp.float32),
        lax.psum_scatter(
            norm_grad.astype(jnp.bfloat16), "dp", scatter_dimension=2, tiled=True
        ).astype(jnp.float32),
    )
    inner_f, inner_s, inner_d = moments(
        inner_grad, inner_first, inner_second, inner_weights, weight_decay
    )
    outer_f, outer_s, outer_d = moments(
        outer_grad, outer_first, outer_second, outer_weights, weight_decay
    )
    expand_f, expand_s, expand_d = moments(
        expand_grad, expand_first, expand_second, expand_weights, weight_decay
    )
    shrink_f, shrink_s, shrink_d = moments(
        shrink_grad, shrink_first, shrink_second, shrink_weights, weight_decay
    )
    norm_f, norm_s, norm_d = moments(norm_grad, norm_first, norm_second, norm_params, 0.0)
    norm_share = 1.0 / lax.axis_size("mp")
    weight_local = squares(
        inner_weights, outer_weights, expand_weights, shrink_weights, norm_params, norm_share
    )
    update_local = squares(inner_d, outer_d, expand_d, shrink_d, norm_d, norm_share)
    weight_total, update_total = lax.psum((weight_local, update_local), ("dp", "mp"))
    counts_all = entry_counts()
    weight_norm = jnp.sqrt(weight_total / counts_all)
    update_norm = jnp.sqrt(update_total / counts_all)
    trust = weight_norm / (update_norm + epsilon)
    inner_new = inner_weights - learn_rate * trust[0:6].reshape(2, 3, 1, 1) * inner_d
    outer_new = outer_weights - learn_rate * trust[6:8].reshape(2, 1, 1) * outer_d
    expand_new = expand_weights - learn_rate * trust[8] * expand_d
    shrink_new = shrink_weights - learn_rate * trust[9] * shrink_d
    norm_new = norm_params - learn_rate * trust[10:16].reshape(2, 3, 1) * norm_d
    table = jnp.stack([weight_norm, update_norm, trust])
    return (
        output.reshape(seq_count, seq_len, model_width),
        input_grad.reshape(seq_count, seq_len, model_width),
        encoder_grad.reshape(seq_count, enc_len, model_width),
        inner_new,
        outer_new,
        expand_new,
        shrink_new,
        norm_new,
        inner_f,
        outer_f,
        expand_f,
        shrink_f,
        norm_f,
        inner_s,
        outer_s,
        expand_s,
        shrink_s,
        norm_s,
        table,
    )


def solution(mesh):
    placed = (
        P("dp", None, None),
        P("dp", None, None),
        P("dp"),
        P("dp", None, None),
        P(None, None, "dp", "mp"),
        P(None, None, "dp", "mp"),
        P(None, None, "dp", "mp"),
        P(None, "mp", "dp"),
        P(None, "mp", "dp"),
        P(None, "mp", "dp"),
        P("dp", "mp"),
        P("dp", "mp"),
        P("dp", "mp"),
        P("mp", "dp"),
        P("mp", "dp"),
        P("mp", "dp"),
        P(None, None, "dp"),
        P(None, None, "dp"),
        P(None, None, "dp"),
    )
    return jax.shard_map(
        on_device,
        mesh=mesh,
        in_specs=placed,
        out_specs=(
            P("dp", None, None),
            P("dp", None, None),
            P("dp", None, None),
            P(None, None, "dp", "mp"),
            P(None, "mp", "dp"),
            P("dp", "mp"),
            P("mp", "dp"),
            P(None, None, "dp"),
            P(None, None, "dp", "mp"),
            P(None, "mp", "dp"),
            P("dp", "mp"),
            P("mp", "dp"),
            P(None, None, "dp"),
            P(None, None, "dp", "mp"),
            P(None, "mp", "dp"),
            P("dp", "mp"),
            P("mp", "dp"),
            P(None, None, "dp"),
            P(),
        ),
        check_vma=False,
    )
```

profile of v0, /device:TPU:0, one launch (start us, length us, event | category | flops | bytes accessed | tf_op | source)
XLA Modules:
  0.0 1257.6 jit_solution(5806136408818106561)
XLA Ops:
  11.3 34.7 %all-gather.5.cloned.1.call-done = bf16[2,3,1024,256]{2,3,1,0:T(8,128)(2,1)} async-done(((bf16[2,3,128,256]{2,3,1,0:T(8,128)(2,1)}), bf16[2,3,1024,256]{2,3,1,0:T(8,128)(2,1)}) %all-gather.5.cloned.1.call-update) | async-done | bytes 3145744 | tf_op jit(solution)/shard_map/all_gather | solution.py:196
  46.0 3.9 fusion.109
  50.1 19.0 %while.94 = (s32[]{:T(128)}, bf16[2,512,256]{2,1,0:T(8,128)(2,1)S(1)}, f32[2,4,512]{2,1,0:T(4,128)S(1)}, s32[2]{0:T(128)S(1)}, s32[]{:T(128)}, /*index=5*/bf16[1...) while((s32[]{:T(128)}, ...), condition=%wide.region_3.4_spmd, body=%wide.region_0.3_spmd.sunk | while | flops 563215872 | bytes 29956300 | solution.py:89
  72.1 3.8 fusion.141
  77.2 8.9 all_gather.17
  86.8 4.9 fusion.93
  91.8 139.2 %all-reduce.9.cloned.1.call-done = f32[1024,1024]{1,0:T(8,128)} async-done(((f32[1024,1024]{1,0:T(8,128)}), f32[1024,1024]{1,0:T(8,128)}) %all-reduce.9.cloned.1.call-update) | async-done | bytes 4194320 | tf_op jit(solution)/shard_map/psum | solution.py:248
  231.0 3.3 fusion.165
  239.4 24.8 %while.95 = (s32[]{:T(128)}, bf16[2,512,256]{2,1,0:T(8,128)(2,1)}, f32[2,4,512]{2,1,0:T(4,128)S(1)}, s32[2]{0:T(128)S(1)}, bf16[1024,4,64]{0,2,1:T(8,128)(2,1)S(...) while((s32[]{:T(128)}, bf16[2,512,256]{2,1,0:T(8,128)(2,1)}, ...), condition=%wide.region_10.11_spmd, body=%wide.region_7.10_spmd.sunk | while | flops 1111619584 | bytes 54067384 | solution.py:89
  243.1 3.3 fusion.250
  246.4 4.5 fusion.251
  255.5 3.3 fusion.250
  258.8 4.5 fusion.251
  264.2 3.3 convolution_convert_fusion.5
  270.4 82.7 %all-reduce.11.cloned.1.call-done = bf16[1024,1024]{1,0:T(8,128)(2,1)} async-done(((bf16[1024,1024]{1,0:T(8,128)(2,1)}), bf16[1024,1024]{1,0:T(8,128)(2,1)}) %all-reduce.11.cloned.1.call-update) | async-done | bytes 2097168 | tf_op jit(solution)/shard_map/psum | solution.py:262
  353.2 3.7 fusion.164
  359.4 23.0 %all-gather.9.cloned.1.call-done = bf16[1024,1024]{1,0:T(8,128)(2,1)} async-done(((bf16[128,1024]{1,0:T(8,128)(2,1)}), bf16[1024,1024]{1,0:T(8,128)(2,1)}) %all-gather.9.cloned.1.call-update) | async-done | bytes 2097168 | tf_op jit(solution)/shard_map/all_gather | solution.py:198
  382.4 15.6 %multiply_convert_fusion.2 = (bf16[1024,1024]{1,0:T(8,128)(2,1)}, f32[1024,1024]{1,0:T(8,128)}, f32[1024,1024]{1,0:T(8,128)}) fusion(bf16[1024,1024]{1,0:T(8,128)(2,1)} %all-gather.9.cloned.1.call-done, f32[1024,1024]{1,0:T(8,128)} %copy-done.6, f32[1024]{0:T(1024)S(1)} %bitcast.330, f32[1024]{0:T(1024)S(1)} %bitcast.320, f32[1024]{0:T(1024)S(1)} %add_rsqrt_fusion.1, ...), kind=kOutput, calls=%fused_computation.120 | convolution fusion | flops 2220883968 | bytes 16793600 | tf_op jit(solution)/shard_map/dot_general | solution.py:268
  398.0 15.0 %all-gather.11.cloned.1.call-done = bf16[1024,1024]{1,0:T(8,128)(2,1)} async-done(((bf16[1024,128]{1,0:T(8,128)(2,1)}), bf16[1024,1024]{1,0:T(8,128)(2,1)}) %all-gather.11.cloned.1.call-update) | async-done | bytes 2097168 | tf_op jit(solution)/shard_map/all_gather | solution.py:199
  412.9 5.9 convolution_convert_fusion.4
  419.3 86.2 %all-reduce.13.cloned.1.call-done = bf16[1024,1024]{1,0:T(8,128)(2,1)} async-done(((bf16[1024,1024]{1,0:T(8,128)(2,1)}), bf16[1024,1024]{1,0:T(8,128)(2,1)}) %all-reduce.13.cloned.1.call-update) | async-done | bytes 2097168 | tf_op jit(solution)/shard_map/psum | solution.py:270
  505.5 3.7 fusion.162
  513.5 3.2 fusion.72
  520.5 3.5 add_convert_fusion.1
  525.3 3.7 convolution_convert_fusion.3
  529.1 85.5 %all-reduce.15.cloned.1.call-done = bf16[1024,1024]{1,0:T(8,128)(2,1)} async-done(((bf16[1024,1024]{1,0:T(8,128)(2,1)}), bf16[1024,1024]{1,0:T(8,128)(2,1)}) %all-reduce.15.cloned.1.call-update) | async-done | bytes 2097168 | tf_op jit(solution)/shard_map/psum | solution.py:286
  614.7 5.9 multiply_reduce_fusion.3
  627.0 82.8 %while.96 = (s32[]{:T(128)}, f32[2048,4,64]{0,2,1:T(8,128)}, f32[2048,4,64]{0,2,1:T(8,128)}, bf16[2,512,256]{2,1,0:T(8,128)(2,1)}, s32[2]{0:T(128)S(1)}, /*index...) while((s32[]{:T(128)}, f32[2048,4,64]{0,2,1:T(8,128)}, ...), condition=%wide.region_24.25_spmd.clone, body=%wide.region_22.24_spmd.clone.sunk | while | flops 2737567744 | bytes 173334832 | solution.py:134
  632.8 4.4 fusion.263
  637.2 7.9 multiply_reduce_fusion.26
  645.1 10.4 multiply_convert_fusion.5
  655.5 6.9 fusion.264
  672.7 5.6 fusion.263
  678.3 7.9 multiply_reduce_fusion.26
  686.2 10.4 multiply_convert_fusion.5
  696.6 6.9 fusion.264
  703.5 4.5 fusion.262
  709.8 3.2 convolution_convert_fusion.2
  713.5 5.2 convolution_convert_fusion
  723.6 7.0 convolution_convert_fusion.1
  732.5 3.9 fusion.118
  744.1 54.7 %all-reduce.17.cloned.1.call-done = bf16[1024,1024]{1,0:T(8,128)(2,1)} async-done(((bf16[1024,1024]{1,0:T(8,128)(2,1)}), bf16[1024,1024]{1,0:T(8,128)(2,1)}) %all-reduce.17.cloned.1.call-update) | async-done | bytes 2097168 | tf_op jit(solution)/shard_map/psum | solution.py:308
  798.7 5.1 multiply_reduce_fusion.4
  805.4 5.4 subtract_multiply_fusion
  818.4 3.8 convolution_convert_fusion.9
  823.1 40.7 %while.97 = (s32[]{:T(128)}, f32[1024,4,64]{0,2,1:T(8,128)S(1)}, f32[1024,4,64]{0,2,1:T(8,128)}, bf16[2,512,256]{2,1,0:T(8,128)(2,1)}, s32[2]{0:T(128)S(1)}, /*i...) while((s32[]{:T(128)}, f32[1024,4,64]{0,2,1:T(8,128)S(1)}, ...), condition=%wide.region_30.31_spmd.clone, body=%wide.region_28.30_spmd.clone.sunk | while | flops 1376255488 | bytes 73201960 | solution.py:134
  828.9 4.5 fusion.277
  833.3 4.4 multiply_reduce_fusion.27
  848.9 4.8 fusion.277
  853.7 4.4 multiply_reduce_fusion.27
  866.6 3.6 fusion.106
  870.5 5.7 copy.134
  876.2 9.5 reshape.427
  888.6 3.4 fusion.89
  891.9 3.1 bitcast_convert_fusion
  900.5 3.4 multiply_reduce_fusion.14
  904.0 3.5 multiply_reduce_fusion.15
  907.5 16.8 %reduce-scatter.22.cloned.1.call-done = bf16[128,6]{1,0:T(8,128)(2,1)} async-done(((bf16[1024,6]{1,0:T(8,128)(2,1)}), bf16[128,6]{1,0:T(8,128)(2,1)}) %reduce-scatter.22.cloned.1.call-update) | async-done | bytes 1552
  926.8 36.8 %reduce-scatter.18.cloned.1.call-done = bf16[128,512]{1,0:T(8,128)(2,1)} async-done(((bf16[1024,512]{1,0:T(8,128)(2,1)}), bf16[128,512]{1,0:T(8,128)(2,1)}) %reduce-scatter.18.cloned.1.call-update) | async-done | bytes 131088
  971.0 42.1 %reduce-scatter.16.cloned.1.call-done = bf16[128,1536]{1,0:T(8,128)(2,1)} async-done(((bf16[1024,1536]{1,0:T(8,128)(2,1)}), bf16[128,1536]{1,0:T(8,128)(2,1)}) %reduce-scatter.16.cloned.1.call-update) | async-done | bytes 393232
  1022.8 47.9 %all-reduce = (f32[16]{0:T(128)S(1)}, f32[16]{0:T(128)S(1)}) all-reduce(f32[16]{0:T(128)S(1)} %concatenate.6, f32[16]{0:T(128)S(1)} %concatenate.7), channel_id=1, replica_groups=mesh['dp'=8,'mp'=4] {'dp','mp'}, use_global_device_ids=true, to_apply=%region_38.39 | all-reduce | flops 32 | bytes 256 | tf_op jit(solution)/shard_map/psum | solution.py:366
  1084.7 155.6 %all-reduce.19.cloned.1.call-done = (bf16[1024,1024]{1,0:T(8,128)(2,1)}, bf16[1,2048,1024]{2,1,0:T(8,128)(2,1)}) async-done(((bf16[1024,1024]{1,0:T(8,128)(2,1)}, bf16[1,2048,1024]{2,1,0:T(8,128)(2,1)}), (bf16[1024,1024]{1,0:T(8,128)(2,1)}, bf16[1,2048,1024]{2,1,0:T(8,128)(2,1)})) %all-reduce.19.cloned.1.call-update) | async-done | bytes 6291472 | tf_op jit(solution)/shard_map/psum | solution.py:328
  1240.3 6.1 add_bitcast_fusion
  1246.4 4.4 reshape.421
  (383 shorter events, 158.9 us)
Async XLA Ops:
  7.2 38.8 %all-gather.5.cloned.1.call-start = ((), (), s32[]{:S(2)}) async-start(), calls=%async_computation.5 | async-start | bytes 3538944 | tf_op jit(solution)/shard_map/all_gather | solution.py:196
  8.6 37.4 %copy-start.16 = (f32[2,3,128,256]{2,3,1,0:T(8,128)}, f32[2,3,128,256]{2,3,1,0:T(8,128)S(1)}, u32[]{:S(2)}) copy-start(f32[2,3,128,256]{2,3,1,0:T(8,128)S(1)} %copy.104) | copy-start | bytes 2359300
  9.6 62.5 %all-gather.7.cloned.1.call-start = ((), (), s32[]{:S(2)}) async-start(), calls=%async_computation.6 | async-start | bytes 1179648 | tf_op jit(solution)/shard_map/all_gather | solution.py:197
  11.3 219.8 %all-reduce.9.cloned.1.call-start = ((), (), s32[]{:S(2)}) async-start(), calls=%async_computation.7 | async-start | bytes 8388608 | tf_op jit(solution)/shard_map/psum | solution.py:248
  69.1 6.7 copy-start.2
  69.2 6.7 copy-start.9
  69.2 6.7 copy-start.13
  69.2 6.7 copy-start.19
  69.2 6.7 copy-start.46
  75.9 277.3 %all-reduce.11.cloned.1.call-start = ((), (), s32[]{:S(2)}) async-start(), calls=%async_computation.8 | async-start | bytes 4194304 | tf_op jit(solution)/shard_map/psum | solution.py:262
  86.8 148.2 %copy-start.51 = (f32[1,1,1024]{2,0,1:T(1,128)}, f32[1,1,1024]{2,0,1:T(1,128)S(1)}, u32[]{:S(2)}) copy-start(f32[1,1,1024]{2,0,1:T(1,128)S(1)} %get-tuple-element.597) | copy-start | bytes 12292
  86.8 148.2 %copy-start.63 = (f32[1,1,1024]{2,0,1:T(1,128)}, f32[1,1,1024]{2,0,1:T(1,128)S(1)}, u32[]{:S(2)}) copy-start(f32[1,1,1024]{2,0,1:T(1,128)S(1)} %get-tuple-element.615) | copy-start | bytes 12292
  264.2 5.2 copy-start.24
  264.2 89.0 %copy-start.49 = (f32[1024]{0:T(1024)S(1)}, f32[1024]{0:T(1024)}, u32[]{:S(2)}) copy-start(f32[1024]{0:T(1024)} %copy-done.48) | copy-start | bytes 12292
  264.2 89.0 %copy-start.52 = (f32[1,1,1024]{2,0,1:T(1,128)S(1)}, f32[1,1,1024]{2,0,1:T(1,128)}, u32[]{:S(2)}) copy-start(f32[1,1,1024]{2,0,1:T(1,128)} %copy-done.51) | copy-start | bytes 12292
  264.2 89.0 %copy-start.55 = (f32[1024]{0:T(1024)S(1)}, f32[1024]{0:T(1024)}, u32[]{:S(2)}) copy-start(f32[1024]{0:T(1024)} %copy-done.54) | copy-start | bytes 12292
  264.2 89.0 %copy-start.64 = (f32[1,1,1024]{2,0,1:T(1,128)S(1)}, f32[1,1,1024]{2,0,1:T(1,128)}, u32[]{:S(2)}) copy-start(f32[1,1,1024]{2,0,1:T(1,128)} %copy-done.63) | copy-start | bytes 12292
  267.5 114.9 %all-gather.9.cloned.1.call-start = ((), (), s32[]{:S(2)}) async-start(), calls=%async_computation.9 | async-start | bytes 2359296 | tf_op jit(solution)/shard_map/all_gather | solution.py:198
  269.4 143.5 %all-gather.11.cloned.1.call-start = ((), (), s32[]{:S(2)}) async-start(), calls=%async_computation.10 | async-start | bytes 2359296 | tf_op jit(solution)/shard_map/all_gather | solution.py:199
  270.2 235.3 %all-reduce.13.cloned.1.call-start = ((), (), s32[]{:S(2)}) async-start(), calls=%async_computation.11 | async-start | bytes 4194304 | tf_op jit(solution)/shard_map/psum | solution.py:270
  356.9 25.5 %copy-start.59 = (f32[1,1,1024]{2,0,1:T(1,128)S(1)}, f32[1,1,1024]{2,0,1:T(1,128)}, u32[]{:S(2)}) copy-start(f32[1,1,1024]{2,0,1:T(1,128)} %get-tuple-element.596) | copy-start | bytes 12292
  356.9 25.5 %copy-start.68 = (f32[1,1,1024]{2,0,1:T(1,128)S(1)}, f32[1,1,1024]{2,0,1:T(1,128)}, u32[]{:S(2)}) copy-start(f32[1,1,1024]{2,0,1:T(1,128)} %get-tuple-element.616) | copy-start | bytes 12292
  356.9 263.6 %copy-start.57 = (f32[1024]{0:T(1024)}, f32[1024]{0:T(1024)S(1)}, u32[]{:S(2)}) copy-start(f32[1024]{0:T(1024)S(1)} %broadcast_multiply_fusion.7) | copy-start | bytes 12292
  359.4 261.1 %copy-start.61 = (f32[1024]{0:T(1024)}, f32[1024]{0:T(1024)S(1)}, u32[]{:S(2)}) copy-start(f32[1024]{0:T(1024)S(1)} %add_rsqrt_fusion.1) | copy-start | bytes 12292
  418.8 195.8 %all-reduce.15.cloned.1.call-start = ((), (), s32[]{:S(2)}) async-start(), calls=%async_computation.12 | async-start | bytes 4194304 | tf_op jit(solution)/shard_map/psum | solution.py:286
  513.5 7.1 copy-start.83
  516.7 7.4 copy-start.11
  529.1 269.7 %all-reduce.17.cloned.1.call-start = ((), (), s32[]{:S(2)}) async-start(), calls=%async_computation.13 | async-start | bytes 4194304 | tf_op jit(solution)/shard_map/psum | solution.py:308
  614.6 5.9 copy-start.7
  614.7 6.5 copy-start.12
  614.7 7.1 copy-start.18
  655.5 6.9 copy-start
  696.6 6.9 copy-start
  713.1 186.3 %reduce-scatter.20.cloned.1.call-start = ((), (), s32[]{:S(2)}) async-start(), calls=%async_computation.17 | async-start | bytes 2359296
  718.8 4.8 copy-start.58
  718.8 4.8 copy-start.60
  718.8 4.8 copy-start.62
  721.5 182.4 %reduce-scatter.14.cloned.1.call-start = ((), (), s32[]{:S(2)}) async-start(), calls=%async_computation.14 | async-start | bytes 2359296 | tf_op jit(solution)/shard_map/reduce_scatter | solution.py:338
  730.7 193.7 %reduce-scatter.22.cloned.1.call-start = ((), (), s32[]{:S(2)}) async-start(), calls=%async_computation.18 | async-start | bytes 294912
  732.4 5.7 copy-start.22
  732.5 6.7 copy-start.79
  741.3 57.5 %copy-start.50 = (f32[1024]{0:T(1024)S(1)}, f32[1024]{0:T(1024)}, u32[]{:S(2)}) copy-start(f32[1024]{0:T(1024)} %copy-done.48) | copy-start | bytes 12292
  741.3 57.4 %copy-start.53 = (f32[1,1,1024]{2,0,1:T(1,128)S(1)}, f32[1,1,1024]{2,0,1:T(1,128)}, u32[]{:S(2)}) copy-start(f32[1,1,1024]{2,0,1:T(1,128)} %copy-done.51) | copy-start | bytes 12292
  741.3 57.4 %copy-start.56 = (f32[1024]{0:T(1024)S(1)}, f32[1024]{0:T(1024)}, u32[]{:S(2)}) copy-start(f32[1024]{0:T(1024)} %copy-done.54) | copy-start | bytes 12292
  805.4 7.4 copy-start.20
  813.6 150.0 %reduce-scatter.18.cloned.1.call-start = ((), (), s32[]{:S(2)}) async-start(), calls=%async_computation.16 | async-start | bytes 1179648
  815.8 7.3 copy-start.3
  815.8 7.3 copy-start.10
  815.8 7.3 copy-start.14
  815.8 7.3 copy-start.47
  818.4 194.7 %reduce-scatter.16.cloned.1.call-start = ((), (), s32[]{:S(2)}) async-start(), calls=%async_computation.15 | async-start | bytes 3538944
  876.2 9.8 copy-start.23
  885.8 354.5 %all-reduce.19.cloned.1.call-start = ((), (), s32[]{:S(2)}) async-start(), calls=%async_computation.19 | async-start | bytes 12582912 | tf_op jit(solution)/shard_map/psum | solution.py:328
  895.1 5.5 copy-start.25
  896.2 7.8 copy-start.26
  897.9 27.4 %copy-start.67 = (f32[2,3,128]{2,0,1:T(2,128)S(1)}, f32[2,3,128]{2,0,1:T(2,128)}, u32[]{:S(2)}) copy-start(f32[2,3,128]{2,0,1:T(2,128)} %param.44) | copy-start | bytes 9220
  897.9 27.4 %copy-start.75 = (f32[2,3,128]{2,0,1:T(2,128)S(1)}, f32[2,3,128]{2,0,1:T(2,128)}, u32[]{:S(2)}) copy-start(f32[2,3,128]{2,0,1:T(2,128)} %param.46) | copy-start | bytes 9220
  897.9 27.4 %copy-start.76 = (f32[2,3,128]{2,0,1:T(2,128)S(1)}, f32[2,3,128]{2,0,1:T(2,128)}, u32[]{:S(2)}) copy-start(f32[2,3,128]{2,0,1:T(2,128)} %param.45) | copy-start | bytes 9220
  904.0 113.5 %copy-start.17 = (f32[2,3,128,256]{2,3,1,0:T(8,128)S(1)}, f32[2,3,128,256]{2,3,1,0:T(8,128)}, u32[]{:S(2)}) copy-start(f32[2,3,128,256]{2,3,1,0:T(8,128)} %copy-done.16) | copy-start | bytes 2359300
  968.9 51.7 %copy-start.78 = (f32[6]{0:T(128)S(1)}, f32[6]{0:T(128)}, u32[]{:S(2)}) copy-start(f32[6]{0:T(128)} %mul.575) | copy-start | bytes 76
  968.9 101.8 %copy-start.77 = (f32[16]{0:T(128)S(1)}, f32[16]{0:T(128)}, u32[]{:S(2)}) copy-start(f32[16]{0:T(128)} %constant.308) | copy-start | bytes 196
  1020.6 57.7 %copy-start.33 = (f32[2,3,128,256]{2,3,1,0:T(8,128)S(1)}, f32[2,3,128,256]{2,3,1,0:T(8,128)}, u32[]{:S(2)}) copy-start(f32[2,3,128,256]{2,3,1,0:T(8,128)} %get-tuple-element.588) | copy-start | bytes 2359300
  1074.8 9.0 copy-start.36
  1240.3 6.1 copy-start.28
  (37 other events, 96.4 us)
Sparse Core Ops, SparseCore 0:
  10.5 35.5 all-gather.4
  48.5 23.5 all-gather.6
  76.0 154.9 all-reduce.8
  267.6 85.5 all-reduce.10
  355.5 26.8 all-gather.8
  384.7 28.1 all-gather.10
  418.9 86.4 all-reduce.12
  529.2 85.4 all-reduce.14
  713.2 85.4 all-reduce.16
  802.2 40.2 reduce-scatter.19
  845.8 41.1 reduce-scatter.13
  890.7 33.5 reduce-scatter.21
  927.5 35.9 reduce-scatter.17
  966.8 46.2 reduce-scatter.15
  1016.1 224.1 all-reduce.18
where the time goes:
time: 1260 us
  waiting for transfers between devices  775 us (62%)
  matrix products  187 us (15%)
  other arithmetic  123 us (10%)
  local copies, waits for them, and re-layouts  83.2 us (7%)
  blocking collectives  56.8 us (5%)
  between operations  16.7 us (1%)
  loops' own time  13.7 us (1%)
    psum x1, waiting for transfers between devices, on_device(): lax.psum(input_part.astype(jnp.bfloat16), 'mp').astype(jnp.float32)  156 us
    psum x1, waiting for transfers between devices, on_device(): lax.psum(jnp.dot(self_mixed, outer_all[0], preferred_element_type=jnp.flo...  139 us
    unnamed x19, waiting for transfers between devices  96 us
    psum x1, waiting for transfers between devices, on_device(): lax.psum(jnp.dot(activation, shrink_all, preferred_element_type=jnp.float...  86.2 us
    psum x1, waiting for transfers between devices, on_device(): lax.psum(contract_cols(pre_grad, expand_all).astype(jnp.bfloat16), 'mp')  85.5 us
    psum x1, waiting for transfers between devices, on_device(): lax.psum(jnp.dot(cross_mixed, outer_all[1], preferred_element_type=jnp.fl...  82.7 us
    unnamed x191, local copies, waits for them, and re-layouts  60.8 us
    psum x1, waiting for transfers between devices, on_device(): lax.psum(hidden_part.astype(jnp.bfloat16), 'mp').astype(jnp.float32)  54.7 us
  transfers between devices with their start and end apart: 15, of which 13 were waited for; matrix products, arithmetic and copies ran while one was open for 17% of the time, Pallas kernels for 0%

commit v1 on v0

v1 whole, which is shorter than its diff:
```python
from functools import partial

import jax
import jax.numpy as jnp
from jax import lax
from jax.experimental import pallas as pl
from jax.experimental.pallas import tpu as pltpu
from jax.sharding import PartitionSpec as P

D = 1024
HEAD = 64
FF = 4096
STEP = 5

first_decay = 0.5
second_decay = 0.6
learn_rate = 0.5
weight_decay = 0.01
epsilon = 1e-06
norm_eps = 1e-05
mask_fill = -1000000000.0

MESH = pl.DeviceIdType.MESH
ANYWHERE = pl.BlockSpec(memory_space=pl.ANY)
IN_VMEM = pl.BlockSpec(memory_space=pltpu.VMEM)
NN = (((1,), (0,)), ((), ()))
NT = (((1,), (1,)), ((), ()))
TN = (((0,), (0,)), ((), ()))
VMEM_LIMIT = 58 << 20


def dot(left, right, dims=NN):
    return lax.dot_general(left, right, dims, preferred_element_type=jnp.float32)


def bf16(values):
    return values.astype(jnp.bfloat16)


def f32(values):
    return values.astype(jnp.float32)


def layer_norm(values, gain_row, bias_row):
    center = values - jnp.mean(values, axis=-1, keepdims=True)
    spread = jnp.mean(center * center, axis=-1, keepdims=True)
    inverse = lax.rsqrt(spread + norm_eps)
    normed = center * inverse
    return (normed * gain_row + bias_row, normed, inverse)


def norm_back(upstream, normed, inverse, gain_row):
    scaled = upstream * gain_row
    inner = (
        scaled
        - jnp.mean(scaled, axis=-1, keepdims=True)
        - normed * jnp.mean(scaled * normed, axis=-1, keepdims=True)
    )
    return (
        inner * inverse,
        jnp.sum(upstream * normed, axis=0, keepdims=True),
        jnp.sum(upstream, axis=0, keepdims=True),
    )


def sizes_of(total, block, limit):
    groups = {}
    for index in range(total // block):
        groups.setdefault(limit(index), []).append(index)
    return groups.items()


def forward_kernel(masked, block, prefix_ref, q_ref, k_ref, v_ref, mixed_ref, sums_ref):
    width = q_ref.shape[1]
    heads = width // HEAD
    keys_total = k_ref.shape[0]
    step = pl.program_id(0)
    lane = lax.broadcasted_iota(jnp.int32, (block, width), 1) // HEAD

    def run(keys, start):
        query = q_ref[...] * jnp.bfloat16(HEAD**-0.5)
        key_rows = k_ref[:keys, :]
        value_rows = v_ref[:keys, :]
        if masked:
            rows = start + lax.broadcasted_iota(jnp.int32, (block, keys), 0)
            cols = lax.broadcasted_iota(jnp.int32, (block, keys), 1)
            allowed = (cols <= rows) | (cols < prefix_ref[0])
        mixed = jnp.zeros((block, width), jnp.float32)
        slot = lax.broadcasted_iota(jnp.int32, (block, 128), 1)
        table = jnp.zeros((block, 128), jnp.float32)
        for head in range(heads):
            scores = dot(jnp.where(lane == head, query, jnp.bfloat16(0)), key_rows, NT)
            if masked:
                scores = jnp.where(allowed, scores, mask_fill)
            row_max = jnp.max(scores, axis=1, keepdims=True)
            powered = jnp.exp(scores - row_max)
            totals = jnp.sum(powered, axis=1, keepdims=True)
            part = dot(bf16(powered), value_rows) * (1.0 / totals)
            mixed = jnp.where(lane == head, part, mixed)
            table = jnp.where(slot == head, row_max + jnp.log(totals), table)
        mixed_ref[...] = bf16(mixed)
        sums_ref[...] = table.T[:8, :]

    if masked:
        limit = lambda index: max(keys_total // 2, (index + 1) * block)
        for keys, blocks in sizes_of(keys_total, block, limit):

            @pl.when((step >= blocks[0]) & (step <= blocks[-1]))
            def _(keys=keys):
                run(keys, step * block)
    else:
        run(keys_total, 0)


def attend_forward(query, key_rows, value_rows, prefix, masked, block=512):
    total, width = query.shape
    keys = key_rows.shape[0]
    block = min(block, total)
    whole = pl.BlockSpec((keys, width), lambda i, p: (0, 0))
    return pl.pallas_call(
        partial(forward_kernel, masked, block),
        grid_spec=pltpu.PrefetchScalarGridSpec(
            num_scalar_prefetch=1,
            grid=(total // block,),
            in_specs=[pl.BlockSpec((block, width), lambda i, p: (i, 0)), whole, whole],
            out_specs=[
                pl.BlockSpec((block, width), lambda i, p: (i, 0)),
                pl.BlockSpec((8, block), lambda i, p: (0, i)),
            ],
        ),
        out_shape=[
            jax.ShapeDtypeStruct((total, width), jnp.bfloat16),
            jax.ShapeDtypeStruct((8, total), jnp.float32),
        ],
        compiler_params=pltpu.CompilerParams(vmem_limit_bytes=VMEM_LIMIT),
        cost_estimate=pl.CostEstimate(
            flops=16 * total * keys * width, bytes_accessed=4 * keys * width, transcendentals=0
        ),
        name="attend_forward",
    )(prefix, query, key_rows, value_rows)


def backward_kernel(
    masked, block, prefix_ref, q_ref, k_ref, v_ref, do_ref, o_ref, sums_ref,
    dq_ref, dk_ref, dv_ref, acc, delta,
):
    width = q_ref.shape[1]
    heads = width // HEAD
    total = q_ref.shape[0]
    step = pl.program_id(0)
    factor = HEAD**-0.5

    @pl.when(step == 0)
    def _():
        product = f32(do_ref[...]) * f32(o_ref[...])
        row = lax.broadcasted_iota(jnp.int32, (8, width), 0)
        col = lax.broadcasted_iota(jnp.int32, (8, width), 1) // HEAD
        pick = jnp.where(row == col, 1.0, 0.0).astype(jnp.float32)
        delta[...] = lax.dot_general(
            pick, product, NT, precision=lax.Precision.HIGHEST, preferred_element_type=jnp.float32
        )
        acc[...] = jnp.zeros_like(acc)

    lane = lax.broadcasted_iota(jnp.int32, (block, width), 1) // HEAD

    def run(first):
        count = total - first
        query = q_ref[first:, :]
        grad_rows = do_ref[first:, :]
        scaled_keys = k_ref[...] * jnp.bfloat16(factor)
        value_rows = v_ref[...]
        if masked:
            rows = first + lax.broadcasted_iota(jnp.int32, (block, count), 1)
            cols = step * block + lax.broadcasted_iota(jnp.int32, (block, count), 0)
            allowed = (cols <= rows) | (cols < prefix_ref[0])
        key_grad = jnp.zeros((block, width), jnp.float32)
        value_grad = jnp.zeros((block, width), jnp.float32)
        query_grad = jnp.zeros((count, width), jnp.float32)
        for head in range(heads):
            own_keys = jnp.where(lane == head, scaled_keys, jnp.bfloat16(0))
            scores = dot(own_keys, query, NT)
            if masked:
                scores = jnp.where(allowed, scores, mask_fill)
            probs = jnp.exp(scores - sums_ref[head : head + 1, first:])
            prob_grad = dot(jnp.where(lane == head, value_rows, jnp.bfloat16(0)), grad_rows, NT)
            score_grad = bf16(probs * (prob_grad - delta[head : head + 1, first:]))
            value_grad = jnp.where(lane == head, dot(bf16(probs), grad_rows), value_grad)
            key_grad = jnp.where(lane == head, dot(score_grad, query), key_grad)
            query_grad = query_grad + dot(score_grad, own_keys, TN)
        acc[first:, :] += query_grad
        dk_ref[...] = bf16(key_grad * factor)
        dv_ref[...] = bf16(value_grad)

    if masked:
        limit = lambda index: 0 if index * block < total // 2 else index * block
        for first, blocks in sizes_of(total, block, limit):

            @pl.when((step >= blocks[0]) & (step <= blocks[-1]))
            def _(first=first):
                run(first)
    else:
        run(0)

    @pl.when(step == pl.num_programs(0) - 1)
    def _():
        dq_ref[...] = bf16(acc[...])


def attend_backward(query, key_rows, value_rows, grad_out, mixed, sums, prefix, masked, block=512):
    total, width = query.shape
    keys = key_rows.shape[0]
    whole = pl.BlockSpec((total, width), lambda i, p: (0, 0))
    part = pl.BlockSpec((block, width), lambda i, p: (i, 0))
    return pl.pallas_call(
        partial(backward_kernel, masked, block),
        grid_spec=pltpu.PrefetchScalarGridSpec(
            num_scalar_prefetch=1,
            grid=(keys // block,),
            in_specs=[
                whole, part, part, whole, whole, pl.BlockSpec((8, total), lambda i, p: (0, 0)),
            ],
            out_specs=[whole, part, part],
            scratch_shapes=[
                pltpu.VMEM((total, width), jnp.float32),
                pltpu.VMEM((8, total), jnp.float32),
            ],
        ),
        out_shape=[jax.ShapeDtypeStruct((total, width), jnp.bfloat16)]
        + [jax.ShapeDtypeStruct((keys, width), jnp.bfloat16)] * 2,
        compiler_params=pltpu.CompilerParams(vmem_limit_bytes=VMEM_LIMIT),
        cost_estimate=pl.CostEstimate(
            flops=40 * total * keys * width, bytes_accessed=4 * keys * width, transcendentals=0
        ),
        name="attend_backward",
    )(prefix, query, key_rows, value_rows, grad_out, mixed, sums)


def greet(n):
    me = lax.axis_index("mp")
    barrier = pltpu.get_barrier_semaphore()
    for distance in range(1, n):
        pl.semaphore_signal(
            barrier, inc=1, device_id={"mp": lax.rem(me + distance, n)}, device_id_type=MESH
        )
    pl.semaphore_wait(barrier, n - 1)


def push(source, target, send_sem, recv_sem, to):
    copy = pltpu.make_async_remote_copy(
        source, target, send_sem, recv_sem, device_id={"mp": to}, device_id_type=MESH
    )
    copy.start()
    return copy


def rows_at(index, size):
    return pl.ds(pl.multiple_of(index * size, size), size)


def heads_to_tokens(n, source, slots, send_sems, recv_sems):
    me = lax.axis_index("mp")
    size = source.shape[0] // n
    copies = []
    for distance in range(1, n):
        to = lax.rem(me + distance, n)
        copies.append(
            push(
                source.at[rows_at(to, size)], slots.at[me],
                send_sems.at[distance - 1], recv_sems.at[distance - 1], to,
            )
        )
    return copies


def tokens_to_heads(n, make, block, target, send_sems, recv_sems, local_sem):
    me = lax.axis_index("mp")
    size, width = block.shape[0], block.shape[1] // n
    copies = []
    for distance in (*range(1, n), 0):
        to = lax.rem(me + distance, n)
        cols = rows_at(to, width)
        block[:, cols] = bf16(make(cols))
        place = target.at[rows_at(me, size)]
        if distance:
            copies.append(
                push(
                    block.at[:, cols], place,
                    send_sems.at[distance - 1], recv_sems.at[distance - 1], to,
                )
            )
        else:
            copy = pltpu.make_async_copy(block.at[:, cols], place, local_sem)
            copy.start()
            copies.append(copy)
    return copies


def merge_heads(n, local, slots, copies, weights_of, start):
    me = lax.axis_index("mp")
    total = start + weights_of(local, me)
    for distance in range(1, n):
        origin = lax.rem(me + n - distance, n)
        copies[distance - 1].wait_recv()
        total = total + weights_of(slots[origin], origin)
    for copy in copies:
        copy.wait_send()
    return total


def self_to_cross_kernel(
    n, mixed_ref, wo_ref, wq_ref, x_ref, gain_ref, bias_ref,
    hidden_ref, normed_ref, inverse_ref, slots_ref, q_ref,
    wo, wq, x_rows, block, wo_sem, wq_sem, x_sem, own_sem, send_in, recv_in, send_out, recv_out,
):
    me = lax.axis_index("mp")
    size = x_rows.shape[0]
    loads = [
        pltpu.make_async_copy(mixed_ref.at[rows_at(me, size)], slots_ref.at[me], own_sem),
        pltpu.make_async_copy(wo_ref, wo, wo_sem),
        pltpu.make_async_copy(x_ref.at[rows_at(me, size)], x_rows, x_sem),
        pltpu.make_async_copy(wq_ref, wq, wq_sem),
    ]
    for load in loads:
        load.start()
    greet(n)
    copies = heads_to_tokens(n, mixed_ref, slots_ref, send_in, recv_in)
    for load in loads:
        load.wait()
    width = mixed_ref.shape[1]
    branch = merge_heads(
        n, slots_ref[me], slots_ref, copies,
        lambda part, group: dot(part, wo[rows_at(group, width), :]), f32(x_rows[...]),
    )
    hidden, normed, inverse = layer_norm(branch, gain_ref[0:1, :], bias_ref[0:1, :])
    hidden_ref[...] = hidden
    normed_ref[...] = normed
    inverse_ref[...] = jnp.broadcast_to(inverse, inverse_ref.shape)
    low = bf16(hidden)
    sent = tokens_to_heads(
        n, lambda cols: dot(low, wq[:, cols]), block, q_ref, send_out, recv_out, own_sem
    )
    for copy in sent:
        copy.wait()


def self_to_cross(n, mixed, wo, wq, tokens, gains, biases):
    total, width = mixed.shape
    size, model = total // n, tokens.shape[1]
    shape = jax.ShapeDtypeStruct
    dma = pltpu.SemaphoreType.DMA
    return pl.pallas_call(
        partial(self_to_cross_kernel, n),
        out_shape=[
            shape((size, model), jnp.float32),
            shape((size, model), jnp.float32),
            shape((size, 128), jnp.float32),
            shape((n, size, width), jnp.bfloat16),
            shape((total, width), jnp.bfloat16),
        ],
        in_specs=[ANYWHERE] * 4 + [IN_VMEM] * 2,
        out_specs=[IN_VMEM] * 4 + [ANYWHERE],
        scratch_shapes=[
            pltpu.VMEM((model, model), jnp.bfloat16),
            pltpu.VMEM((model, model), jnp.bfloat16),
            pltpu.VMEM((size, model), jnp.bfloat16),
            pltpu.VMEM((size, model), jnp.bfloat16),
            dma, dma, dma, dma,
            dma((n - 1,)), dma((n - 1,)), dma((n - 1,)), dma((n - 1,)),
        ],
        compiler_params=pltpu.CompilerParams(
            collective_id=1, has_side_effects=True, vmem_limit_bytes=VMEM_LIMIT
        ),
        cost_estimate=pl.CostEstimate(
            flops=30 * 10**9, bytes_accessed=8 * total * width, transcendentals=0
        ),
        name="self_to_cross",
    )(mixed, wo, wq, tokens, gains, biases)


def feed_kernel(
    n, mixed_ref, wo_ref, expand_ref, shrink_ref, hidden_one_ref, cot_ref, gain_ref, bias_ref,
    out_ref, second_ref, dmix_ref, shrink_grad_ref, expand_grad_ref, wo_grad_ref, norm_grad_ref,
    wo, expand, shrink, slots, hidden_two, normed_two, low_two, low_three, act, slope,
    y_own, y_send, y_recv, d_send, d_recv, cot, block,
    load_sems, own_sem, send_in, recv_in, send_out, recv_out, pair_send, pair_recv,
):
    me = lax.axis_index("mp")
    mate = me + 1 - 2 * lax.rem(me, 2)
    size = cot.shape[0]
    half = size // 2
    width = mixed_ref.shape[1]
    hidden_units = act.shape[1]
    chunk = min(512, hidden_units)
    loads = [
        pltpu.make_async_copy(mixed_ref.at[rows_at(me, size)], slots.at[me], load_sems.at[0]),
        pltpu.make_async_copy(wo_ref, wo, load_sems.at[1]),
        pltpu.make_async_copy(expand_ref, expand, load_sems.at[2]),
        pltpu.make_async_copy(shrink_ref, shrink, load_sems.at[3]),
        pltpu.make_async_copy(cot_ref.at[rows_at(me, size)], cot, load_sems.at[4]),
    ]
    for load in loads:
        load.start()
    greet(n)
    copies = heads_to_tokens(n, mixed_ref, slots, send_in, recv_in)
    loads[0].wait()
    loads[1].wait()
    branch = merge_heads(
        n, slots[me], slots, copies,
        lambda part, group: dot(part, wo[rows_at(group, width), :]), hidden_one_ref[...],
    )
    hidden, normed, inverse_two = layer_norm(branch, gain_ref[1:2, :], bias_ref[1:2, :])
    hidden_two[...] = hidden
    normed_two[...] = normed
    low_two[:size, :] = bf16(hidden)
    own, other = pl.ds(0, size), pl.ds(size, size)
    pair = []

    def to_mate(source, target):
        index = len(pair)
        pair.append(push(source, target, pair_send.at[index], pair_recv.at[index], mate))
        return pair[-1]

    hidden_copy = to_mate(low_two.at[own], low_two.at[other])
    loads[2].wait()

    def expand_rows(start, count):
        rows = low_two[start : start + count, :]
        for first in range(0, hidden_units, chunk):
            pre = dot(rows, expand[:, first : first + chunk])
            cdf = 0.5 + 0.5 * lax.erf(pre * 0.7071067811865476)
            act[start : start + count, first : first + chunk] = bf16(pre * cdf)
            slope[start : start + count, first : first + chunk] = bf16(
                cdf + pre * jnp.exp(-0.5 * pre * pre) * 0.3989422804014327
            )

    expand_rows(0, size)
    loads[3].wait()
    hidden_copy.wait_recv()
    y_copies = []
    for start in (0, half):
        expand_rows(size + start, half)
        y_send[start : start + half, :] = bf16(
            dot(act[size + start : size + start + half, :], shrink[...])
        )
        y_copies.append(to_mate(y_send.at[pl.ds(start, half)], y_recv.at[pl.ds(start, half)]))
    y_own[...] = dot(act[:size, :], shrink[...])
    for copy in y_copies:
        copy.wait_recv()
    output, normed, inverse = layer_norm(
        hidden_two[...] + y_own[...] + f32(y_recv[...]), gain_ref[2:3, :], bias_ref[2:3, :]
    )
    out_ref[...] = bf16(output)
    loads[4].wait()
    third, gain_three, bias_three = norm_back(f32(cot[...]), normed, inverse, gain_ref[2:3, :])
    low_three[:size, :] = bf16(third)
    grad_copy = to_mate(low_three.at[own], low_three.at[other])

    def back_rows(start, count):
        rows = low_three[start : start + count, :]
        for first in range(0, hidden_units, chunk):
            grad = dot(rows, shrink[first : first + chunk, :], NT)
            spot = (slice(start, start + count), slice(first, first + chunk))
            slope[spot] = bf16(grad * f32(slope[spot]))

    back_rows(0, size)
    grad_copy.wait_recv()
    d_copies = []
    for start in (0, half):
        back_rows(size + start, half)
        d_send[start : start + half, :] = bf16(
            dot(slope[size + start : size + start + half, :], expand[...], NT)
        )
        d_copies.append(to_mate(d_send.at[pl.ds(start, half)], d_recv.at[pl.ds(start, half)]))
    y_own[...] = third + dot(slope[:size, :], expand[...], NT)
    for copy in d_copies:
        copy.wait_recv()
    second, gain_two, bias_two = norm_back(
        y_own[...] + f32(d_recv[...]), normed_two[...], inverse_two, gain_ref[1:2, :]
    )
    second_ref[...] = second
    low = bf16(second)
    sent = tokens_to_heads(
        n, lambda cols: dot(low, wo[cols, :], NT), block, dmix_ref, send_out, recv_out, own_sem
    )
    norm_grad_ref[...] = jnp.concatenate(
        [gain_two, gain_three, bias_two, bias_three, jnp.zeros((4, norm_grad_ref.shape[1]))], axis=0
    )
    for first in range(0, hidden_units, chunk):
        shrink_grad_ref[first : first + chunk, :] = bf16(
            dot(act[:, first : first + chunk], low_three[...], TN)
        )
    for first in range(0, low_two.shape[1], 256):
        expand_grad_ref[first : first + 256, :] = bf16(
            dot(low_two[:, first : first + 256], slope[...], TN)
        )
    for group in range(n):
        wo_grad_ref[group * width : (group + 1) * width, :] = bf16(dot(slots[group], low, TN))
    for copy in sent:
        copy.wait()
    for copy in pair:
        copy.wait_send()


def feed(n, mixed, wo, expand, shrink, hidden_one, cotangent, gains, biases):
    total, width = mixed.shape
    model, units = expand.shape
    size = total // n
    shape = jax.ShapeDtypeStruct
    dma = pltpu.SemaphoreType.DMA
    low, wide = jnp.bfloat16, jnp.float32
    return pl.pallas_call(
        partial(feed_kernel, n),
        out_shape=[
            shape((size, model), low),
            shape((size, model), wide),
            shape((total, width), low),
            shape((units, model), low),
            shape((model, units), low),
            shape((model, model), low),
            shape((8, model), wide),
        ],
        in_specs=[ANYWHERE] * 4 + [IN_VMEM, ANYWHERE] + [IN_VMEM] * 2,
        out_specs=[IN_VMEM] * 2 + [ANYWHERE] + [IN_VMEM] * 4,
        scratch_shapes=[
            pltpu.VMEM((model, model), low),
            pltpu.VMEM((model, units), low),
            pltpu.VMEM((units, model), low),
            pltpu.VMEM((n, size, width), low),
            pltpu.VMEM((size, model), wide),
            pltpu.VMEM((size, model), wide),
            pltpu.VMEM((2 * size, model), low),
            pltpu.VMEM((2 * size, model), low),
            pltpu.VMEM((2 * size, units), low),
            pltpu.VMEM((2 * size, units), low),
            pltpu.VMEM((size, model), wide),
            pltpu.VMEM((size, model), low),
            pltpu.VMEM((size, model), low),
            pltpu.VMEM((size, model), low),
            pltpu.VMEM((size, model), low),
            pltpu.VMEM((size, model), low),
            pltpu.VMEM((size, model), low),
            dma((5,)), dma,
            dma((n - 1,)), dma((n - 1,)), dma((n - 1,)), dma((n - 1,)),
            dma((6,)), dma((6,)),
        ],
        compiler_params=pltpu.CompilerParams(
            collective_id=2, has_side_effects=True, vmem_limit_bytes=VMEM_LIMIT
        ),
        cost_estimate=pl.CostEstimate(
            flops=80 * 10**9, bytes_accessed=8 * total * width, transcendentals=0
        ),
        name="feed",
    )(mixed, wo, expand, shrink, hidden_one, cotangent, gains, biases)


def cross_to_self_kernel(
    n, dq_ref, wo_ref, wq_ref, second_ref, hidden_ref, normed_ref, inverse_ref, mixed_ref, gain_ref,
    first_ref, dmix_ref, wq_grad_ref, wo_grad_ref, norm_grad_ref,
    wo, wq, slots, block, wo_sem, wq_sem, own_sem, send_in, recv_in, send_out, recv_out,
):
    me = lax.axis_index("mp")
    size, model = block.shape
    width = dq_ref.shape[1]
    loads = [
        pltpu.make_async_copy(dq_ref.at[rows_at(me, size)], slots.at[me], own_sem),
        pltpu.make_async_copy(wq_ref, wq, wq_sem),
        pltpu.make_async_copy(wo_ref, wo, wo_sem),
    ]
    for load in loads:
        load.start()
    greet(n)
    copies = heads_to_tokens(n, dq_ref, slots, send_in, recv_in)
    for load in loads:
        load.wait()
    upstream = merge_heads(
        n, slots[me], slots, copies,
        lambda part, group: dot(part, wq[:, rows_at(group, width)], NT), second_ref[...],
    )
    first, gain_one, bias_one = norm_back(
        upstream, normed_ref[...], inverse_ref[:, 0:1], gain_ref[0:1, :]
    )
    first_ref[...] = first
    low = bf16(first)
    sent = tokens_to_heads(
        n, lambda cols: dot(low, wo[cols, :], NT), block, dmix_ref, send_out, recv_out, own_sem
    )
    norm_grad_ref[...] = jnp.concatenate(
        [gain_one, bias_one, jnp.zeros((6, model), jnp.float32)], axis=0
    )
    hidden_low = bf16(hidden_ref[...])
    for group in range(n):
        cols = slice(group * width, (group + 1) * width)
        wq_grad_ref[:, cols] = bf16(dot(hidden_low, slots[group], TN))
        wo_grad_ref[cols, :] = bf16(dot(mixed_ref[group], low, TN))
    for copy in sent:
        copy.wait()


def cross_to_self(n, dq, wo, wq, second, hidden, normed, inverse, slots, gains):
    total, width = dq.shape
    size, model = second.shape
    shape = jax.ShapeDtypeStruct
    dma = pltpu.SemaphoreType.DMA
    return pl.pallas_call(
        partial(cross_to_self_kernel, n),
        out_shape=[
            shape((size, model), jnp.float32),
            shape((total, width), jnp.bfloat16),
            shape((model, model), jnp.bfloat16),
            shape((model, model), jnp.bfloat16),
            shape((8, model), jnp.float32),
        ],
        in_specs=[ANYWHERE] * 3 + [IN_VMEM] * 6,
        out_specs=[IN_VMEM, ANYWHERE] + [IN_VMEM] * 3,
        scratch_shapes=[
            pltpu.VMEM((model, model), jnp.bfloat16),
            pltpu.VMEM((model, model), jnp.bfloat16),
            pltpu.VMEM((n, size, width), jnp.bfloat16),
            pltpu.VMEM((size, model), jnp.bfloat16),
            dma, dma, dma,
            dma((n - 1,)), dma((n - 1,)), dma((n - 1,)), dma((n - 1,)),
        ],
        compiler_params=pltpu.CompilerParams(
            collective_id=3, has_side_effects=True, vmem_limit_bytes=VMEM_LIMIT
        ),
        cost_estimate=pl.CostEstimate(
            flops=30 * 10**9, bytes_accessed=8 * total * width, transcendentals=0
        ),
        name="cross_to_self",
    )(dq, wo, wq, second, hidden, normed, inverse, slots, gains)


def sum_all_kernel(n_dp, n_mp, mine_ref, total_ref, slots, send_sems, recv_sems):
    n = n_dp * n_mp
    me = lax.axis_index("dp") * n_mp + lax.axis_index("mp")
    barrier = pltpu.get_barrier_semaphore()

    def place(distance):
        to = lax.rem(me + distance, n)
        return {"dp": to // n_mp, "mp": lax.rem(to, n_mp)}

    def signal(distance, carry):
        pl.semaphore_signal(barrier, inc=1, device_id=place(distance), device_id_type=MESH)
        return carry

    lax.fori_loop(1, n, signal, 0)
    pl.semaphore_wait(barrier, n - 1)

    def copy(distance):
        return pltpu.make_async_remote_copy(
            mine_ref, slots.at[me], send_sems.at[distance - 1], recv_sems.at[distance - 1],
            device_id=place(distance), device_id_type=MESH,
        )

    def start(distance, carry):
        copy(distance).start()
        return carry

    def finish(distance, carry):
        copy(distance).wait()
        return carry

    slots[me] = mine_ref[...]
    lax.fori_loop(1, n, start, 0)
    lax.fori_loop(1, n, finish, 0)
    total_ref[...] = jnp.sum(slots[...], axis=0)


def sum_all(n_dp, n_mp, block):
    n = n_dp * n_mp
    dma = pltpu.SemaphoreType.DMA
    return pl.pallas_call(
        partial(sum_all_kernel, n_dp, n_mp),
        out_shape=jax.ShapeDtypeStruct(block.shape, jnp.float32),
        in_specs=[IN_VMEM],
        out_specs=IN_VMEM,
        scratch_shapes=[
            pltpu.VMEM((n,) + block.shape, jnp.float32), dma((n - 1,)), dma((n - 1,)),
        ],
        compiler_params=pltpu.CompilerParams(collective_id=4, has_side_effects=True),
        name="sum_all",
    )(block)


def moments(upstream, first_moment, second_moment, master, decay):
    first_new = first_decay * first_moment + (1.0 - first_decay) * upstream
    second_new = second_decay * second_moment + (1.0 - second_decay) * upstream * upstream
    direction = (
        first_new
        / (1.0 - first_decay**STEP)
        / (jnp.sqrt(second_new / (1.0 - second_decay**STEP)) + epsilon)
        + decay * master
    )
    return (first_new, second_new, direction)


def squares(inner, outer, expand, shrink, norms, norm_share):
    return jnp.concatenate(
        [
            jnp.sum(inner * inner, axis=(2, 3)).reshape(6),
            jnp.sum(outer * outer, axis=(1, 2)),
            jnp.sum(expand * expand)[None],
            jnp.sum(shrink * shrink)[None],
            jnp.sum(norms * norms, axis=2).reshape(6) * norm_share,
        ]
    )


def entry_counts():
    return jnp.array([D * D] * 8 + [D * FF] * 2 + [D] * 6, dtype=jnp.float32)


def swap_far(values, n):
    return lax.ppermute(values, "mp", [(i, (i + n // 2) % n) for i in range(n)])


def on_device(
    inputs,
    encoder,
    prefix,
    cotangent,
    inner_weights,
    inner_first,
    inner_second,
    outer_weights,
    outer_first,
    outer_second,
    expand_weights,
    expand_first,
    expand_second,
    shrink_weights,
    shrink_first,
    shrink_second,
    norm_params,
    norm_first,
    norm_second,
):
    n_dp, n_mp = lax.axis_size("dp"), lax.axis_size("mp")
    seq_count, seq_len, model = inputs.shape
    tokens = inputs.reshape(seq_len, model)
    states = encoder.reshape(-1, model)
    inner_low, outer_low = bf16(inner_weights), bf16(outer_weights)
    expand_low, shrink_low = bf16(expand_weights), bf16(shrink_weights)

    self_weights = lax.all_gather(inner_low[0], "dp", axis=1, tiled=True)
    norm_all = f32(lax.all_gather(bf16(norm_params), "dp", axis=2, tiled=True))
    gains, biases = norm_all[0], norm_all[1]
    outer_all = (
        lax.all_gather(outer_low, ("dp", "mp"))
        .reshape((n_dp, n_mp) + outer_low.shape)
        .transpose(2, 1, 3, 0, 4)
        .reshape(2, model, model)
    )
    query_all = (
        lax.all_gather(inner_low[1, 0], ("dp", "mp"))
        .reshape((n_dp, n_mp) + inner_low.shape[2:])
        .transpose(0, 2, 1, 3)
        .reshape(model, model)
    )
    source_weights = lax.all_gather(inner_low[1, 1:], "dp", axis=1, tiled=True)
    expand_two = lax.all_gather(
        jnp.concatenate([expand_low, swap_far(expand_low, n_mp)], axis=1), "dp", axis=0, tiled=True
    )
    shrink_two = lax.all_gather(
        jnp.concatenate([shrink_low, swap_far(shrink_low, n_mp)], axis=0), "dp", axis=1, tiled=True
    )

    project = lambda rows, weights: bf16(
        jnp.einsum("td,cdm->ctm", rows, weights, preferred_element_type=jnp.float32)
    )
    self_proj = project(tokens, self_weights)
    self_mixed, self_sums = attend_forward(self_proj[0], self_proj[1], self_proj[2], prefix, True)
    hidden_one, normed_one, inverse_one, self_slots, cross_query = self_to_cross(
        n_mp, self_mixed, outer_all[0], query_all, tokens, gains, biases
    )
    source = project(states, source_weights)
    cross_mixed, cross_sums = attend_forward(cross_query, source[0], source[1], prefix, False)
    out_rows, grad_second, cross_dmix, shrink_grad, expand_grad, cross_wo_grad, norm_rows = feed(
        n_mp, cross_mixed, outer_all[1], expand_two, shrink_two, hidden_one,
        cotangent.reshape(seq_len, model), gains, biases,
    )
    layer_out = f32(lax.all_gather(out_rows, "mp", axis=0, tiled=True))
    cross_dq, cross_dk, cross_dv = attend_backward(
        cross_query, source[0], source[1], cross_dmix, cross_mixed, cross_sums, prefix, False
    )
    state_part = dot(cross_dk, source_weights[0], NT) + dot(cross_dv, source_weights[1], NT)
    encoder_grad = f32(lax.psum(bf16(state_part), "mp"))
    source_grad = jnp.stack([dot(states, cross_dk, TN), dot(states, cross_dv, TN)])
    grad_first, self_dmix, query_grad, self_wo_grad, norm_one = cross_to_self(
        n_mp, cross_dq, outer_all[0], query_all, grad_second, hidden_one, normed_one, inverse_one,
        self_slots, gains,
    )
    self_grads = jnp.stack(
        attend_backward(
            self_proj[0], self_proj[1], self_proj[2], self_dmix, self_mixed, self_sums, prefix, True
        )
    )
    self_inner_grad = jnp.einsum(
        "td,ctm->cdm", tokens, self_grads, preferred_element_type=jnp.float32
    )
    input_part = jnp.einsum(
        "ctm,cdm->td", self_grads, self_weights, preferred_element_type=jnp.float32
    )
    input_rows = grad_first + f32(
        lax.psum_scatter(bf16(input_part), "mp", scatter_dimension=0, tiled=True)
    )
    input_grad = f32(lax.all_gather(bf16(input_rows), "mp", axis=0, tiled=True))

    scatter = lambda values, axis, dim: lax.psum_scatter(
        bf16(values), axis, scatter_dimension=dim, tiled=True
    )
    shrink_both = scatter(shrink_grad, "dp", 1)
    expand_both = scatter(expand_grad, "dp", 0)
    units = shrink_low.shape[0]
    shrink_grad = f32(shrink_both[:units]) + f32(swap_far(shrink_both[units:], n_mp))
    expand_grad = f32(expand_both[:, :units]) + f32(swap_far(expand_both[:, units:], n_mp))
    outer_grad = f32(
        scatter(scatter(jnp.stack([self_wo_grad, cross_wo_grad]), "dp", 2), "mp", 1)
    )
    query_grad = f32(scatter(scatter(query_grad, "dp", 0), "mp", 1))
    inner_grad = jnp.stack(
        [
            f32(scatter(self_inner_grad, "dp", 1)),
            jnp.concatenate([query_grad[None], f32(scatter(source_grad, "dp", 1))]),
        ]
    )
    norm_grad = jnp.stack(
        [
            jnp.stack([norm_one[0], norm_rows[0], norm_rows[1]]),
            jnp.stack([norm_one[1], norm_rows[2], norm_rows[3]]),
        ]
    )
    norm_grad = lax.psum(
        lax.psum_scatter(norm_grad, "dp", scatter_dimension=2, tiled=True), "mp"
    )
    inner_f, inner_s, inner_d = moments(
        inner_grad, inner_first, inner_second, inner_weights, weight_decay
    )
    outer_f, outer_s, outer_d = moments(
        outer_grad, outer_first, outer_second, outer_weights, weight_decay
    )
    expand_f, expand_s, expand_d = moments(
        expand_grad, expand_first, expand_second, expand_weights, weight_decay
    )
    shrink_f, shrink_s, shrink_d = moments(
        shrink_grad, shrink_first, shrink_second, shrink_weights, weight_decay
    )
    norm_f, norm_s, norm_d = moments(norm_grad, norm_first, norm_second, norm_params, 0.0)
    norm_share = 1.0 / n_mp
    weight_local = squares(
        inner_weights, outer_weights, expand_weights, shrink_weights, norm_params, norm_share
    )
    update_local = squares(inner_d, outer_d, expand_d, shrink_d, norm_d, norm_share)
    both = jnp.concatenate([weight_local, update_local])
    totals = sum_all(n_dp, n_mp, jnp.zeros((8, 128), jnp.float32).at[0, :32].set(both))
    counts_all = entry_counts()
    weight_norm = jnp.sqrt(totals[0, 0:16] / counts_all)
    update_norm = jnp.sqrt(totals[0, 16:32] / counts_all)
    trust = weight_norm / (update_norm + epsilon)
    inner_new = inner_weights - learn_rate * trust[0:6].reshape(2, 3, 1, 1) * inner_d
    outer_new = outer_weights - learn_rate * trust[6:8].reshape(2, 1, 1) * outer_d
    expand_new = expand_weights - learn_rate * trust[8] * expand_d
    shrink_new = shrink_weights - learn_rate * trust[9] * shrink_d
    norm_new = norm_params - learn_rate * trust[10:16].reshape(2, 3, 1) * norm_d
    table = jnp.stack([weight_norm, update_norm, trust])
    return (
        layer_out.reshape(seq_count, seq_len, model),
        input_grad.reshape(seq_count, seq_len, model),
        encoder_grad.reshape(seq_count, -1, model),
        inner_new,
        outer_new,
        expand_new,
        shrink_new,
        norm_new,
        inner_f,
        outer_f,
        expand_f,
        shrink_f,
        norm_f,
        inner_s,
        outer_s,
        expand_s,
        shrink_s,
        norm_s,
        table,
    )


def solution(mesh):
    placed = (
        P("dp", None, None),
        P("dp", None, None),
        P("dp"),
        P("dp", None, None),
        P(None, None, "dp", "mp"),
        P(None, None, "dp", "mp"),
        P(None, None, "dp", "mp"),
        P(None, "mp", "dp"),
        P(None, "mp", "dp"),
        P(None, "mp", "dp"),
        P("dp", "mp"),
        P("dp", "mp"),
        P("dp", "mp"),
        P("mp", "dp"),
        P("mp", "dp"),
        P("mp", "dp"),
        P(None, None, "dp"),
        P(None, None, "dp"),
        P(None, None, "dp"),
    )
    return jax.shard_map(
        on_device,
        mesh=mesh,
        in_specs=placed,
        out_specs=(
            P("dp", None, None),
            P("dp", None, None),
            P("dp", None, None),
            P(None, None, "dp", "mp"),
            P(None, "mp", "dp"),
            P("dp", "mp"),
            P("mp", "dp"),
            P(None, None, "dp"),
            P(None, None, "dp", "mp"),
            P(None, "mp", "dp"),
            P("dp", "mp"),
            P("mp", "dp"),
            P(None, None, "dp"),
            P(None, None, "dp", "mp"),
            P(None, "mp", "dp"),
            P("dp", "mp"),
            P("mp", "dp"),
            P(None, None, "dp"),
            P(),
        ),
        check_vma=False,
    )
```

time: 1260 us -> 1130 us (0.90)
  Pallas kernels: 0 us -> 227 us
  matrix products: 187 us -> 27.4 us
  other arithmetic: 123 us -> 40.5 us
  waiting for transfers between devices: 775 us -> 696 us
  blocking collectives: 56.8 us -> 20.5 us
  loops' own time: 13.7 us -> 0 us
    psum x6 -> x1, waiting for transfers between devices: 604 us -> 155 us  [on_device(): encoder_grad = f32(lax.psum(bf16(state_part), 'mp'))]
    pallas_call x0 -> x8, Pallas kernels: none -> 227 us  [the longest x1 85.3 us: feed(): pl.pallas_call(partial(feed_kernel, n), out_shape=[shape((size, model), l...]
    dot_general x50 -> x7, matrix products: 183 us -> 22.6 us  [the longest x4 9.89 us: dot(): lax.dot_general(left, right, dims, preferred_element_type=jnp.float32)]
    all_gather x4 -> x8, waiting for transfers between devices: 75.5 us -> 193 us  [the longest x1 59.4 us: on_device(): lax.all_gather(outer_low, ('dp', 'mp'))]
    reduce_scatter x1 -> x5, waiting for transfers between devices: 0.01 us -> 103 us  [the longest x4 92.5 us: on_device(): lax.psum_scatter(bf16(values), axis, scatter_dimension=dim, tiled=True)]
    unnamed x19 -> x24, waiting for transfers between devices: 96 us -> 199 us
    ppermute x0 -> x4, waiting for transfers between devices: none -> 45.9 us  [swap_far(): return lax.ppermute(values, 'mp', [(i, (i + n // 2) % n) for i in range(n)])]
    reduce_sum x14 -> x0, other arithmetic: 39.2 us -> none  [the longest x3 13.7 us: norm_back(): jnp.sum(upstream * normed, axis=0)]
  transfers between devices with their start and end apart: 15 -> 23, of which waited for: 13 -> 20; matrix products, arithmetic and copies ran while one was open for 17% -> 12% of each run, Pallas kernels for 0% -> 7%
where the time goes in v1:
time: 1130 us; the launch traced here: 1120 us
  waiting for transfers between devices  696 us (62%)
  Pallas kernels  227 us (20%)
  local copies, waits for them, and re-layouts  80.2 us (7%)
  other arithmetic  40.5 us (4%)
  matrix products  27.4 us (2%)
  blocking collectives  20.5 us (2%)
  between operations  17.1 us (2%)
    unnamed x24, waiting for transfers between devices  199 us
    psum x1, waiting for transfers between devices, on_device(): encoder_grad = f32(lax.psum(bf16(state_part), 'mp'))  155 us
    reduce_scatter x4, waiting for transfers between devices, on_device(): lax.psum_scatter(bf16(values), axis, scatter_dimension=dim, tiled=True)  92.5 us
    pallas_call x1, Pallas kernels, feed(): pl.pallas_call(partial(feed_kernel, n), out_shape=[shape((size, model), l...  85.3 us
    all_gather x1, waiting for transfers between devices, on_device(): lax.all_gather(outer_low, ('dp', 'mp'))  59.4 us
    unnamed x113, local copies, waits for them, and re-layouts  56 us
    all_gather x1, waiting for transfers between devices, on_device(): lax.all_gather(inner_low[1, 0], ('dp', 'mp'))  47 us
    all_gather x1, waiting for transfers between devices, on_device(): layer_out = f32(lax.all_gather(out_rows, 'mp', axis=0, tiled=True))  46.2 us
  transfers between devices with their start and end apart: 23, of which 20 were waited for; matrix products, arithmetic and copies ran while one was open for 12% of the time, Pallas kernels for 7%

profile of v1, /device:TPU:0, one launch (start us, length us, event | category | flops | bytes accessed | tf_op | source)
XLA Modules:
  0.0 1118.6 jit_solution(11237603327278675870)
XLA Ops:
  12.0 4.1 collective-permute-start
  16.1 11.9 %collective-permute-done = bf16[128,1024]{1,0:T(8,128)(2,1)S(1)} collective-permute-done((bf16[128,1024]{1,0:T(8,128)(2,1)S(1)}, bf16[128,1024]{1,0:T(8,128)(2,1)S(1)}, u32[]{:S(2)}, u32[]{:S(2)}) %collective-permute-start) | collective-permute-done | bytes 262176 | tf_op jit(solution)/shard_map/ppermute | solution.py:714
  29.0 14.0 %collective-permute-done.1 = bf16[1024,128]{1,0:T(8,128)(2,1)S(1)} collective-permute-done((bf16[1024,128]{1,0:T(8,128)(2,1)S(1)}, bf16[1024,128]{1,0:T(8,128)(2,1)S(1)}, u32[]{:S(2)}, u32[]{:S(2)}) %collective-permute-start.1) | collective-permute-done | bytes 262176 | tf_op jit(solution)/shard_map/ppermute | solution.py:714
  45.2 8.6 all_gather.34
  54.5 4.9 fusion.10
  59.4 1.5 slice_bitcast_fusion
  60.9 4.2 all-gather.21.cloned.1.call-done
  65.2 3.2 fusion.28
  69.6 8.6 attend_forward.2
  78.2 47.0 %all-gather.25.cloned.1.call-done = bf16[32,1,128,256]{3,2,1,0:T(8,128)(2,1)} async-done(((bf16[1,1,128,256]{3,2,1,0:T(8,128)(2,1)}), bf16[32,1,128,256]{3,2,1,0:T(8,128)(2,1)}) %all-gather.25.cloned.1.call-update) | async-done | bytes 2097168 | tf_op jit(solution)/shard_map/all_gather | solution.py:755
  125.2 3.2 copy.119
  128.4 1.8 copy.159
  130.2 59.4 %all-gather.23.cloned.1.call-done = bf16[64,256,128]{2,1,0:T(8,128)(2,1)} async-done(((bf16[2,256,128]{2,1,0:T(8,128)(2,1)}), bf16[64,256,128]{2,1,0:T(8,128)(2,1)}) %all-gather.23.cloned.1.call-update) | async-done | bytes 4194320 | tf_op jit(solution)/shard_map/all_gather | solution.py:749
  189.6 4.9 copy.184
  194.8 1.9 copy.186
  196.7 1.9 copy.185
  198.7 28.6 %self_to_cross.1 = (f32[256,1024]{1,0:T(8,128)}, f32[256,1024]{1,0:T(8,128)}, f32[256,128]{1,0:T(8,128)}, bf16[4,256,256]{2,1,0:T(8,128)(2,1)}, bf16[1024,256]{1,0:T(8,128)(2,1)}) custom-call(bf16[1024,256]{1,0:T(8,128)(2,1)} %get-tuple-element.58.mixed_ref.o_ref, bf16[1024,1024]{1,0:T(8,128)(2,1)} %bitcast.168, bf16[1024,1024]{1,0:T(8,128)(2,1)} %bitcast.166, ...), custom_call_target="tpu_custom_call" | custom-call | flops 30000001024 | bytes 2097152 | tf_op jit(solution)/shard_map/self_to_cross/pallas_call | solution.py:351
  227.2 23.5 %attend_forward.3 = (bf16[1024,256]{1,0:T(8,128)(2,1)}, f32[8,1024]{1,0:T(8,128)}) custom-call(s32[1]{0:T(128)S(6)} %copy.188.prefix_ref, bf16[1024,256]{1,0:T(8,128)(2,1)} %get-tuple-element.59.q_ref, bf16[2048,256]{1,0:T(8,128)(2,1)} %get-tuple-element.179.k_ref, bf16[2048,256]{1,0:T(8,128)(2,1)} %get-tuple-element.178.v_ref), custom_call_target="tpu_custom_call" | custom-call | flops 8589934592 | bytes 2097152 | tf_op jit(solution)/shard_map/attend_forward/pallas_call | solution.py:120
  250.8 16.1 %all-gather.15.cloned.1.call-done.shrink_ref = bf16[2048,1024]{1,0:T(8,128)(2,1)} async-done(((bf16[2048,128]{1,0:T(8,128)(2,1)}), bf16[2048,1024]{1,0:T(8,128)(2,1)}) %all-gather.15.cloned.1.call-update) | async-done | bytes 4194320 | tf_op jit(solution)/shard_map/all_gather | solution.py:764
  267.0 85.3 %feed.1 = (bf16[256,1024]{1,0:T(8,128)(2,1)}, f32[256,1024]{1,0:T(8,128)}, bf16[1024,256]{1,0:T(8,128)(2,1)}, bf16[2048,1024]{1,0:T(8,128)(2,1)}, bf16[1024,2048...) custom-call(bf16[1024,256]{1,0:T(8,128)(2,1)} %get-tuple-element.60.mixed_ref.o_ref, ...), custom_call_target="tpu_custom_call" | custom-call | flops 80000000000 | bytes 2097152 | tf_op jit(solution)/shard_map/feed/pallas_call | solution.py:511
  352.3 26.9 %attend_backward.2 = (bf16[1024,256]{1,0:T(8,128)(2,1)}, bf16[2048,256]{1,0:T(8,128)(2,1)}, bf16[2048,256]{1,0:T(8,128)(2,1)}) custom-call(s32[1]{0:T(128)S(6)} %copy.188.prefix_ref, bf16[1024,256]{1,0:T(8,128)(2,1)} %get-tuple-element.59.q_ref, bf16[2048,256]{1,0:T(8,128)(2,1)} %get-tuple-element.179.k_ref, bf16[2048,256]{1,0:T(8,128)(2,1)} %get-tuple-element.178.v_ref, ...), custom_call_target="tpu_custom_call" | custom-call | flops 21474836480 | bytes 2097152 | tf_op jit(solution)/shard_map/attend_backward/pallas_call | solution.py:214
  379.3 30.7 %cross_to_self.1 = (f32[256,1024]{1,0:T(8,128)}, bf16[1024,256]{1,0:T(8,128)(2,1)}, bf16[1024,1024]{1,0:T(8,128)(2,1)}, bf16[1024,1024]{1,0:T(8,128)(2,1)}, f32[8,1024]{1,0:T(8,128)}) custom-call(bf16[1024,256]{1,0:T(8,128)(2,1)} %get-tuple-element.65.dq_ref, bf16[1024,1024]{1,0:T(8,128)(2,1)} %bitcast.169, bf16[1024,1024]{1,0:T(8,128)(2,1)} %bitcast.167, ...), custom_call_target="tpu_custom_call" | custom-call | flops 30000001024 | bytes 2097152 | tf_op jit(solution)/shard_map/cross_to_self/pallas_call | solution.py:604
  410.0 13.3 %attend_backward.3 = (bf16[1024,256]{1,0:T(8,128)(2,1)}, bf16[1024,256]{1,0:T(8,128)(2,1)}, bf16[1024,256]{1,0:T(8,128)(2,1)}) custom-call(s32[1]{0:T(128)S(6)} %copy.188.prefix_ref, bf16[1024,256]{1,0:T(8,128)(2,1)} %get-tuple-element.182.q_ref, bf16[1024,256]{1,0:T(8,128)(2,1)} %get-tuple-element.181.k_ref, bf16[1024,256]{1,0:T(8,128)(2,1)} %get-tuple-element.180.v_ref, ...), custom_call_target="tpu_custom_call" | custom-call | flops 10737418240 | bytes 1048576 | tf_op jit(solution)/shard_map/attend_backward/pallas_call | solution.py:214
  423.3 4.6 bitcast_convert_fusion
  431.0 4.0 fusion.39
  438.9 4.8 fusion.25
  443.7 2.9 copy.146
  446.7 1.5 copy.161
  448.9 3.7 reduce-scatter.23.cloned.1.call-done
  455.1 3.4 fusion.6
  458.6 1.5 copy-done.12
  460.1 4.3 pad_maximum_fusion
  464.4 11.3 %copy.150 = bf16[2,1024,1024]{1,0,2:T(2,128)(2,1)} copy(bf16[2,1024,1024]{2,1,0:T(8,128)(2,1)} %pad_maximum_fusion) | data formatting | bytes 8388608
  475.7 5.6 copy.163
  481.4 6.5 copy.152
  488.1 10.8 reduce-scatter.21.cloned.1.call-done
  498.9 2.1 add_convert_fusion.1
  502.8 33.2 %reduce-scatter.39.cloned.1.call-done = f32[128,6]{1,0:T(8,128)} async-done(((f32[1024,6]{1,0:T(8,128)}), f32[128,6]{1,0:T(8,128)}) %reduce-scatter.39.cloned.1.call-update) | async-done | bytes 3088
  537.0 11.9 %psum.15 = f32[2,3,128]{2,1,0:T(4,128)S(1)} all-reduce(f32[2,3,128]{2,1,0:T(4,128)S(1)} %copy.155), channel_id=1, replica_groups=mesh['dp'=8,'mp'=4] {'mp'}, use_global_device_ids=true, to_apply=%region_20.0 | all-reduce | flops 768 | bytes 6144 | tf_op jit(solution)/shard_map/psum | solution.py:833
  551.1 24.4 %reduce-scatter.33.cloned.1.call-done = bf16[128,512]{1,0:T(8,128)(2,1)} async-done(((bf16[1024,512]{1,0:T(8,128)(2,1)}), bf16[128,512]{1,0:T(8,128)(2,1)}) %reduce-scatter.33.cloned.1.call-update) | async-done | bytes 131088
  576.5 41.0 %reduce-scatter.31.cloned.1.call-done = bf16[128,768]{1,0:T(8,128)(2,1)} async-done(((bf16[1024,768]{1,0:T(8,128)(2,1)}), bf16[128,768]{1,0:T(8,128)(2,1)}) %reduce-scatter.31.cloned.1.call-update) | async-done | bytes 196624
  618.8 46.2 %all-gather.17.cloned.1.call-done = bf16[1024,1024]{1,0:T(8,128)(2,1)} async-done(((bf16[256,1024]{1,0:T(8,128)(2,1)}), bf16[1024,1024]{1,0:T(8,128)(2,1)}) %all-gather.17.cloned.1.call-update) | async-done | bytes 2097168 | tf_op jit(solution)/shard_map/all_gather | solution.py:782
  665.0 4.1 bitcast_convert_fusion.2
  669.1 16.6 %reduce-scatter.25.cloned.1.call-done = bf16[128,256]{1,0:T(8,128)(2,1)} async-done(((bf16[128,1024]{1,0:T(8,128)(2,1)}), bf16[128,256]{1,0:T(8,128)(2,1)}) %reduce-scatter.25.cloned.1.call-update) | async-done | bytes 65552 | tf_op jit(solution)/shard_map/reduce_scatter | solution.py:809
  686.7 51.9 %reduce-scatter.29.cloned.1.call-done = bf16[128,2048]{1,0:T(8,128)(2,1)} async-done(((bf16[1024,2048]{1,0:T(8,128)(2,1)}), bf16[128,2048]{1,0:T(8,128)(2,1)}) %reduce-scatter.29.cloned.1.call-update) | async-done | bytes 524304 | tf_op jit(solution)/shard_map/reduce_scatter | solution.py:809
  738.5 1.7 slice.166
  740.2 2.4 collective-permute-start.2
  742.6 1.8 multiply_reduce_fusion
  744.6 2.3 copy.138
  748.0 154.5 %all-reduce.3.cloned.1.call-done = bf16[1,2048,1024]{2,1,0:T(8,128)(2,1)} async-done(((bf16[1,2048,1024]{2,1,0:T(8,128)(2,1)}), bf16[1,2048,1024]{2,1,0:T(8,128)(2,1)}) %all-reduce.3.cloned.1.call-update) | async-done | bytes 4194320 | tf_op jit(solution)/shard_map/psum | solution.py:787
  902.5 6.6 reshape.159
  909.1 47.0 %reduce-scatter.35.cloned.1.call-done = bf16[128,2048]{1,0:T(8,128)(2,1)} async-done(((bf16[1024,2048]{1,0:T(8,128)(2,1)}), bf16[128,2048]{1,0:T(8,128)(2,1)}) %reduce-scatter.35.cloned.1.call-update) | async-done | bytes 524304
  958.8 52.2 %reduce-scatter.37.cloned.1.call-done = bf16[128,2048]{1,0:T(8,128)(2,1)} async-done(((bf16[1024,2048]{1,0:T(8,128)(2,1)}), bf16[128,2048]{1,0:T(8,128)(2,1)}) %reduce-scatter.37.cloned.1.call-update) | async-done | bytes 524304
  1012.9 2.4 collective-permute-start.3
  1015.6 3.4 multiply_reduce_fusion.3
  1019.0 20.0 %collective-permute-done.3 = bf16[1024,128]{1,0:T(8,128)(2,1)} collective-permute-done((bf16[1024,128]{1,0:T(8,128)(2,1)}, bf16[1024,128]{1,0:T(8,128)(2,1)}, u32[]{:S(2)}, u32[]{:S(2)}) %collective-permute-start.3) | collective-permute-done | bytes 262176 | tf_op jit(solution)/shard_map/ppermute | solution.py:714
  1039.0 3.3 multiply_reduce_fusion.2
  1042.4 19.8 %all-gather.19.cloned.1.call-done = bf16[1024,1024]{1,0:T(8,128)(2,1)} async-done(((bf16[256,1024]{1,0:T(8,128)(2,1)}), bf16[1024,1024]{1,0:T(8,128)(2,1)}) %all-gather.19.cloned.1.call-update) | async-done | bytes 2097168 | tf_op jit(solution)/shard_map/all_gather | solution.py:807
  1062.1 4.1 bitcast_convert_fusion.1
  1066.2 20.3 %reduce-scatter.27.cloned.1.call-done = bf16[2,256,128]{2,1,0:T(8,128)(2,1)} async-done(((bf16[2,1024,128]{2,1,0:T(8,128)(2,1)}), bf16[2,256,128]{2,1,0:T(8,128)(2,1)}) %reduce-scatter.27.cloned.1.call-update) | async-done | bytes 131088 | tf_op jit(solution)/shard_map/reduce_scatter | solution.py:809
  1086.5 2.0 multiply_reduce_fusion.6
  1088.5 2.8 concatenate.18
  1091.9 10.6 sum_all.1
  1108.1 1.9 multiply_subtract_fusion.1
  (194 shorter events, 40.4 us)
Async XLA Ops:
  7.2 4.0 copy-start.8
  7.2 4.7 copy-start.4
  7.2 47.3 %all-gather.27.cloned.1.call-start = ((), (), s32[]{:S(2)}) async-start(), calls=%async_computation.23 | async-start | bytes 1179648 | tf_op jit(solution)/shard_map/all_gather | solution.py:760
  8.7 20.1 %copy-start = (f32[2,3,128,256]{2,3,1,0:T(8,128)}, f32[2,3,128,256]{2,3,1,0:T(8,128)S(1)}, u32[]{:S(2)}) copy-start(f32[2,3,128,256]{2,3,1,0:T(8,128)S(1)} %copy.115) | copy-start | bytes 2359300
  8.8 20.1 %copy-start.2 = (f32[1024,128]{1,0:T(8,128)S(1)}, f32[1024,128]{1,0:T(8,128)}, u32[]{:S(2)}) copy-start(f32[1024,128]{1,0:T(8,128)} %param.35) | copy-start | bytes 1572868
  9.5 55.7 %all-gather.21.cloned.1.call-start = ((), (), s32[]{:S(2)}) async-start(), calls=%async_computation.20 | async-start | bytes 1769472 | tf_op jit(solution)/shard_map/all_gather | solution.py:745
  10.3 114.9 %all-gather.25.cloned.1.call-start = ((), (), s32[]{:S(2)}) async-start(), calls=%async_computation.22 | async-start | bytes 2162688 | tf_op jit(solution)/shard_map/all_gather | solution.py:755
  11.1 178.5 %all-gather.23.cloned.1.call-start = ((), (), s32[]{:S(2)}) async-start(), calls=%async_computation.21 | async-start | bytes 4325376 | tf_op jit(solution)/shard_map/all_gather | solution.py:749
  11.8 239.0 %all-gather.13.cloned.1.call-start = ((), (), s32[]{:S(2)}) async-start(), calls=%async_computation.10 | async-start | bytes 4718592 | tf_op jit(solution)/shard_map/all_gather | solution.py:761
  11.9 32.6 %copy-start.27 = (f32[2,3,128]{2,0,1:T(2,128)S(1)}, f32[2,3,128]{2,0,1:T(2,128)}, u32[]{:S(2)}) copy-start(f32[2,3,128]{2,0,1:T(2,128)} %param.38) | copy-start | bytes 9220
  12.0 16.0 %collective-permute-start = (bf16[128,1024]{1,0:T(8,128)(2,1)S(1)}, bf16[128,1024]{1,0:T(8,128)(2,1)S(1)}, u32[]{:S(2)}, u32[]{:S(2)}) collective-permute-start(bf16[128,1024]{1,0:T(8,128)(2,1)S(1)} %convert_element_type.78), channel_id=1, source_target_pairs={{0,2},{1,3},{2,0},{3,1},{4,6},{5,7},{6,4},{7,5},{8,10},{9,11},{10,... | collective-permute-start | bytes 786440 | tf_op jit(solution)/shard_map/ppermute | solution.py:714
  28.8 238.1 %all-gather.15.cloned.1.call-start = ((), (), s32[]{:S(2)}) async-start(), calls=%async_computation.11 | async-start | bytes 4718592 | tf_op jit(solution)/shard_map/all_gather | solution.py:764
  28.9 14.1 %collective-permute-start.1 = (bf16[1024,128]{1,0:T(8,128)(2,1)S(1)}, bf16[1024,128]{1,0:T(8,128)(2,1)S(1)}, u32[]{:S(2)}, u32[]{:S(2)}) collective-permute-start(bf16[1024,128]{1,0:T(8,128)(2,1)S(1)} %convert_element_type.79), channel_id=1, source_target_pairs={{0,2},{1,3},{2,0},{3,1},{4,6},{5,7},{6,4},{7,5},{8,10},{9,11},{10,... | collective-permute-start | bytes 786440 | tf_op jit(solution)/shard_map/ppermute | solution.py:714
  43.9 408.7 %reduce-scatter.23.cloned.1.call-start = ((), (), s32[]{:S(2)}) async-start(), calls=%async_computation.16 | async-start | bytes 2359296 | tf_op jit(solution)/shard_map/reduce_scatter | solution.py:809
  59.4 5.8 copy-start.37
  410.0 88.9 %reduce-scatter.21.cloned.1.call-start = ((), (), s32[]{:S(2)}) async-start(), calls=%async_computation.13 | async-start | bytes 2621440 | tf_op jit(solution)/shard_map/reduce_scatter | solution.py:805
  410.0 13.3 %copy-start.38 = (bf16[1,3,1024,256]{2,3,1,0:T(8,128)(2,1)S(1)}, bf16[1,3,1024,256]{2,3,1,0:T(8,128)(2,1)}, u32[]{:S(2)}) copy-start(bf16[1,3,1024,256]{2,3,1,0:T(8,128)(2,1)} %all-gather.21.cloned.1.call-done) | copy-start | bytes 4718596
  427.8 0.9 copy-start.29
  427.8 3.2 copy-start.13
  427.9 108.1 %reduce-scatter.39.cloned.1.call-start = ((), (), s32[]{:S(2)}) async-start(), calls=%async_computation.28 | async-start | bytes 589824
  431.0 4.0 copy-start.15
  431.0 4.1 copy-start.36
  436.5 139.0 %reduce-scatter.33.cloned.1.call-start = ((), (), s32[]{:S(2)}) async-start(), calls=%async_computation.25 | async-start | bytes 1179648
  437.6 1.4 copy-start.39
  437.6 1.4 copy-start.40
  438.9 178.7 %reduce-scatter.31.cloned.1.call-start = ((), (), s32[]{:S(2)}) async-start(), calls=%async_computation.24 | async-start | bytes 1769472
  448.2 216.8 %all-gather.17.cloned.1.call-start = ((), (), s32[]{:S(2)}) async-start(), calls=%async_computation.12 | async-start | bytes 2621440 | tf_op jit(solution)/shard_map/all_gather | solution.py:782
  448.8 236.9 %reduce-scatter.25.cloned.1.call-start = ((), (), s32[]{:S(2)}) async-start(), calls=%async_computation.17 | async-start | bytes 327680 | tf_op jit(solution)/shard_map/reduce_scatter | solution.py:809
  452.6 286.0 %reduce-scatter.29.cloned.1.call-start = ((), (), s32[]{:S(2)}) async-start(), calls=%async_computation.19 | async-start | bytes 4718592 | tf_op jit(solution)/shard_map/reduce_scatter | solution.py:809
  452.6 1.2 copy-start.14
  453.2 2.0 copy-start.16
  453.2 449.3 %all-reduce.3.cloned.1.call-start = ((), (), s32[]{:S(2)}) async-start(), calls=%async_computation.15 | async-start | bytes 8388608 | tf_op jit(solution)/shard_map/psum | solution.py:787
  458.5 1.6 copy-start.12
  458.6 497.5 %reduce-scatter.35.cloned.1.call-start = ((), (), s32[]{:S(2)}) async-start(), calls=%async_computation.26 | async-start | bytes 4718592
  481.4 529.6 %reduce-scatter.37.cloned.1.call-start = ((), (), s32[]{:S(2)}) async-start(), calls=%async_computation.27 | async-start | bytes 4718592
  488.0 10.9 copy-start.17
  488.0 13.0 %copy-start.19 = (f32[2,3,128,256]{3,2,1,0:T(8,128)S(1)}, f32[2,3,128,256]{3,2,1,0:T(8,128)}, u32[]{:S(2)}) copy-start(f32[2,3,128,256]{3,2,1,0:T(8,128)} %param.27) | copy-start | bytes 2359300
  488.0 574.1 %all-gather.19.cloned.1.call-start = ((), (), s32[]{:S(2)}) async-start(), calls=%async_computation.14 | async-start | bytes 2621440 | tf_op jit(solution)/shard_map/all_gather | solution.py:807
  498.9 2.4 copy-start.20
  500.9 0.7 copy-start.30
  500.9 1.1 copy-start.6
  500.9 48.0 %copy-start.28 = (f32[2,3,128]{2,0,1:T(2,128)S(1)}, f32[2,3,128]{2,0,1:T(2,128)}, u32[]{:S(2)}) copy-start(f32[2,3,128]{2,0,1:T(2,128)} %param.38) | copy-start | bytes 9220
  501.0 48.0 %copy-start.31 = (f32[2,3,128]{2,0,1:T(2,128)S(1)}, f32[2,3,128]{2,0,1:T(2,128)}, u32[]{:S(2)}) copy-start(f32[2,3,128]{2,0,1:T(2,128)} %param.40) | copy-start | bytes 9220
  501.0 48.0 %copy-start.32 = (f32[2,3,128]{2,0,1:T(2,128)S(1)}, f32[2,3,128]{2,0,1:T(2,128)}, u32[]{:S(2)}) copy-start(f32[2,3,128]{2,0,1:T(2,128)} %param.39) | copy-start | bytes 9220
  501.0 585.5 %reduce-scatter.27.cloned.1.call-start = ((), (), s32[]{:S(2)}) async-start(), calls=%async_computation.18 | async-start | bytes 655360 | tf_op jit(solution)/shard_map/reduce_scatter | solution.py:809
  618.8 123.9 %copy-start.1 = (f32[2,3,128,256]{2,3,1,0:T(8,128)S(1)}, f32[2,3,128,256]{2,3,1,0:T(8,128)}, u32[]{:S(2)}) copy-start(f32[2,3,128,256]{2,3,1,0:T(8,128)} %copy-done) | copy-start | bytes 2359300
  740.2 275.3 %collective-permute-start.2 = (bf16[128,1024]{1,0:T(8,128)(2,1)}, bf16[128,1024]{1,0:T(8,128)(2,1)}, u32[]{:S(2)}, u32[]{:S(2)}) collective-permute-start(bf16[128,1024]{1,0:T(8,128)(2,1)} %slice.166), channel_id=1, source_target_pairs={{0,2},{1,3},{2,0},{3,1},{4,6},{5,7},{6,4},{7,5},{8,10},{9,11},{10,... | collective-permute-start | bytes 786440 | tf_op jit(solution)/shard_map/ppermute | solution.py:714
  957.5 58.0 %copy-start.5 = (f32[128,1024]{1,0:T(8,128)S(1)}, f32[128,1024]{1,0:T(8,128)}, u32[]{:S(2)}) copy-start(f32[128,1024]{1,0:T(8,128)} %param.32) | copy-start | bytes 1572868
  957.5 58.0 %copy-start.21 = (f32[128,1024]{1,0:T(8,128)S(1)}, f32[128,1024]{1,0:T(8,128)}, u32[]{:S(2)}) copy-start(f32[128,1024]{1,0:T(8,128)} %param.33) | copy-start | bytes 1572868
  957.6 58.0 %copy-start.22 = (f32[128,1024]{1,0:T(8,128)S(1)}, f32[128,1024]{1,0:T(8,128)}, u32[]{:S(2)}) copy-start(f32[128,1024]{1,0:T(8,128)} %param.34) | copy-start | bytes 1572868
  1012.9 26.1 %collective-permute-start.3 = (bf16[1024,128]{1,0:T(8,128)(2,1)}, bf16[1024,128]{1,0:T(8,128)(2,1)}, u32[]{:S(2)}, u32[]{:S(2)}) collective-permute-start(bf16[1024,128]{1,0:T(8,128)(2,1)} %copy.157), channel_id=1, source_target_pairs={{0,2},{1,3},{2,0},{3,1},{4,6},{5,7},{6,4},{7,5},{8,10},{9,11},{10,... | collective-permute-start | bytes 786440 | tf_op jit(solution)/shard_map/ppermute | solution.py:714
  1015.3 23.7 %copy-start.3 = (f32[1024,128]{1,0:T(8,128)S(1)}, f32[1024,128]{1,0:T(8,128)}, u32[]{:S(2)}) copy-start(f32[1024,128]{1,0:T(8,128)} %param.35) | copy-start | bytes 1572868
  1015.5 23.5 %copy-start.23 = (f32[1024,128]{1,0:T(8,128)S(1)}, f32[1024,128]{1,0:T(8,128)}, u32[]{:S(2)}) copy-start(f32[1024,128]{1,0:T(8,128)} %param.36) | copy-start | bytes 1572868
  1015.5 23.5 %copy-start.24 = (f32[1024,128]{1,0:T(8,128)S(1)}, f32[1024,128]{1,0:T(8,128)}, u32[]{:S(2)}) copy-start(f32[1024,128]{1,0:T(8,128)} %param.37) | copy-start | bytes 1572868
  1042.3 44.2 %copy-start.9 = (f32[2,256,128]{2,1,0:T(8,128)S(1)}, f32[2,256,128]{2,1,0:T(8,128)}, u32[]{:S(2)}) copy-start(f32[2,256,128]{2,1,0:T(8,128)} %param.29) | copy-start | bytes 786436
  1042.3 44.2 %copy-start.25 = (f32[2,256,128]{2,1,0:T(8,128)S(1)}, f32[2,256,128]{2,1,0:T(8,128)}, u32[]{:S(2)}) copy-start(f32[2,256,128]{2,1,0:T(8,128)} %param.30) | copy-start | bytes 786436
  1042.3 44.2 %copy-start.26 = (f32[2,256,128]{2,1,0:T(8,128)S(1)}, f32[2,256,128]{2,1,0:T(8,128)}, u32[]{:S(2)}) copy-start(f32[2,256,128]{2,1,0:T(8,128)} %param.31) | copy-start | bytes 786436
  1042.3 46.2 %copy-start.34 = (f32[6]{0:T(128)S(1)}, f32[6]{0:T(128)}, u32[]{:S(2)}) copy-start(f32[6]{0:T(128)} %reshape.160) | copy-start | bytes 76
  1042.3 46.2 %copy-start.35 = (f32[6]{0:T(128)S(1)}, f32[6]{0:T(128)}, u32[]{:S(2)}) copy-start(f32[6]{0:T(128)} %mul.294) | copy-start | bytes 76
  1042.3 60.1 %copy-start.33 = (f32[1,16]{1,0:T(1,128)S(1)}, f32[1,16]{1,0:T(1,128)}, u32[]{:S(2)}) copy-start(f32[1,16]{1,0:T(1,128)} %constant.106) | copy-start | bytes 196
  1066.2 40.0 %copy-start.7 = (f32[2,3,128,256]{2,3,1,0:T(8,128)S(1)}, f32[2,3,128,256]{2,3,1,0:T(8,128)}, u32[]{:S(2)}) copy-start(f32[2,3,128,256]{2,3,1,0:T(8,128)} %get-tuple-element.175) | copy-start | bytes 2359300
  1106.3 3.7 copy-start.11
  1106.3 4.5 copy-start.10
  1106.4 4.5 copy-start.18
Sparse Core Ops, SparseCore 0:
  10.5 26.2 all-gather.26
  39.2 25.8 all-gather.20
  68.7 56.4 all-gather.24
  128.6 60.9 all-gather.22
  191.9 35.2 all-gather.12
  229.6 37.3 all-gather.14
  410.1 42.4 reduce-scatter.22
  454.9 43.8 reduce-scatter.20
  502.5 33.4 reduce-scatter.38
  539.3 36.0 reduce-scatter.32
  579.1 38.4 reduce-scatter.30
  619.1 45.9 all-gather.16
  667.4 18.2 reduce-scatter.24
  688.9 49.6 reduce-scatter.28
  741.5 161.0 all-reduce.2
  905.7 50.3 reduce-scatter.34
  959.7 51.2 reduce-scatter.36
  1013.0 49.0 all-gather.18
  1065.0 21.4 reduce-scatter.26

commit v2 on v1

v2 whole, which is shorter than its diff:
```python
from functools import partial

import jax
import jax.numpy as jnp
from jax import lax
from jax.experimental import pallas as pl
from jax.experimental.pallas import tpu as pltpu
from jax.sharding import PartitionSpec as P

D = 1024
HEAD = 64
FF = 4096
STEP = 5

first_decay = 0.5
second_decay = 0.6
learn_rate = 0.5
weight_decay = 0.01
epsilon = 1e-06
norm_eps = 1e-05
mask_fill = -1000000000.0

MESH = pl.DeviceIdType.MESH
ANYWHERE = pl.BlockSpec(memory_space=pl.ANY)
IN_VMEM = pl.BlockSpec(memory_space=pltpu.VMEM)
NN = (((1,), (0,)), ((), ()))
NT = (((1,), (1,)), ((), ()))
TN = (((0,), (0,)), ((), ()))
VMEM_LIMIT = 54 << 20


def dot(left, right, dims=NN):
    return lax.dot_general(left, right, dims, preferred_element_type=jnp.float32)


def bf16(values):
    return values.astype(jnp.bfloat16)


def f32(values):
    return values.astype(jnp.float32)


def layer_norm(values, gain_row, bias_row):
    center = values - jnp.mean(values, axis=-1, keepdims=True)
    spread = jnp.mean(center * center, axis=-1, keepdims=True)
    inverse = lax.rsqrt(spread + norm_eps)
    normed = center * inverse
    return (normed * gain_row + bias_row, normed, inverse)


def norm_back(upstream, normed, inverse, gain_row):
    scaled = upstream * gain_row
    inner = (
        scaled
        - jnp.mean(scaled, axis=-1, keepdims=True)
        - normed * jnp.mean(scaled * normed, axis=-1, keepdims=True)
    )
    return (
        inner * inverse,
        jnp.sum(upstream * normed, axis=0, keepdims=True),
        jnp.sum(upstream, axis=0, keepdims=True),
    )


class Place:
    def __init__(self, n_mp, side):
        self.n, self.side = n_mp, side
        self.z = lax.axis_index("mp")
        dp = lax.axis_index("dp")
        self.core = lax.rem(dp, 2)
        self.x = lax.rem(dp // 2, side)
        self.y = dp // (2 * side)

    def at(self, y, x, core):
        return {"dp": (y * self.side + x) * 2 + core}

    def x_peer(self, distance):
        other = lax.rem(self.x + distance, self.side)
        return other, self.at(self.y, other, self.core)

    def y_peer(self, distance):
        other = lax.rem(self.y + distance, self.side)
        return other, self.at(other, self.x, self.core)

    def sibling(self):
        return self.at(self.y, self.x, 1 - self.core)

    def line(self):
        return [{"mp": lax.rem(self.z + distance, self.n)} for distance in range(1, self.n)]

    def plane(self):
        steps = range(1, self.side)
        return (
            [self.x_peer(step)[1] for step in steps]
            + [self.y_peer(step)[1] for step in steps]
            + [self.sibling()]
        )


def greet(others):
    barrier = pltpu.get_barrier_semaphore()
    for other in others:
        pl.semaphore_signal(barrier, inc=1, device_id=other, device_id_type=MESH)
    pl.semaphore_wait(barrier, len(others))


def push(source, target, send_sem, recv_sem, to):
    copy = pltpu.make_async_remote_copy(
        source, target, send_sem, recv_sem, device_id=to, device_id_type=MESH
    )
    copy.start()
    return copy


def rows_at(index, size):
    return pl.ds(pl.multiple_of(index * size, size), size)


def heads_to_tokens(n, source, slots, send_sems, recv_sems):
    me = lax.axis_index("mp")
    size = source.shape[0] // n
    copies = []
    for distance in range(1, n):
        to = lax.rem(me + distance, n)
        copies.append(
            push(
                source.at[rows_at(to, size)], slots.at[me],
                send_sems.at[distance - 1], recv_sems.at[distance - 1], {"mp": to},
            )
        )
    return copies


def tokens_to_heads(n, make, blocks, target, send_sems, recv_sems, local_sem):
    me = lax.axis_index("mp")
    size = blocks.shape[1]
    copies = []
    for distance in (*range(1, n), 0):
        to = lax.rem(me + distance, n)
        blocks[to] = bf16(make(to))
        place = target.at[rows_at(me, size)]
        if distance:
            copies.append(
                push(
                    blocks.at[to], place,
                    send_sems.at[distance - 1], recv_sems.at[distance - 1], {"mp": to},
                )
            )
        else:
            copy = pltpu.make_async_copy(blocks.at[to], place, local_sem)
            copy.start()
            copies.append(copy)
    return copies


def merge_heads(n, slots, copies, part_of, start):
    me = lax.axis_index("mp")
    total = start + part_of(slots[me], me)
    for distance in range(1, n):
        origin = lax.rem(me + n - distance, n)
        copies[distance - 1].wait_recv()
        total = total + part_of(slots[origin], origin)
    for copy in copies:
        copy.wait_send()
    return total


def load_groups(n, bundle, first, width, target, sems):
    return [
        pltpu.make_async_copy(
            bundle.at[:, pl.ds(group * 3 * width + first, width)], target.at[group], sems.at[group]
        )
        for group in range(n)
    ]


class Give:
    def __init__(self, place, out, sems):
        self.place, self.n, self.me, self.out = place, place.n, place.z, out
        self.sems = {"right": sems[0:2], "left": sems[2:4]}

    @staticmethod
    def sems(n):
        return [pltpu.SemaphoreType.DMA((max(n - 1, 1),))] * 4

    def _copy(self, way, step):
        ahead = 1 if way == "right" else -1
        chunk = lax.rem(self.me - ahead * step + self.n, self.n)
        return pltpu.make_async_remote_copy(
            self.out.at[chunk], self.out.at[chunk],
            self.sems[way][0].at[step], self.sems[way][1].at[step],
            device_id={"mp": lax.rem(self.me + ahead + self.n, self.n)}, device_id_type=MESH,
        )

    def _spots(self):
        return (("right", self.me), ("left", self.n - 1 - self.me))

    def step(self, step):
        for way, spot in self._spots():

            @pl.when((spot >= step) & (spot < self.n - 1))
            def _():
                if step > 0:
                    self._copy(way, step - 1).wait_recv()
                self._copy(way, step).start()

    def finish(self):
        for way, spot in self._spots():

            @pl.when(spot == self.n - 1)
            def _():
                for step in range(self.n - 1):
                    self._copy(way, step).wait_recv()

            for step in range(self.n - 1):

                @pl.when((spot >= step) & (spot < self.n - 1))
                def _():
                    self._copy(way, step).wait_send()


def sizes_of(total, block, limit):
    groups = {}
    for index in range(total // block):
        groups.setdefault(limit(index), []).append(index)
    return groups.items()


def forward_kernel(masked, block, prefix_ref, q_ref, k_ref, v_ref, mixed_ref, sums_ref):
    width = q_ref.shape[1]
    heads = width // HEAD
    keys_total = k_ref.shape[0]
    step = pl.program_id(0)
    lane = lax.broadcasted_iota(jnp.int32, (block, width), 1) // HEAD

    def run(keys, start):
        query = q_ref[...] * jnp.bfloat16(HEAD**-0.5)
        key_rows = k_ref[:keys, :]
        value_rows = v_ref[:keys, :]
        if masked:
            rows = start + lax.broadcasted_iota(jnp.int32, (block, keys), 0)
            cols = lax.broadcasted_iota(jnp.int32, (block, keys), 1)
            allowed = (cols <= rows) | (cols < prefix_ref[0])
        mixed = jnp.zeros((block, width), jnp.float32)
        slot = lax.broadcasted_iota(jnp.int32, (block, 128), 1)
        table = jnp.zeros((block, 128), jnp.float32)
        for head in range(heads):
            scores = dot(jnp.where(lane == head, query, jnp.bfloat16(0)), key_rows, NT)
            if masked:
                scores = jnp.where(allowed, scores, mask_fill)
            row_max = jnp.max(scores, axis=1, keepdims=True)
            powered = jnp.exp(scores - row_max)
            totals = jnp.sum(powered, axis=1, keepdims=True)
            part = dot(bf16(powered), value_rows) * (1.0 / totals)
            mixed = jnp.where(lane == head, part, mixed)
            table = jnp.where(slot == head, row_max + jnp.log(totals), table)
        mixed_ref[...] = bf16(mixed)
        sums_ref[...] = table.T[:8, :]

    if masked:
        limit = lambda index: max(keys_total // 2, (index + 1) * block)
        for keys, blocks in sizes_of(keys_total, block, limit):

            @pl.when((step >= blocks[0]) & (step <= blocks[-1]))
            def _(keys=keys):
                run(keys, step * block)
    else:
        run(keys_total, 0)


def attend_forward(query, key_rows, value_rows, prefix, masked, block=512):
    total, width = query.shape
    keys = key_rows.shape[0]
    block = min(block, total)
    whole = pl.BlockSpec((keys, width), lambda i, p: (0, 0))
    return pl.pallas_call(
        partial(forward_kernel, masked, block),
        grid_spec=pltpu.PrefetchScalarGridSpec(
            num_scalar_prefetch=1,
            grid=(total // block,),
            in_specs=[pl.BlockSpec((block, width), lambda i, p: (i, 0)), whole, whole],
            out_specs=[
                pl.BlockSpec((block, width), lambda i, p: (i, 0)),
                pl.BlockSpec((8, block), lambda i, p: (0, i)),
            ],
        ),
        out_shape=[
            jax.ShapeDtypeStruct((total, width), jnp.bfloat16),
            jax.ShapeDtypeStruct((8, total), jnp.float32),
        ],
        compiler_params=pltpu.CompilerParams(vmem_limit_bytes=VMEM_LIMIT),
        cost_estimate=pl.CostEstimate(
            flops=16 * total * keys * width, bytes_accessed=4 * keys * width, transcendentals=0
        ),
        name="attend_forward",
    )(prefix, query, key_rows, value_rows)


def backward_kernel(
    masked, block, n, prefix_ref, q_ref, k_ref, v_ref, do_ref, o_ref, sums_ref, *refs,
):
    if n:
        mine_ref, states_ref, dq_ref, dk_ref, dv_ref, all_ref, source_ref, *refs = refs
        acc, delta, source, own_sem, *sems = refs
        give = Give(Place(n, 1), all_ref, sems)
    else:
        dq_ref, dk_ref, dv_ref, acc, delta = refs
    width = q_ref.shape[1]
    heads = width // HEAD
    total = q_ref.shape[0]
    step = pl.program_id(0)
    factor = HEAD**-0.5

    @pl.when(step == 0)
    def _():
        if n:
            source[...] = jnp.zeros_like(source)
            own = pltpu.make_async_copy(mine_ref, all_ref.at[give.me], own_sem)
            own.start()
            greet(give.place.line())
            own.wait()
            give.step(0)
        product = f32(do_ref[...]) * f32(o_ref[...])
        row = lax.broadcasted_iota(jnp.int32, (8, width), 0)
        col = lax.broadcasted_iota(jnp.int32, (8, width), 1) // HEAD
        pick = jnp.where(row == col, 1.0, 0.0).astype(jnp.float32)
        delta[...] = lax.dot_general(
            pick, product, NT, precision=lax.Precision.HIGHEST, preferred_element_type=jnp.float32
        )
        acc[...] = jnp.zeros_like(acc)

    if n:
        steps = pl.num_programs(0)
        for later in range(1, n - 1):

            @pl.when(step == (later + 1) * steps // n)
            def _():
                give.step(later)

    lane = lax.broadcasted_iota(jnp.int32, (block, width), 1) // HEAD

    def run(first):
        count = total - first
        query = q_ref[first:, :]
        grad_rows = do_ref[first:, :]
        scaled_keys = k_ref[...] * jnp.bfloat16(factor)
        value_rows = v_ref[...]
        if masked:
            rows = first + lax.broadcasted_iota(jnp.int32, (block, count), 1)
            cols = step * block + lax.broadcasted_iota(jnp.int32, (block, count), 0)
            allowed = (cols <= rows) | (cols < prefix_ref[0])
        key_grad = jnp.zeros((block, width), jnp.float32)
        value_grad = jnp.zeros((block, width), jnp.float32)
        query_grad = jnp.zeros((count, width), jnp.float32)
        for head in range(heads):
            own_keys = jnp.where(lane == head, scaled_keys, jnp.bfloat16(0))
            scores = dot(own_keys, query, NT)
            if masked:
                scores = jnp.where(allowed, scores, mask_fill)
            probs = jnp.exp(scores - sums_ref[head : head + 1, first:])
            prob_grad = dot(jnp.where(lane == head, value_rows, jnp.bfloat16(0)), grad_rows, NT)
            score_grad = bf16(probs * (prob_grad - delta[head : head + 1, first:]))
            value_grad = jnp.where(lane == head, dot(bf16(probs), grad_rows), value_grad)
            key_grad = jnp.where(lane == head, dot(score_grad, query), key_grad)
            query_grad = query_grad + dot(score_grad, own_keys, TN)
        acc[first:, :] += query_grad
        dk_ref[...] = bf16(key_grad * factor)
        dv_ref[...] = bf16(value_grad)
        if n:
            source[:, :width] += dot(states_ref[...], dk_ref[...], TN)
            source[:, width:] += dot(states_ref[...], dv_ref[...], TN)

    if masked:
        limit = lambda index: 0 if index * block < total // 2 else index * block
        for first, blocks in sizes_of(total, block, limit):

            @pl.when((step >= blocks[0]) & (step <= blocks[-1]))
            def _(first=first):
                run(first)
    else:
        run(0)

    @pl.when(step == pl.num_programs(0) - 1)
    def _():
        dq_ref[...] = bf16(acc[...])
        if n:
            source_ref[...] = bf16(source[...])
            give.finish()


def attend_backward(
    query, key_rows, value_rows, grad_out, mixed, sums, prefix, masked, n=0, mine=(), states=(), block=512
):
    total, width = query.shape
    keys = key_rows.shape[0]
    whole = pl.BlockSpec((total, width), lambda i, p: (0, 0))
    part = pl.BlockSpec((block, width), lambda i, p: (i, 0))
    return pl.pallas_call(
        partial(backward_kernel, masked, block, n),
        grid_spec=pltpu.PrefetchScalarGridSpec(
            num_scalar_prefetch=1,
            grid=(keys // block,),
            in_specs=[
                whole, part, part, whole, whole, pl.BlockSpec((8, total), lambda i, p: (0, 0)),
            ]
            + [pl.BlockSpec(rows.shape, lambda i, p: (0, 0)) for rows in mine]
            + [pl.BlockSpec((block, rows.shape[1]), lambda i, p: (i, 0)) for rows in states],
            out_specs=[whole, part, part]
            + [ANYWHERE] * len(mine)
            + [pl.BlockSpec((rows.shape[1], 2 * width), lambda i, p: (0, 0)) for rows in states],
            scratch_shapes=[
                pltpu.VMEM((total, width), jnp.float32),
                pltpu.VMEM((8, total), jnp.float32),
            ]
            + [pltpu.VMEM((rows.shape[1], 2 * width), jnp.float32) for rows in states]
            + [pltpu.SemaphoreType.DMA] * len(mine)
            + Give.sems(n) * len(mine),
        ),
        out_shape=[jax.ShapeDtypeStruct((total, width), jnp.bfloat16)]
        + [jax.ShapeDtypeStruct((keys, width), jnp.bfloat16)] * 2
        + [jax.ShapeDtypeStruct((n,) + rows.shape, rows.dtype) for rows in mine]
        + [jax.ShapeDtypeStruct((rows.shape[1], 2 * width), rows.dtype) for rows in states],
        compiler_params=pltpu.CompilerParams(
            vmem_limit_bytes=VMEM_LIMIT,
            **(dict(collective_id=6, has_side_effects=True) if n else {}),
        ),
        cost_estimate=pl.CostEstimate(
            flops=4 * total * keys * width, bytes_accessed=4 * keys * width, transcendentals=0
        ),
        name="attend_backward",
    )(prefix, query, key_rows, value_rows, grad_out, mixed, sums, *mine, *states)


class Spread:
    def __init__(self, place, home, send_sems, recv_sems):
        self.place, self.home, self.send, self.recv = place, home, send_sems, recv_sems
        self.half = home.shape[3] // 2
        self.copies = {"first": [], "second": [], "core": []}
        self.index = 0

    def _push(self, stage, block, to):
        spot = self.index
        self.index += 1
        self.copies[stage].append(push(block, block, self.send.at[spot], self.recv.at[spot], to))

    def first(self):
        p, half = self.place, self.half
        for step in range(1, p.side):
            own = self.home.at[p.y, p.x, p.core]
            self._push("first", own.at[pl.ds(0, half)], p.x_peer(step)[1])
            self._push("first", own.at[pl.ds(half, half)], p.y_peer(step)[1])

    def second(self):
        p, half = self.place, self.half
        for copy in self.copies["first"]:
            copy.wait_recv()
        for step in range(1, p.side):
            self._push(
                "second", self.home.at[p.y, :, p.core, pl.ds(0, half)], p.y_peer(step)[1]
            )
            self._push(
                "second", self.home.at[:, p.x, p.core, pl.ds(half, half)], p.x_peer(step)[1]
            )

    def core(self):
        for copy in self.copies["second"]:
            copy.wait_recv()
        self._push("core", self.home.at[:, :, self.place.core], self.place.sibling())

    def finish(self):
        for copy in self.copies["core"] or self.copies["second"]:
            copy.wait_recv()
        for stage in self.copies.values():
            for copy in stage:
                copy.wait_send()

    @staticmethod
    def sems(side):
        return pltpu.SemaphoreType.DMA((4 * (side - 1) + 1,))


def front_kernel(
    n, side, inner_ref, outer_ref, norm_ref, expand_ref, shrink_ref, home_self, home_rest, feed_ref,
    self_sems_send, self_sems_recv, rest_send, rest_recv, line_send, line_recv,
    block_self, block_line, block_rest, own_sems, far_send, far_recv,
):
    p = Place(n, side)
    width = inner_ref.shape[3]
    for index in range(3):
        block_self[:, index * width : (index + 1) * width] = bf16(inner_ref[0, index])
    block_line[:, :width] = bf16(inner_ref[1, 0])
    for index in range(2):
        block_line[:, (index + 1) * width : (index + 2) * width] = outer_ref[index]
        block_rest[:, index * width : (index + 1) * width] = bf16(inner_ref[1, index + 1])
    block_rest[:, 2 * width :] = norm_ref[...]
    units = expand_ref.shape[1]
    feed_ref[:, :units] = bf16(expand_ref[...])
    feed_ref[:, 2 * units : 3 * units] = shrink_ref[...]
    whole = 3 * width
    line_cols = pl.ds(pl.multiple_of(p.z * whole, whole), whole)
    spot = home_rest.at[p.y, p.x, p.core]
    own = [
        pltpu.make_async_copy(block_self, home_self.at[p.y, p.x, p.core], own_sems.at[0]),
        pltpu.make_async_copy(block_line, spot.at[:, line_cols], own_sems.at[1]),
        pltpu.make_async_copy(
            block_rest, spot.at[:, pl.ds(n * whole, block_rest.shape[1])], own_sems.at[2]
        ),
    ]
    for copy in own:
        copy.start()
    greet(p.line() + p.plane())
    line = [
        push(block_line, spot.at[:, line_cols], line_send.at[index], line_recv.at[index], other)
        for index, other in enumerate(p.line())
    ]
    far = {"mp": lax.rem(p.z + n // 2, n)}
    far_copies = [
        push(
            feed_ref.at[:, pl.ds(2 * index * units, units)],
            feed_ref.at[:, pl.ds((2 * index + 1) * units, units)],
            far_send.at[index], far_recv.at[index], far,
        )
        for index in range(2)
    ]
    for copy in own:
        copy.wait()
    near = Spread(p, home_self, self_sems_send, self_sems_recv)
    rest = Spread(p, home_rest, rest_send, rest_recv)
    near.first()
    near.second()
    near.core()
    for copy in line:
        copy.wait_recv()
    rest.first()
    near.finish()
    rest.second()
    rest.core()
    rest.finish()
    for copy in line:
        copy.wait_send()
    for copy in far_copies:
        copy.wait()


def front(n_dp, n_mp, inner, outer_t, norm_t, expand, shrink_t):
    rows, width = inner.shape[2:]
    side = round((n_dp // 2) ** 0.5)
    whole = 3 * width
    columns = n_mp * whole + 2 * width + norm_t.shape[1]
    low = jnp.bfloat16
    dma = pltpu.SemaphoreType.DMA
    near, rest, feed_block = pl.pallas_call(
        partial(front_kernel, n_mp, side),
        out_shape=[
            jax.ShapeDtypeStruct((side, side, 2, rows, whole), low),
            jax.ShapeDtypeStruct((side, side, 2, rows, columns), low),
            jax.ShapeDtypeStruct((rows, 4 * expand.shape[1]), low),
        ],
        in_specs=[IN_VMEM] * 5,
        out_specs=[ANYWHERE, ANYWHERE, IN_VMEM],
        scratch_shapes=[
            Spread.sems(side), Spread.sems(side), Spread.sems(side), Spread.sems(side),
            dma((n_mp - 1,)), dma((n_mp - 1,)),
            pltpu.VMEM((rows, whole), low),
            pltpu.VMEM((rows, whole), low),
            pltpu.VMEM((rows, 2 * width + norm_t.shape[1]), low),
            dma((3,)), dma((2,)), dma((2,)),
        ],
        compiler_params=pltpu.CompilerParams(
            collective_id=0, has_side_effects=True, vmem_limit_bytes=VMEM_LIMIT
        ),
        cost_estimate=pl.CostEstimate(flops=40 * 10**9, bytes_accessed=1 << 20, transcendentals=0),
        name="front",
    )(inner, outer_t, norm_t, expand, shrink_t)
    return near.reshape(n_dp * rows, whole), rest.reshape(n_dp * rows, columns), feed_block


def self_to_cross_kernel(
    n, side, mixed_ref, bundle_ref, x_ref, feed_ref, gain_ref, bias_ref,
    hidden_ref, normed_ref, inverse_ref, slots_ref, q_ref, home_ref,
    wo, wq, x_rows, blocks, wo_sems, wq_sems, x_sem, own_sem, send_in, recv_in, send_out, recv_out,
    feed_block, feed_sem, feed_send, feed_recv,
):
    p = Place(n, side)
    me = p.z
    size = x_rows.shape[0]
    width = mixed_ref.shape[1]
    loads = [
        pltpu.make_async_copy(mixed_ref.at[rows_at(me, size)], slots_ref.at[me], own_sem),
        pltpu.make_async_copy(x_ref.at[rows_at(me, size)], x_rows, x_sem),
        *load_groups(n, bundle_ref, width, width, wo, wo_sems),
        *load_groups(n, bundle_ref, 0, width, wq, wq_sems),
    ]
    feed_load = pltpu.make_async_copy(feed_ref, feed_block, feed_sem)
    feed_load.start()
    for load in loads:
        load.start()
    greet(p.line() + p.plane())
    copies = heads_to_tokens(n, mixed_ref, slots_ref, send_in, recv_in)
    feed_load.wait()
    home_copy = pltpu.make_async_copy(feed_block, home_ref.at[p.y, p.x, p.core], feed_sem)
    home_copy.start()
    home_copy.wait()
    spread = Spread(p, home_ref, feed_send, feed_recv)
    spread.first()
    for load in loads:
        load.wait()
    branch = merge_heads(
        n, slots_ref, copies, lambda part, group: dot(part, wo[group], NT), f32(x_rows[...])
    )
    hidden, normed, inverse = layer_norm(branch, gain_ref[0:1, :], bias_ref[0:1, :])
    hidden_ref[...] = hidden
    normed_ref[...] = normed
    inverse_ref[...] = jnp.broadcast_to(inverse, inverse_ref.shape)
    low = bf16(hidden)
    sent = tokens_to_heads(
        n, lambda group: dot(low, wq[group]), blocks, q_ref, send_out, recv_out, own_sem
    )
    spread.second()
    for copy in sent:
        copy.wait()
    spread.finish()


def self_to_cross(n_dp, n, mixed, bundle, tokens, feed_block, gains, biases):
    side = round((n_dp // 2) ** 0.5)
    total, width = mixed.shape
    size, model = total // n, tokens.shape[1]
    shape = jax.ShapeDtypeStruct
    dma = pltpu.SemaphoreType.DMA
    return pl.pallas_call(
        partial(self_to_cross_kernel, n, side),
        out_shape=[
            shape((size, model), jnp.float32),
            shape((size, model), jnp.float32),
            shape((size, 128), jnp.float32),
            shape((n, size, width), jnp.bfloat16),
            shape((total, width), jnp.bfloat16),
            shape((side, side, 2) + feed_block.shape, jnp.bfloat16),
        ],
        in_specs=[ANYWHERE] * 4 + [IN_VMEM] * 2,
        out_specs=[IN_VMEM] * 4 + [ANYWHERE] * 2,
        scratch_shapes=[
            pltpu.VMEM((n, model, width), jnp.bfloat16),
            pltpu.VMEM((n, model, width), jnp.bfloat16),
            pltpu.VMEM((size, model), jnp.bfloat16),
            pltpu.VMEM((n, size, width), jnp.bfloat16),
            dma((n,)), dma((n,)), dma, dma,
            dma((n - 1,)), dma((n - 1,)), dma((n - 1,)), dma((n - 1,)),
            pltpu.VMEM(feed_block.shape, jnp.bfloat16),
            dma, Spread.sems(side), Spread.sems(side),
        ],
        compiler_params=pltpu.CompilerParams(
            collective_id=1, has_side_effects=True, vmem_limit_bytes=VMEM_LIMIT
        ),
        cost_estimate=pl.CostEstimate(
            flops=10**9, bytes_accessed=8 * total * width, transcendentals=0
        ),
        name="self_to_cross",
    )(mixed, bundle, tokens, feed_block, gains, biases)


def feed_kernel(
    n, side, mixed_ref, bundle_ref, home_ref, hidden_one_ref, cot_ref, gain_ref, bias_ref,
    out_ref, second_ref, dmix_ref, shrink_grad_ref, expand_grad_ref, wo_grad_ref, norm_grad_ref,
    wo, weights, slots, hidden_two, normed_two, low_two, low_three, act, slope,
    y_own, y_send, y_recv, d_send, d_recv, cot, blocks,
    load_sems, wo_sems, own_sem, send_in, recv_in, send_out, recv_out, pair_send, pair_recv,
    home_sems, home_send, home_recv,
):
    p = Place(n, side)
    me = p.z
    mate = {"mp": me + 1 - 2 * lax.rem(me, 2)}
    size = cot.shape[0]
    half = size // 2
    width = mixed_ref.shape[1]
    hidden_units = act.shape[1]
    chunk = min(512, hidden_units)
    loads = [
        pltpu.make_async_copy(mixed_ref.at[rows_at(me, size)], slots.at[me], load_sems.at[0]),
        *load_groups(n, bundle_ref, 2 * width, width, wo, wo_sems),
        pltpu.make_async_copy(cot_ref.at[rows_at(me, size)], cot, load_sems.at[1]),
    ]
    rows = home_ref.shape[3]
    places = [(y, x) for y in range(side) for x in range(side)]
    spots = [rows_at((y * side + x) * 2 + p.core, rows) for y, x in places]
    homes = [
        pltpu.make_async_copy(home_ref.at[y, x, p.core], weights.at[spot], home_sems.at[index])
        for index, ((y, x), spot) in enumerate(zip(places, spots))
    ]
    for load in loads + homes:
        load.start()
    greet(p.line() + [p.sibling()])
    copies = heads_to_tokens(n, mixed_ref, slots, send_in, recv_in)
    home_copies = [
        push(
            home_ref.at[y, x, p.core], weights.at[spot],
            home_send.at[index], home_recv.at[index], p.sibling(),
        )
        for index, ((y, x), spot) in enumerate(zip(places, spots))
    ]
    for load in loads[: n + 1]:
        load.wait()
    branch = merge_heads(
        n, slots, copies, lambda part, group: dot(part, wo[group], NT), hidden_one_ref[...]
    )
    hidden, normed, inverse_two = layer_norm(branch, gain_ref[1:2, :], bias_ref[1:2, :])
    hidden_two[...] = hidden
    normed_two[...] = normed
    low_two[:size, :] = bf16(hidden)
    own, other = pl.ds(0, size), pl.ds(size, size)
    pair = []

    def to_mate(source, target):
        index = len(pair)
        pair.append(push(source, target, pair_send.at[index], pair_recv.at[index], mate))
        return pair[-1]

    hidden_copy = to_mate(low_two.at[own], low_two.at[other])
    for copy in homes:
        copy.wait()
    for copy in home_copies:
        copy.wait_recv()
    expand = weights.at[:, pl.ds(0, hidden_units)]
    shrink = weights.at[:, pl.ds(hidden_units, hidden_units)]

    def expand_rows(start, count):
        rows = low_two[start : start + count, :]
        for first in range(0, hidden_units, chunk):
            pre = dot(rows, expand[:, first : first + chunk])
            cdf = 0.5 + 0.5 * lax.erf(pre * 0.7071067811865476)
            act[start : start + count, first : first + chunk] = bf16(pre * cdf)
            slope[start : start + count, first : first + chunk] = bf16(
                cdf + pre * jnp.exp(-0.5 * pre * pre) * 0.3989422804014327
            )

    expand_rows(0, size)
    hidden_copy.wait_recv()
    y_copies = []
    for start in (0, half):
        expand_rows(size + start, half)
        y_send[start : start + half, :] = bf16(
            dot(act[size + start : size + start + half, :], shrink[...], NT)
        )
        y_copies.append(to_mate(y_send.at[pl.ds(start, half)], y_recv.at[pl.ds(start, half)]))
    y_own[...] = dot(act[:size, :], shrink[...], NT)
    for copy in y_copies:
        copy.wait_recv()
    output, normed, inverse = layer_norm(
        hidden_two[...] + y_own[...] + f32(y_recv[...]), gain_ref[2:3, :], bias_ref[2:3, :]
    )
    out_ref[...] = bf16(output)
    loads[n + 1].wait()
    third, gain_three, bias_three = norm_back(f32(cot[...]), normed, inverse, gain_ref[2:3, :])
    low_three[:size, :] = bf16(third)
    grad_copy = to_mate(low_three.at[own], low_three.at[other])

    def back_rows(start, count):
        rows = low_three[start : start + count, :]
        for first in range(0, hidden_units, chunk):
            grad = dot(rows, shrink[:, first : first + chunk])
            spot = (slice(start, start + count), slice(first, first + chunk))
            slope[spot] = bf16(grad * f32(slope[spot]))

    back_rows(0, size)
    grad_copy.wait_recv()
    d_copies = []
    for start in (0, half):
        back_rows(size + start, half)
        d_send[start : start + half, :] = bf16(
            dot(slope[size + start : size + start + half, :], expand[...], NT)
        )
        d_copies.append(to_mate(d_send.at[pl.ds(start, half)], d_recv.at[pl.ds(start, half)]))
    y_own[...] = third + dot(slope[:size, :], expand[...], NT)
    for copy in d_copies:
        copy.wait_recv()
    second, gain_two, bias_two = norm_back(
        y_own[...] + f32(d_recv[...]), normed_two[...], inverse_two, gain_ref[1:2, :]
    )
    second_ref[...] = second
    low = bf16(second)
    sent = tokens_to_heads(
        n, lambda group: dot(low, wo[group]), blocks, dmix_ref, send_out, recv_out, own_sem
    )
    norm_grad_ref[...] = jnp.concatenate(
        [gain_two, gain_three, bias_two, bias_three, jnp.zeros((4, norm_grad_ref.shape[1]))], axis=0
    )
    for first in range(0, low_two.shape[1], 256):
        rows = slice(first, first + 256)
        shrink_grad_ref[rows, :] = bf16(dot(low_three[:, rows], act[...], TN))
        expand_grad_ref[rows, :] = bf16(dot(low_two[:, rows], slope[...], TN))
    for group in range(n):
        wo_grad_ref[:, group * width : (group + 1) * width] = bf16(dot(low, slots[group], TN))
    for copy in sent:
        copy.wait()
    for copy in pair + home_copies:
        copy.wait_send()


def feed(n, mixed, bundle, home, hidden_one, cotangent, gains, biases):
    total, width = mixed.shape
    side, model, units = home.shape[0], hidden_one.shape[1], home.shape[4] // 2
    size = total // n
    shape = jax.ShapeDtypeStruct
    dma = pltpu.SemaphoreType.DMA
    low, wide = jnp.bfloat16, jnp.float32
    return pl.pallas_call(
        partial(feed_kernel, n, side),
        out_shape=[
            shape((size, model), low),
            shape((size, model), wide),
            shape((total, width), low),
            shape((model, units), low),
            shape((model, units), low),
            shape((model, model), low),
            shape((8, model), wide),
        ],
        in_specs=[ANYWHERE] * 3 + [IN_VMEM, ANYWHERE] + [IN_VMEM] * 2,
        out_specs=[IN_VMEM] * 2 + [ANYWHERE] + [IN_VMEM] * 4,
        scratch_shapes=[
            pltpu.VMEM((n, model, width), low),
            pltpu.VMEM((model, 2 * units), low),
            pltpu.VMEM((n, size, width), low),
            pltpu.VMEM((size, model), wide),
            pltpu.VMEM((size, model), wide),
            pltpu.VMEM((2 * size, model), low),
            pltpu.VMEM((2 * size, model), low),
            pltpu.VMEM((2 * size, units), low),
            pltpu.VMEM((2 * size, units), low),
            pltpu.VMEM((size, model), wide),
            pltpu.VMEM((size, model), low),
            pltpu.VMEM((size, model), low),
            pltpu.VMEM((size, model), low),
            pltpu.VMEM((size, model), low),
            pltpu.VMEM((size, model), low),
            pltpu.VMEM((n, size, width), low),
            dma((2,)), dma((n,)), dma,
            dma((n - 1,)), dma((n - 1,)), dma((n - 1,)), dma((n - 1,)),
            dma((6,)), dma((6,)),
            dma((side * side,)), dma((side * side,)), dma((side * side,)),
        ],
        compiler_params=pltpu.CompilerParams(
            collective_id=2, has_side_effects=True, vmem_limit_bytes=VMEM_LIMIT
        ),
        cost_estimate=pl.CostEstimate(
            flops=80 * 10**9, bytes_accessed=8 * total * width, transcendentals=0
        ),
        name="feed",
    )(mixed, bundle, home, hidden_one, cotangent, gains, biases)


def cross_to_self_kernel(
    n, dq_ref, bundle_ref, second_ref, hidden_ref, normed_ref, inverse_ref, mixed_ref, gain_ref, norm_ref,
    first_ref, dmix_ref, weight_grad_ref, norm_grad_ref,
    wo, wq, slots, blocks, wo_sems, wq_sems, own_sem, send_in, recv_in, send_out, recv_out,
):
    p = Place(n, 1)
    me = p.z
    size, model = second_ref.shape
    width = dq_ref.shape[1]
    loads = [
        pltpu.make_async_copy(dq_ref.at[rows_at(me, size)], slots.at[me], own_sem),
        *load_groups(n, bundle_ref, 0, width, wq, wq_sems),
        *load_groups(n, bundle_ref, width, width, wo, wo_sems),
    ]
    for load in loads:
        load.start()
    greet(p.line())
    copies = heads_to_tokens(n, dq_ref, slots, send_in, recv_in)
    for load in loads:
        load.wait()
    upstream = merge_heads(
        n, slots, copies, lambda part, group: dot(part, wq[group], NT), second_ref[...]
    )
    first, gain_one, bias_one = norm_back(
        upstream, normed_ref[...], inverse_ref[:, 0:1], gain_ref[0:1, :]
    )
    first_ref[...] = first
    low = bf16(first)
    sent = tokens_to_heads(
        n, lambda group: dot(low, wo[group]), blocks, dmix_ref, send_out, recv_out, own_sem
    )
    hidden_low = bf16(hidden_ref[...])
    for group in range(n):
        cols = 2 * group * width
        weight_grad_ref[:, cols : cols + width] = bf16(dot(hidden_low, slots[group], TN))
        weight_grad_ref[:, cols + width : cols + 2 * width] = bf16(dot(low, mixed_ref[group], TN))
    rows = jnp.concatenate(
        [
            gain_one, norm_ref[0:2, :], bias_one, norm_ref[2:4, :],
            jnp.zeros((122, model), jnp.float32),
        ],
        axis=0,
    )
    norm_grad_ref[...] = bf16(rows.T)
    for copy in sent:
        copy.wait()


def cross_to_self(n, dq, bundle, second, hidden, normed, inverse, slots, gains, norm_rows):
    total, width = dq.shape
    size, model = second.shape
    shape = jax.ShapeDtypeStruct
    dma = pltpu.SemaphoreType.DMA
    return pl.pallas_call(
        partial(cross_to_self_kernel, n),
        out_shape=[
            shape((size, model), jnp.float32),
            shape((total, width), jnp.bfloat16),
            shape((model, 2 * model), jnp.bfloat16),
            shape((model, 128), jnp.bfloat16),
        ],
        in_specs=[ANYWHERE] * 2 + [IN_VMEM] * 7,
        out_specs=[IN_VMEM, ANYWHERE, IN_VMEM, IN_VMEM],
        scratch_shapes=[
            pltpu.VMEM((n, model, width), jnp.bfloat16),
            pltpu.VMEM((n, model, width), jnp.bfloat16),
            pltpu.VMEM((n, size, width), jnp.bfloat16),
            pltpu.VMEM((n, size, width), jnp.bfloat16),
            dma((n,)), dma((n,)), dma,
            dma((n - 1,)), dma((n - 1,)), dma((n - 1,)), dma((n - 1,)),
        ],
        compiler_params=pltpu.CompilerParams(
            collective_id=3, has_side_effects=True, vmem_limit_bytes=VMEM_LIMIT
        ),
        cost_estimate=pl.CostEstimate(
            flops=10**9, bytes_accessed=8 * total * width, transcendentals=0
        ),
        name="cross_to_self",
    )(dq, bundle, second, hidden, normed, inverse, slots, gains, norm_rows)


class Reduce:
    def __init__(self, place, sources, scratch):
        self.place, self.sources = place, sources
        (
            self.keep, self.first_a, self.first_b, self.second_a, self.second_b,
            self.local, self.send, self.recv,
        ) = scratch
        self.half = self.keep.shape[2] // 2
        self.copies = {"core": [], "first": [], "second": []}
        self.index = 0

    @staticmethod
    def scratch(side, rows, columns, sources):
        low, dma = jnp.bfloat16, pltpu.SemaphoreType.DMA
        block = pltpu.VMEM((side, side, rows, columns), low)
        first = pltpu.VMEM((side - 1, side, rows // 2, columns), low)
        second = pltpu.VMEM((side - 1, rows // 2, columns), low)
        count = sources + 4 * (side - 1)
        return [
            block, first, first, second, second, dma((2, sources)), dma((count,)), dma((count,)),
        ]

    def _push(self, stage, source, target, to):
        spot = self.index
        self.index += 1
        self.copies[stage].append(push(source, target, self.send.at[spot], self.recv.at[spot], to))

    def core_start(self):
        p, column = self.place, 0
        for source in self.sources:
            cols = pl.ds(column, source.shape[4])
            column += source.shape[4]
            self._push(
                "core", source.at[:, :, 1 - p.core], self.keep.at[:, :, :, cols], p.sibling()
            )

    def _load(self, stage, index):
        y, x = index // self.place.side, index % self.place.side
        column, loads = 0, []
        for spot, source in enumerate(self.sources):
            cols = pl.ds(column, source.shape[4])
            column += source.shape[4]
            loads.append(
                pltpu.make_async_copy(
                    source.at[y, x, self.place.core], stage.at[index % 2, :, cols],
                    self.local.at[index % 2, spot],
                )
            )
        return loads

    def core_finish(self, stage):
        side, keep, columns = self.place.side, self.keep, self.keep.shape[3]
        for load in self._load(stage, 0):
            load.start()
        for copy in self.copies["core"]:
            copy.wait_recv()
        for index in range(side * side):
            if index + 1 < side * side:
                for load in self._load(stage, index + 1):
                    load.start()
            for load in self._load(stage, index):
                load.wait()
            y, x = index // side, index % side
            keep[y, x] = bf16(f32(keep[y, x]) + f32(stage[index % 2, :, :columns]))

    def first_start(self):
        p, half = self.place, self.half
        top, bottom = pl.ds(0, half), pl.ds(half, half)
        for step in range(1, p.side):
            other, to = p.x_peer(step)
            self._push("first", self.keep.at[:, other, top], self.first_a.at[step - 1], to)
            other, to = p.y_peer(step)
            self._push("first", self.keep.at[other, :, bottom], self.first_b.at[step - 1], to)

    def first_finish(self):
        p, half, keep = self.place, self.half, self.keep
        for copy in self.copies["first"]:
            copy.wait_recv()

        def add(index, carry):
            total = f32(keep[index, p.x, :half, :])
            for step in range(p.side - 1):
                total = total + f32(self.first_a[step, index])
            keep[index, p.x, :half, :] = bf16(total)
            total = f32(keep[p.y, index, half:, :])
            for step in range(p.side - 1):
                total = total + f32(self.first_b[step, index])
            keep[p.y, index, half:, :] = bf16(total)
            return carry

        lax.fori_loop(0, p.side, add, 0)

    def second_start(self):
        p, half = self.place, self.half
        top, bottom = pl.ds(0, half), pl.ds(half, half)
        for step in range(1, p.side):
            other, to = p.y_peer(step)
            self._push("second", self.keep.at[other, p.x, top], self.second_a.at[step - 1], to)
            other, to = p.x_peer(step)
            self._push("second", self.keep.at[p.y, other, bottom], self.second_b.at[step - 1], to)

    def second_wait(self):
        for copy in self.copies["second"]:
            copy.wait_recv()

    def total(self, cols):
        p, half = self.place, self.half
        top, bottom = f32(self.keep[p.y, p.x, :half, cols]), f32(self.keep[p.y, p.x, half:, cols])
        for step in range(p.side - 1):
            top = top + f32(self.second_a[step, :, cols])
            bottom = bottom + f32(self.second_b[step, :, cols])
        return jnp.concatenate([top, bottom], axis=0)

    def finish(self):
        for stage in self.copies.values():
            for copy in stage:
                copy.wait_send()


class Fold:
    def __init__(self, place, make, out, scratch):
        self.n, self.me, self.make, self.out = place.n, place.z, make, out
        self.parts, self.held, self.down_send, self.down_recv, self.back_send, self.back_recv, self.own = scratch
        self.chunks = self.held.shape[1]
        self.ring = self.parts.shape[1]
        self.ticks = self.chunks + 2 * (self.n - 1) - 1

    @staticmethod
    def scratch(chunks, rows, columns, ring=6):
        low, dma = jnp.bfloat16, pltpu.SemaphoreType.DMA((2, chunks))
        return [
            pltpu.VMEM((2, ring, rows, columns), low), pltpu.VMEM((2, chunks, rows, columns), low),
            dma, dma, dma, dma, dma,
        ]

    def _flows(self):
        n, me = self.n, self.me
        return (
            (0, me, lax.rem(me + 1, n), lax.rem(me + n - 1, n)),
            (1, n - 1 - me, lax.rem(me + n - 1, n), lax.rem(me + 1, n)),
        )

    def _down(self, flow, chunk, to, first):
        source = self.parts.at[flow, lax.rem(chunk, self.ring)] if first else self.held.at[flow, chunk]
        return pltpu.make_async_remote_copy(
            source, self.held.at[flow, chunk],
            self.down_send.at[flow, chunk], self.down_recv.at[flow, chunk],
            device_id={"mp": to}, device_id_type=MESH,
        )

    def _back(self, flow, chunk, to, first):
        source = (self.held if first else self.out).at[flow, chunk]
        return pltpu.make_async_remote_copy(
            source, self.out.at[flow, chunk],
            self.back_send.at[flow, chunk], self.back_recv.at[flow, chunk],
            device_id={"mp": to}, device_id_type=MESH,
        )

    def _keep(self, flow, chunk):
        return pltpu.make_async_copy(
            self.held.at[flow, chunk], self.out.at[flow, chunk], self.own.at[flow, chunk]
        )

    def tick(self, tick):
        last = self.n - 1
        for flow, spot, ahead, behind in self._flows():
            if tick < self.chunks:
                if tick >= self.ring:

                    @pl.when(spot == 0)
                    def _():
                        self._down(flow, tick - self.ring, ahead, True).wait_send()

                self.parts[flow, tick % self.ring] = bf16(self.make(flow, tick))

                @pl.when(spot == 0)
                def _():
                    self._down(flow, tick, ahead, True).start()

            chunk = tick - spot

            @pl.when((spot > 0) & (chunk >= 0) & (chunk < self.chunks))
            def _():
                self._down(flow, chunk, ahead, False).wait_recv()
                self.held[flow, chunk] = bf16(
                    f32(self.held[flow, chunk]) + f32(self.parts[flow, lax.rem(chunk, self.ring)])
                )

                @pl.when(spot < last)
                def _():
                    self._down(flow, chunk, ahead, False).start()

                @pl.when(spot == last)
                def _():
                    self._back(flow, chunk, behind, True).start()
                    self._keep(flow, chunk).start()

            given = tick - 2 * last + spot

            @pl.when((spot > 0) & (spot < last) & (given >= 0) & (given < self.chunks))
            def _():
                self._back(flow, given, behind, False).wait_recv()
                self._back(flow, given, behind, False).start()

    def finish(self):
        last = self.n - 1
        for flow, spot, ahead, behind in self._flows():

            @pl.when(spot == 0)
            def _():
                def wait(chunk, carry):
                    self._back(flow, chunk, behind, False).wait_recv()
                    return carry

                lax.fori_loop(0, self.chunks, wait, 0)

                def sent(chunk, carry):
                    self._down(flow, chunk, ahead, True).wait_send()
                    return carry

                lax.fori_loop(max(self.chunks - self.ring, 0), self.chunks, sent, 0)

            @pl.when((spot > 0) & (spot < last))
            def _():
                def sent(chunk, carry):
                    self._down(flow, chunk, ahead, False).wait_send()
                    self._back(flow, chunk, behind, False).wait_send()
                    return carry

                lax.fori_loop(0, self.chunks, sent, 0)

            @pl.when(spot == last)
            def _():
                def sent(chunk, carry):
                    self._back(flow, chunk, behind, True).wait_send()
                    self._keep(flow, chunk).wait()
                    return carry

                lax.fori_loop(0, self.chunks, sent, 0)


class Everyone:
    def __init__(self, n_dp, n_mp, mine, slots, send_sems, recv_sems):
        self.n, self.n_mp = n_dp * n_mp, n_mp
        self.me = lax.axis_index("dp") * n_mp + lax.axis_index("mp")
        self.mine, self.slots, self.send, self.recv = mine, slots, send_sems, recv_sems

    def _to(self, distance):
        to = lax.rem(self.me + distance, self.n)
        return {"dp": to // self.n_mp, "mp": lax.rem(to, self.n_mp)}

    def _copy(self, distance):
        return pltpu.make_async_remote_copy(
            self.mine, self.slots.at[self.me], self.send.at[distance - 1], self.recv.at[distance - 1],
            device_id=self._to(distance), device_id_type=MESH,
        )

    def greet(self):
        barrier = pltpu.get_barrier_semaphore()

        def signal(distance, carry):
            pl.semaphore_signal(barrier, inc=1, device_id=self._to(distance), device_id_type=MESH)
            return carry

        lax.fori_loop(1, self.n, signal, 0)
        pl.semaphore_wait(barrier, self.n - 1)

    def total(self):
        def start(distance, carry):
            self._copy(distance).start()
            return carry

        def wait(distance, carry):
            self._copy(distance).wait()
            return carry

        self.slots[self.me] = self.mine[...]
        lax.fori_loop(1, self.n, start, 0)
        lax.fori_loop(1, self.n, wait, 0)
        return jnp.sum(self.slots[...], axis=0)


def moments(upstream, first_moment, second_moment, master, decay):
    first_new = first_decay * first_moment + (1.0 - first_decay) * upstream
    second_new = second_decay * second_moment + (1.0 - second_decay) * upstream * upstream
    direction = (
        first_new
        / (1.0 - first_decay**STEP)
        / (jnp.sqrt(second_new / (1.0 - second_decay**STEP)) + epsilon)
        + decay * master
    )
    return (first_new, second_new, direction)


def tensors(inner, outer, expand, shrink, norms):
    found = [inner.at[a, c] for a in range(2) for c in range(3)]
    found += [outer.at[0], outer.at[1], expand, shrink]
    found += [norms.at[pl.ds(row, 1)] for row in range(6)]
    return list(zip(found, [weight_decay] * 10 + [0.0] * 6))


def square_row(squares, share):
    lane = lax.broadcasted_iota(jnp.int32, (1, 128), 1)
    row = jnp.zeros((1, 128), jnp.float32)
    for index, values in enumerate(squares):
        total = jnp.sum(jnp.sum(values, axis=0, keepdims=True), axis=1, keepdims=True)
        row = jnp.where(lane == index, total * share if index >= 10 else total, row)
    return row


def update_kernel(*refs):
    (
        sums_ref, grads, weights, firsts, seconds, table_ref,
        new_weights, new_firsts, new_seconds,
    ) = refs[0], refs[1:6], refs[6:11], refs[11:16], refs[16:21], refs[21], refs[22:27], refs[27:32], refs[32:37]
    lane = lax.broadcasted_iota(jnp.int32, (1, 128), 1)
    counts = jnp.where(lane < 8, float(D * D), jnp.where(lane < 10, float(D * FF), float(D)))
    weight_norm = jnp.sqrt(sums_ref[0:1, :] / counts)
    update_norm = jnp.sqrt(sums_ref[1:2, :] / counts)
    trust = weight_norm / (update_norm + epsilon)
    table_ref[...] = jnp.concatenate([weight_norm, update_norm, trust], axis=0)[:, :16]
    groups = [tensors(*group) for group in (grads, weights, firsts, seconds, new_weights, new_firsts, new_seconds)]
    for index, parts in enumerate(zip(*groups)):
        grad, weight, first, second, new_weight, new_first, new_second = [part[0] for part in parts]
        ratio = jnp.sum(jnp.where(lane == index, trust, 0.0), axis=1, keepdims=True)
        master = weight[...]
        first_new, second_new, direction = moments(
            grad[...], first[...], second[...], master, parts[0][1]
        )
        new_first[...] = first_new
        new_second[...] = second_new
        new_weight[...] = master - learn_rate * ratio * direction


def update(sums, grads, weights, firsts, seconds):
    shape = lambda values: jax.ShapeDtypeStruct(values.shape, jnp.float32)
    results = [shape(values) for values in weights]
    return pl.pallas_call(
        update_kernel,
        out_shape=[jax.ShapeDtypeStruct((3, 16), jnp.float32)] + results * 3,
        compiler_params=pltpu.CompilerParams(vmem_limit_bytes=VMEM_LIMIT),
        name="update",
    )(sums, *grads, *weights, *firsts, *seconds)


def finish_kernel(
    n, side, units, width, dq_ref, dk_ref, dv_ref, near_ref, x_ref, first_ref,
    cross_dk_ref, cross_dv_ref, source_ref,
    shrink_ref, expand_ref, cross_wo_ref, weight_ref, norm_ref, source_grad_ref, *refs,
):
    states, refs = refs[:15], refs[15:]
    out_ref, sums_ref, grads, refs = refs[0], refs[1], refs[2:7], refs[7:]
    masters, refs = refs[:15], refs[15:]
    (
        master_sems, inner, stage, far_send, far_recv, group_send, group_recv,
        far_send_sem, far_recv_sem, group_send_sems, group_recv_sems,
        mine, slots, everyone_send, everyone_recv, *scratch,
    ) = refs
    n_dp = 2 * side * side
    p = Place(n, side)
    everyone = Everyone(n_dp, n, mine, slots, everyone_send, everyone_recv)
    master_loads = [
        pltpu.make_async_copy(source, target, master_sems.at[index])
        for index, (source, target) in enumerate(zip(states, masters))
    ]
    me = p.z
    own_heads = (dq_ref, dk_ref, dv_ref)
    size, model = first_ref.shape
    rows = inner.shape[3]
    chunk_rows = out_ref.shape[2]
    source_chunks = cross_dk_ref.shape[0] // (2 * chunk_rows)

    def make(flow, chunk):
        if chunk < source_chunks:
            spot = pl.ds((flow * source_chunks + chunk) * chunk_rows, chunk_rows)
            return dot(cross_dk_ref[spot, :], source_ref[:, :width], NT) + dot(
                cross_dv_ref[spot, :], source_ref[:, width:], NT
            )
        tokens = x_ref.shape[0]
        start = flow * (tokens // 2) + (chunk - source_chunks) * chunk_rows
        spot = pl.ds(start, chunk_rows)
        total = jnp.zeros((chunk_rows, model), jnp.float32)
        for index, own in enumerate(own_heads):
            total = total + dot(own[spot, :], near_ref[:, index * width : (index + 1) * width], NT)
        here = first_ref[start % size : start % size + chunk_rows, :]
        return total + jnp.where(me == start // size, here, 0.0)

    fold = Fold(p, make, out_ref, scratch[:7])
    feed_sum = Reduce(p, [shrink_ref, expand_ref], scratch[7:15])
    group_sum = Reduce(p, [cross_wo_ref, weight_ref, norm_ref, source_grad_ref], scratch[15:23])
    inner_sum = Reduce(p, [inner], scratch[23:31])

    everyone.greet()
    feed_sum.core_start()
    group_sum.core_start()

    ticks = iter(range(fold.ticks))

    def advance(count):
        for _ in range(count):
            fold.tick(next(ticks))

    advance(2)
    for load in master_loads:
        load.start()

    per = 256
    for start in range(0, model, per):
        turned = x_ref[:, start : start + per]
        for index, own in enumerate(own_heads):
            block = bf16(dot(turned, own[...], TN))
            for row in range(0, per, rows):
                flat = (start + row) // rows
                y, x, core = flat // (2 * side), flat // 2 % side, flat % 2
                inner[y, x, core, :, index * width : (index + 1) * width] = block[row : row + rows]
    inner_sum.core_start()
    for load in master_loads:
        load.wait()
    weights, firsts, seconds = (tensors(*masters[index : index + 5]) for index in (0, 5, 10))
    share = 1.0 / n
    mine[...] = jnp.zeros(mine.shape, jnp.float32)
    mine[0:1, :] = square_row([ref[...] * ref[...] for ref, _ in weights], share)
    feed_sum.core_finish(stage)
    feed_sum.first_start()
    advance(1)
    inner_sum.core_finish(stage)
    group_sum.core_finish(stage)
    group_sum.first_start()
    inner_sum.first_start()
    advance(2)
    feed_sum.first_finish()
    feed_sum.second_start()
    advance(2)
    feed_sum.second_wait()
    far = {"mp": lax.rem(me + n // 2, n)}
    far_send[:, :units] = bf16(feed_sum.total(slice(units, 2 * units)))
    far_send[:, units:] = bf16(feed_sum.total(slice(3 * units, 4 * units)))
    far_copy = push(far_send, far_recv, far_send_sem, far_recv_sem, far)
    group_sum.first_finish()
    inner_sum.first_finish()
    group_sum.second_start()
    inner_sum.second_start()
    advance(2)
    group_sum.second_wait()
    whole = n * width
    for group in range(n):
        group_send[group, :, :width] = bf16(
            group_sum.total(slice(group * width, (group + 1) * width))
        )
        start = whole + 2 * group * width
        group_send[group, :, width : 3 * width] = bf16(
            group_sum.total(slice(start, start + 2 * width))
        )
        group_send[group, :, 3 * width :] = bf16(
            group_sum.total(slice(3 * whole, 3 * whole + norm_ref.shape[4]))
        )
    group_copies = []
    for distance in range(1, n):
        to = lax.rem(me + distance, n)
        group_copies.append(
            push(
                group_send.at[to], group_recv.at[distance - 1],
                group_send_sems.at[distance - 1], group_recv_sems.at[distance - 1], {"mp": to},
            )
        )
    grad_inner, grad_outer, grad_expand, grad_shrink, grad_norms = grads
    advance(1)
    inner_sum.second_wait()
    for index in range(3):
        grad_inner[0, index] = inner_sum.total(slice(index * width, (index + 1) * width))
    start = 3 * whole + norm_ref.shape[4]
    for index in range(2):
        grad_inner[1, index + 1] = group_sum.total(
            slice(start + index * width, start + (index + 1) * width)
        )
    advance(2)
    far_copy.wait_recv()
    grad_shrink[...] = (feed_sum.total(slice(0, units)) + f32(far_recv[:, :units])).T
    grad_expand[...] = feed_sum.total(slice(2 * units, 3 * units)) + f32(far_recv[:, units:])

    def direction_square(index):
        (grad, decay), first, second, weight = [group[index] for group in (found, firsts, seconds, weights)]
        step = moments(grad[...], first[0][...], second[0][...], weight[0][...], decay)[2]
        return step * step

    found = tensors(*grads)
    early = {index: direction_square(index) for index in (0, 1, 2, 4, 5, 8, 9)}
    advance(1)
    for distance in range(1, n):
        group_copies[distance - 1].wait_recv()
    received = lambda cols: sum(
        [f32(group_recv[distance - 1, :, cols]) for distance in range(1, n)], f32(group_send[me, :, cols])
    )
    grad_outer[1] = received(slice(0, width)).T
    grad_inner[1, 0] = received(slice(width, 2 * width))
    grad_outer[0] = received(slice(2 * width, 3 * width)).T
    grad_norms[...] = received(slice(3 * width, 3 * width + norm_ref.shape[4])).T[:6, :]
    advance(1)
    mine[1:2, :] = square_row(
        [early[index] if index in early else direction_square(index) for index in range(16)], share
    )
    sums_ref[...] = everyone.total()
    for tick in ticks:
        fold.tick(tick)
    fold.finish()
    for copy in (far_copy, *group_copies):
        copy.wait_send()
    for batch in (feed_sum, group_sum, inner_sum):
        batch.finish()


def finish(
    n_dp, n_mp, own_heads, near, tokens, first, source_heads, source_weights,
    shrink, expand, cross_wo, weights, norms, source_grad, states,
):
    side = round((n_dp // 2) ** 0.5)
    total, width = own_heads[0].shape
    size, model = first.shape
    units = expand.shape[1] // 2
    rows = model // n_dp
    low, wide = jnp.bfloat16, jnp.float32
    shape = jax.ShapeDtypeStruct
    dma = pltpu.SemaphoreType.DMA
    by_place = lambda values: values.reshape(side, side, 2, rows, values.shape[1])
    early = [by_place(values) for values in (shrink, expand, cross_wo, weights, norms, source_grad)]
    columns = [sum(values.shape[4] for values in group) for group in (early[:2], early[2:])]
    bundle = 3 * width + norms.shape[1]
    devices = n_dp * n_mp
    chunk_rows = min(128, size // 2)
    chunks = (total + source_heads[0].shape[0]) // (2 * chunk_rows)
    both, sums, *grads = pl.pallas_call(
        partial(finish_kernel, n_mp, side, units, width),
        out_shape=[shape((2, chunks, chunk_rows, model), low), shape((8, 128), wide)]
        + [shape(values.shape, wide) for values in states[:5]],
        in_specs=[IN_VMEM] * 9 + [ANYWHERE] * (6 + len(states)),
        out_specs=[ANYWHERE] + [IN_VMEM] * 6,
        scratch_shapes=[
            *[pltpu.VMEM(values.shape, wide) for values in states],
            dma((len(states),)),
            pltpu.VMEM((side, side, 2, rows, 3 * width), low),
            pltpu.VMEM((2, rows, max(columns)), low),
            pltpu.VMEM((rows, 2 * units), low),
            pltpu.VMEM((rows, 2 * units), low),
            pltpu.VMEM((n_mp, rows, bundle), low),
            pltpu.VMEM((n_mp - 1, rows, bundle), low),
            dma, dma, dma((n_mp - 1,)), dma((n_mp - 1,)),
            pltpu.VMEM((8, 128), wide),
            pltpu.VMEM((devices, 8, 128), wide),
            dma((devices - 1,)), dma((devices - 1,)),
            *Fold.scratch(chunks, chunk_rows, model),
            *Reduce.scratch(side, rows, columns[0], 2),
            *Reduce.scratch(side, rows, columns[1], 4),
            *Reduce.scratch(side, rows, 3 * width, 1),
        ],
        compiler_params=pltpu.CompilerParams(
            collective_id=5, has_side_effects=True, vmem_limit_bytes=VMEM_LIMIT
        ),
        cost_estimate=pl.CostEstimate(flops=10**9, bytes_accessed=1 << 20, transcendentals=0),
        name="finish",
    )(*own_heads, near, tokens, first, *source_heads, source_weights, *early, *states)
    split = source_heads[0].shape[0] // (2 * chunk_rows)
    return both[:, :split], both[:, split:], sums, grads


def on_device(
    inputs,
    encoder,
    prefix,
    cotangent,
    inner_weights,
    inner_first,
    inner_second,
    outer_weights,
    outer_first,
    outer_second,
    expand_weights,
    expand_first,
    expand_second,
    shrink_weights,
    shrink_first,
    shrink_second,
    norm_params,
    norm_first,
    norm_second,
):
    n_dp, n_mp = lax.axis_size("dp"), lax.axis_size("mp")
    seq_count, seq_len, model = inputs.shape
    tokens = inputs.reshape(seq_len, model)
    states = encoder.reshape(-1, model)
    rows, width = inner_weights.shape[2:]
    units = expand_weights.shape[1]

    norm_t = jnp.pad(bf16(norm_params).reshape(6, rows).T, ((0, 0), (0, 122)))
    near, bundle, feed_block = front(
        n_dp, n_mp, inner_weights, bf16(jnp.swapaxes(outer_weights, 1, 2)), norm_t,
        expand_weights, bf16(shrink_weights.T),
    )
    last = n_mp * 3 * width
    source_weights = bundle[:, last : last + 2 * width]
    norm_all = f32(bundle[:, last + 2 * width :].T)
    gains, biases = norm_all[0:3], norm_all[3:6]

    self_proj = bf16(dot(tokens, near))
    split = lambda values, count: [
        values[:, index * width : (index + 1) * width] for index in range(count)
    ]
    self_q, self_k, self_v = split(self_proj, 3)
    self_mixed, self_sums = attend_forward(self_q, self_k, self_v, prefix, True)
    hidden_one, normed_one, inverse_one, self_slots, cross_query, home = self_to_cross(
        n_dp, n_mp, self_mixed, bundle, tokens, feed_block, gains, biases
    )
    cross_k, cross_v = split(bf16(dot(states, source_weights)), 2)
    cross_mixed, cross_sums = attend_forward(cross_query, cross_k, cross_v, prefix, False)
    out_rows, grad_second, cross_dmix, shrink_grad, expand_grad, cross_wo_grad, norm_rows = feed(
        n_mp, cross_mixed, bundle, home, hidden_one, cotangent.reshape(seq_len, model), gains, biases,
    )
    cross_dq, cross_dk, cross_dv, layer_low, source_grad = attend_backward(
        cross_query, cross_k, cross_v, cross_dmix, cross_mixed, cross_sums, prefix, False,
        n_mp, (out_rows,), (states,),
    )
    grad_first, self_dmix, weight_grad, norm_grad = cross_to_self(
        n_mp, cross_dq, bundle, grad_second, hidden_one, normed_one, inverse_one,
        self_slots, gains, norm_rows,
    )
    self_grads = attend_backward(
        self_q, self_k, self_v, self_dmix, self_mixed, self_sums, prefix, True
    )
    flat = lambda values: values.reshape(6, rows)
    weights = [inner_weights, outer_weights, expand_weights, shrink_weights, flat(norm_params)]
    firsts = [inner_first, outer_first, expand_first, shrink_first, flat(norm_first)]
    seconds = [inner_second, outer_second, expand_second, shrink_second, flat(norm_second)]
    encoder_low, input_low, sums, grads = finish(
        n_dp, n_mp, self_grads, near, tokens, grad_first, (cross_dk, cross_dv), source_weights,
        shrink_grad, expand_grad, cross_wo_grad, weight_grad, norm_grad, source_grad,
        weights + firsts + seconds,
    )
    table, *results = update(sums, grads, weights, firsts, seconds)
    for index in (4, 9, 14):
        results[index] = results[index].reshape(2, 3, rows)
    return (
        f32(layer_low).reshape(seq_count, seq_len, model),
        f32(input_low).reshape(seq_count, seq_len, model),
        f32(encoder_low).reshape(seq_count, -1, model),
        *results,
        table,
    )


def solution(mesh):
    placed = (
        P("dp", None, None),
        P("dp", None, None),
        P("dp"),
        P("dp", None, None),
        P(None, None, "dp", "mp"),
        P(None, None, "dp", "mp"),
        P(None, None, "dp", "mp"),
        P(None, "mp", "dp"),
        P(None, "mp", "dp"),
        P(None, "mp", "dp"),
        P("dp", "mp"),
        P("dp", "mp"),
        P("dp", "mp"),
        P("mp", "dp"),
        P("mp", "dp"),
        P("mp", "dp"),
        P(None, None, "dp"),
        P(None, None, "dp"),
        P(None, None, "dp"),
    )
    return jax.shard_map(
        on_device,
        mesh=mesh,
        in_specs=placed,
        out_specs=(
            P("dp", None, None),
            P("dp", None, None),
            P("dp", None, None),
            P(None, None, "dp", "mp"),
            P(None, "mp", "dp"),
            P("dp", "mp"),
            P("mp", "dp"),
            P(None, None, "dp"),
            P(None, None, "dp", "mp"),
            P(None, "mp", "dp"),
            P("dp", "mp"),
            P("mp", "dp"),
            P(None, None, "dp"),
            P(None, None, "dp", "mp"),
            P(None, "mp", "dp"),
            P("dp", "mp"),
            P("mp", "dp"),
            P(None, None, "dp"),
            P(),
        ),
        check_vma=False,
    )
```

time: 1130 us -> 594 us (0.53)
  waiting for transfers between devices: 696 us -> 0 us
  Pallas kernels: 227 us -> 543 us
  local copies, waits for them, and re-layouts: 80.2 us -> 21.1 us
  other arithmetic: 40.5 us -> 11.1 us
  matrix products: 27.4 us -> 6.76 us
  blocking collectives: 20.5 us -> 0 us
  between operations: 17.1 us -> 1.83 us
    pallas_call x5 -> x7, Pallas kernels: 165 us -> 493 us  [the longest x1 227 us: finish(): pl.pallas_call(partial(finish_kernel, n_mp, side, units, width), out_shap...]
    unnamed x24 -> x0, waiting for transfers between devices: 199 us -> none
    all_gather x8 -> x0, waiting for transfers between devices: 193 us -> none  [the longest x1 59.4 us: on_device(): lax.all_gather(outer_low, ('dp', 'mp'))]
    psum x1 -> x0, waiting for transfers between devices: 155 us -> none  [on_device(): encoder_grad = f32(lax.psum(bf16(state_part), 'mp'))]
    reduce_scatter x5 -> x0, waiting for transfers between devices: 103 us -> none  [the longest x4 92.5 us: on_device(): lax.psum_scatter(bf16(values), axis, scatter_dimension=dim, tiled=True)]
    unnamed x113 -> x20, local copies, waits for them, and re-layouts: 56 us -> 5.37 us
    ppermute x4 -> x0, waiting for transfers between devices: 45.9 us -> none  [swap_far(): return lax.ppermute(values, 'mp', [(i, (i + n // 2) % n) for i in range(n)])]
    dot_general x4 -> x0, matrix products: 17.5 us -> none  [the longest x2 8.13 us: on_device(): jnp.einsum('td,cdm->ctm', rows, weights, preferred_element_type=jnp.float32)]
  transfers between devices with their start and end apart: 23 -> 0, of which waited for: 20 -> 0; matrix products, arithmetic and copies ran while one was open for 12% -> 0% of each run, Pallas kernels for 7% -> 0%
where the time goes in v2:
time: 594 us; the launch traced here: 584 us
  Pallas kernels  543 us (91%)
  local copies, waits for them, and re-layouts  21.1 us (4%)
  other arithmetic  11.1 us (2%)
  matrix products  6.76 us (1%)
    pallas_call x1, Pallas kernels, finish(): pl.pallas_call(partial(finish_kernel, n_mp, side, units, width), out_shap...  227 us
    pallas_call x1, Pallas kernels, feed(): pl.pallas_call(partial(feed_kernel, n, side), out_shape=[shape((size, mod...  85.2 us
    pallas_call x1, Pallas kernels, front(): pl.pallas_call(partial(front_kernel, n_mp, side), out_shape=[jax.ShapeDty...  61.6 us
    pallas_call x1, Pallas kernels, self_to_cross(): pl.pallas_call(partial(self_to_cross_kernel, n, side), out_shape=[shape((...  58.3 us
    pallas_call x2, Pallas kernels, attend_backward(): pl.pallas_call(partial(backward_kernel, masked, block, n), grid_spec=pltp...  52.9 us
    pallas_call x1, Pallas kernels, cross_to_self(): pl.pallas_call(partial(cross_to_self_kernel, n), out_shape=[shape((size,...  26.7 us
    pallas_call x2, Pallas kernels, attend_forward(): pl.pallas_call(partial(forward_kernel, masked, block), grid_spec=pltpu.Pr...  23.7 us

profile of v2, /device:TPU:0, one launch (start us, length us, event | category | flops | bytes accessed | tf_op | source)
XLA Modules:
  0.0 583.8 jit_solution(1866233118486606134)
XLA Ops:
  0.7 1.9 copy.57
  2.5 1.7 copy.54
  4.2 0.7 convert_element_type.38
  5.0 0.1 copy.56
  5.1 0.6 pad.4.norm_ref
  5.7 0.0 copy-start
  5.7 61.6 %front.1 = (bf16[2,2,2,128,768]{4,3,2,1,0:T(8,128)(2,1)}, bf16[2,2,2,128,3712]{4,3,2,1,0:T(8,128)(2,1)}, bf16[128,4096]{1,0:T(8,128)(2,1)}) custom-call(f32[2,3,128,256]{3,2,1,0:T(8,128)} %refs_6_.3, bf16[2,128,256]{2,1,0:T(8,128)(2,1)} %bitcast.58, bf16[128,128]{1,0:T(8,128)(2,1)} %pad.4.norm_ref, f32[128,1024]{1,0:T(8,128)} %refs_8_.3, ...), custom_call_target="tpu_custom_call" | custom-call | flops 40000000000 | bytes 1048576 | tf_op jit(solution)/shard_map/front/pallas_call | solution.py:553
  67.3 0.0 copy-done
  67.3 3.2 fusion.1
  70.5 1.2 fusion.6
  72.4 8.4 %attend_forward.2 = (bf16[1024,256]{1,0:T(8,128)(2,1)}, f32[8,1024]{1,0:T(8,128)}) custom-call(s32[1]{0:T(128)S(6)} %copy.73.prefix_ref, bf16[1024,256]{1,0:T(8,128)(2,1)} %get-tuple-element.171.q_ref, bf16[1024,256]{1,0:T(8,128)(2,1)} %get-tuple-element.170.k_ref, bf16[1024,256]{1,0:T(8,128)(2,1)} %get-tuple-element.169.v_ref), custom_call_target="tpu_custom_call" | custom-call | flops 4294967296 | bytes 1048576 | tf_op jit(solution)/shard_map/attend_forward/pallas_call | solution.py:277
  80.7 1.0 convert_bitcast_fusion
  81.7 0.2 fusion.7
  81.9 0.8 copy.59.gain_ref
  82.7 0.8 copy.60.bias_ref
  83.5 0.0 copy-start.1
  83.5 58.3 %self_to_cross.1 = (f32[256,1024]{1,0:T(8,128)}, f32[256,1024]{1,0:T(8,128)}, f32[256,128]{1,0:T(8,128)}, bf16[4,256,256]{2,1,0:T(8,128)(2,1)}, bf16[1024,256]{1...) custom-call(bf16[1024,256]{1,0:T(8,128)(2,1)} %get-tuple-element.75.mixed_ref.o_ref, bf16[1024,3712]{1,0:T(8,128)(2,1)} %bitcast.38, ...), custom_call_target="tpu_custom_call" | custom-call | flops 1000000000 | bytes 2097152 | tf_op jit(solution)/shard_map/self_to_cross/pallas_call | solution.py:632
  141.8 0.0 copy-done.1
  141.8 3.6 fusion
  145.4 1.5 fusion.5
  146.8 15.4 %attend_forward.3 = (bf16[1024,256]{1,0:T(8,128)(2,1)}, f32[8,1024]{1,0:T(8,128)}) custom-call(s32[1]{0:T(128)S(6)} %copy.73.prefix_ref, bf16[1024,256]{1,0:T(8,128)(2,1)} %get-tuple-element.78.q_ref, bf16[2048,256]{1,0:T(8,128)(2,1)} %get-tuple-element.168.k_ref, bf16[2048,256]{1,0:T(8,128)(2,1)} %get-tuple-element.167.v_ref), custom_call_target="tpu_custom_call" | custom-call | flops 8589934592 | bytes 2097152 | tf_op jit(solution)/shard_map/attend_forward/pallas_call | solution.py:277
  162.2 85.2 %feed.1 = (bf16[256,1024]{1,0:T(8,128)(2,1)}, f32[256,1024]{1,0:T(8,128)}, bf16[1024,256]{1,0:T(8,128)(2,1)}, bf16[1024,2048]{1,0:T(8,128)(2,1)}, bf16[1024,2048...) custom-call(bf16[1024,256]{1,0:T(8,128)(2,1)} %get-tuple-element.79.mixed_ref.o_ref, ...), custom_call_target="tpu_custom_call" | custom-call | flops 80000000000 | bytes 2097152 | tf_op jit(solution)/shard_map/feed/pallas_call | solution.py:808
  247.4 39.5 %attend_backward.2 = (bf16[1024,256]{1,0:T(8,128)(2,1)}, bf16[2048,256]{1,0:T(8,128)(2,1)}, bf16[2048,256]{1,0:T(8,128)(2,1)}, bf16[4,256,1024]{2,1,0:T(8,128)(2,1)}, bf16[1024,512]{1,0:T(8,128)(2,1)}) custom-call(s32[1]{0:T(128)S(6)} %copy.73.prefix_ref, bf16[1024,256]{1,0:T(8,128)(2,1)} %get-tuple-element.78.q_ref, ...), custom_call_target="tpu_custom_call" | custom-call | flops 2147483648 | bytes 2097152 | tf_op jit(solution)/shard_map/attend_backward/pallas_call | solution.py:399
  286.9 26.7 %cross_to_self.1 = (f32[256,1024]{1,0:T(8,128)}, bf16[1024,256]{1,0:T(8,128)(2,1)}, bf16[1024,2048]{1,0:T(8,128)(2,1)}, bf16[1024,128]{1,0:T(8,128)(2,1)}) custom-call(bf16[1024,256]{1,0:T(8,128)(2,1)} %get-tuple-element.86.dq_ref, bf16[1024,3712]{1,0:T(8,128)(2,1)} %bitcast.41, f32[256,1024]{1,0:T(8,128)} %get-tuple-element.87.second_ref, ...), custom_call_target="tpu_custom_call" | custom-call | flops 1000000000 | bytes 2097152 | tf_op jit(solution)/shard_map/cross_to_self/pallas_call | solution.py:906
  313.6 0.0 copy-start.3
  313.6 0.0 copy-start.4
  313.6 0.0 copy-start.5
  313.6 13.4 %attend_backward.3 = (bf16[1024,256]{1,0:T(8,128)(2,1)}, bf16[1024,256]{1,0:T(8,128)(2,1)}, bf16[1024,256]{1,0:T(8,128)(2,1)}) custom-call(s32[1]{0:T(128)S(6)} %copy.73.prefix_ref, bf16[1024,256]{1,0:T(8,128)(2,1)} %get-tuple-element.171.q_ref, bf16[1024,256]{1,0:T(8,128)(2,1)} %get-tuple-element.170.k_ref, bf16[1024,256]{1,0:T(8,128)(2,1)} %get-tuple-element.169.v_ref, ...), custom_call_target="tpu_custom_call" | custom-call | flops 1073741824 | bytes 1048576 | tf_op jit(solution)/shard_map/attend_backward/pallas_call | solution.py:399
  327.0 2.3 slice.50.source_ref
  329.3 0.0 copy-done.3
  329.3 0.6 reshape.124.refs_4_.refs_10_
  329.9 0.0 copy-done.4
  329.9 0.6 reshape.125.refs_9_.refs_15_
  330.5 0.0 copy-done.5
  330.5 0.6 reshape.126.refs_14_.refs_20_
  331.1 227.4 %finish.1 = (bf16[2,12,128,1024]{3,2,1,0:T(8,128)(2,1)}, f32[8,128]{1,0:T(8,128)}, f32[2,3,128,256]{3,2,1,0:T(8,128)}, f32[2,256,128]{2,1,0:T(8,128)}, f32[128,1...) custom-call(bf16[1024,256]{1,0:T(8,128)(2,1)} %get-tuple-element.94.dq_ref, ...), custom_call_target="tpu_custom_call" | custom-call | flops 1000000000 | bytes 1048576 | tf_op jit(solution)/shard_map/finish/pallas_call | solution.py:1464
  558.5 7.3 %update.1 = (f32[3,16]{1,0:T(4,128)}, f32[2,3,128,256]{3,2,1,0:T(8,128)}, f32[2,256,128]{2,1,0:T(8,128)}, f32[128,1024]{1,0:T(8,128)}, f32[1024,128]{1,0:T(8,128...) custom-call(f32[8,128]{1,0:T(8,128)} %get-tuple-element.107.refs_0_,, ...), custom_call_target="tpu_custom_call" | custom-call | tf_op jit(solution)/shard_map/update/pallas_call | solution.py:1271
  565.8 0.7 reshape.131
  566.5 0.6 copy.68
  567.1 0.7 reshape.132
  567.8 0.6 copy.69
  568.3 0.7 reshape.133
  569.0 0.6 copy.70
  569.6 2.6 slice.43
  572.2 4.4 convert.6
  576.7 1.8 slice.42
  578.4 0.0 copy-start.2
  578.4 2.5 convert.5
  580.9 0.0 copy-done.2
  580.9 2.5 bitcast_convert_fusion
  (5 shorter events, 0.0 us)
Async XLA Ops:
  5.7 61.6 %copy-start = (bf16[1,1024,1024]{2,1,0:T(8,128)(2,1)S(1)}, bf16[1,1024,1024]{2,1,0:T(8,128)(2,1)}, u32[]{:S(2)}) copy-start(bf16[1,1024,1024]{2,1,0:T(8,128)(2,1)} %param.19) | copy-start | bytes 6291460
  83.5 58.3 %copy-start.1 = (bf16[1,2048,1024]{2,1,0:T(8,128)(2,1)S(1)}, bf16[1,2048,1024]{2,1,0:T(8,128)(2,1)}, u32[]{:S(2)}) copy-start(bf16[1,2048,1024]{2,1,0:T(8,128)(2,1)} %param.20) | copy-start | bytes 12582916
  313.6 15.7 %copy-start.3 = (f32[2,3,128]{2,0,1:T(2,128)S(1)}, f32[2,3,128]{2,0,1:T(2,128)}, u32[]{:S(2)}) copy-start(f32[2,3,128]{2,0,1:T(2,128)} %param.35) | copy-start | bytes 9220
  313.6 16.3 %copy-start.4 = (f32[2,3,128]{2,0,1:T(2,128)S(1)}, f32[2,3,128]{2,0,1:T(2,128)}, u32[]{:S(2)}) copy-start(f32[2,3,128]{2,0,1:T(2,128)} %param.36) | copy-start | bytes 9220
  313.6 16.9 %copy-start.5 = (f32[2,3,128]{2,0,1:T(2,128)S(1)}, f32[2,3,128]{2,0,1:T(2,128)}, u32[]{:S(2)}) copy-start(f32[2,3,128]{2,0,1:T(2,128)} %param.37) | copy-start | bytes 9220
  578.4 2.5 copy-start.2

commit v3 on v2

v3 whole, which is shorter than its diff:
```python
from functools import partial

import jax
import jax.numpy as jnp
from jax import lax
from jax.experimental import pallas as pl
from jax.experimental.pallas import tpu as pltpu
from jax.sharding import PartitionSpec as P

D = 1024
HEAD = 64
FF = 4096
STEP = 5

first_decay = 0.5
second_decay = 0.6
learn_rate = 0.5
weight_decay = 0.01
epsilon = 1e-06
norm_eps = 1e-05
mask_fill = -1000000000.0

MESH = pl.DeviceIdType.MESH
ANYWHERE = pl.BlockSpec(memory_space=pl.ANY)
IN_VMEM = pl.BlockSpec(memory_space=pltpu.VMEM)
NN = (((1,), (0,)), ((), ()))
NT = (((1,), (1,)), ((), ()))
TN = (((0,), (0,)), ((), ()))
VMEM_LIMIT = 52 << 20


def dot(left, right, dims=NN):
    return lax.dot_general(left, right, dims, preferred_element_type=jnp.float32)


def bf16(values):
    return values.astype(jnp.bfloat16)


def f32(values):
    return values.astype(jnp.float32)


def layer_norm(values, gain_row, bias_row):
    center = values - jnp.mean(values, axis=-1, keepdims=True)
    spread = jnp.mean(center * center, axis=-1, keepdims=True)
    inverse = lax.rsqrt(spread + norm_eps)
    normed = center * inverse
    return (normed * gain_row + bias_row, normed, inverse)


def norm_back(upstream, normed, inverse, gain_row):
    scaled = upstream * gain_row
    inner = (
        scaled
        - jnp.mean(scaled, axis=-1, keepdims=True)
        - normed * jnp.mean(scaled * normed, axis=-1, keepdims=True)
    )
    return (
        inner * inverse,
        jnp.sum(upstream * normed, axis=0, keepdims=True),
        jnp.sum(upstream, axis=0, keepdims=True),
    )


class Place:
    def __init__(self, n_mp, side):
        self.n, self.side = n_mp, side
        self.z = lax.axis_index("mp")
        dp = lax.axis_index("dp")
        self.core = lax.rem(dp, 2)
        self.x = lax.rem(dp // 2, side)
        self.y = dp // (2 * side)

    def at(self, y, x, core):
        return {"dp": (y * self.side + x) * 2 + core}

    def x_peer(self, distance):
        other = lax.rem(self.x + distance, self.side)
        return other, self.at(self.y, other, self.core)

    def y_peer(self, distance):
        other = lax.rem(self.y + distance, self.side)
        return other, self.at(other, self.x, self.core)

    def sibling(self):
        return self.at(self.y, self.x, 1 - self.core)

    def line(self):
        return [{"mp": lax.rem(self.z + distance, self.n)} for distance in range(1, self.n)]

    def plane(self):
        steps = range(1, self.side)
        return (
            [self.x_peer(step)[1] for step in steps]
            + [self.y_peer(step)[1] for step in steps]
            + [self.sibling()]
        )


def greet(others):
    barrier = pltpu.get_barrier_semaphore()
    for other in others:
        pl.semaphore_signal(barrier, inc=1, device_id=other, device_id_type=MESH)
    pl.semaphore_wait(barrier, len(others))


def push(source, target, send_sem, recv_sem, to):
    copy = pltpu.make_async_remote_copy(
        source, target, send_sem, recv_sem, device_id=to, device_id_type=MESH
    )
    copy.start()
    return copy


def rows_at(index, size):
    return pl.ds(pl.multiple_of(index * size, size), size)


def heads_to_tokens(n, source, slots, send_sems, recv_sems):
    me = lax.axis_index("mp")
    size = source.shape[0] // n
    copies = []
    for distance in range(1, n):
        to = lax.rem(me + distance, n)
        copies.append(
            push(
                source.at[rows_at(to, size)], slots.at[me],
                send_sems.at[distance - 1], recv_sems.at[distance - 1], {"mp": to},
            )
        )
    return copies


def tokens_to_heads(n, make, blocks, target, send_sems, recv_sems, local_sem):
    me = lax.axis_index("mp")
    size = blocks.shape[1]
    copies = []
    for distance in (*range(1, n), 0):
        to = lax.rem(me + distance, n)
        blocks[to] = bf16(make(to))
        place = target.at[rows_at(me, size)]
        if distance:
            copies.append(
                push(
                    blocks.at[to], place,
                    send_sems.at[distance - 1], recv_sems.at[distance - 1], {"mp": to},
                )
            )
        else:
            copy = pltpu.make_async_copy(blocks.at[to], place, local_sem)
            copy.start()
            copies.append(copy)
    return copies


def merge_heads(n, slots, copies, part_of, start):
    me = lax.axis_index("mp")
    total = start + part_of(slots[me], me)
    for distance in range(1, n):
        origin = lax.rem(me + n - distance, n)
        copies[distance - 1].wait_recv()
        total = total + part_of(slots[origin], origin)
    for copy in copies:
        copy.wait_send()
    return total


def load_groups(n, bundle, stride, first, width, target, sems):
    return [
        pltpu.make_async_copy(
            bundle.at[:, pl.ds(group * stride + first, width)], target.at[group], sems.at[group]
        )
        for group in range(n)
    ]


class Give:
    def __init__(self, place, out, sems):
        self.place, self.n, self.me, self.out = place, place.n, place.z, out
        self.sems = {"right": sems[0:2], "left": sems[2:4]}

    @staticmethod
    def sems(n):
        return [pltpu.SemaphoreType.DMA((max(n - 1, 1),))] * 4

    def _copy(self, way, step):
        ahead = 1 if way == "right" else -1
        chunk = lax.rem(self.me - ahead * step + self.n, self.n)
        return pltpu.make_async_remote_copy(
            self.out.at[chunk], self.out.at[chunk],
            self.sems[way][0].at[step], self.sems[way][1].at[step],
            device_id={"mp": lax.rem(self.me + ahead + self.n, self.n)}, device_id_type=MESH,
        )

    def _spots(self):
        return (("right", self.me), ("left", self.n - 1 - self.me))

    def step(self, step):
        for way, spot in self._spots():

            @pl.when((spot >= step) & (spot < self.n - 1))
            def _():
                if step > 0:
                    self._copy(way, step - 1).wait_recv()
                self._copy(way, step).start()

    def finish(self):
        for way, spot in self._spots():

            @pl.when(spot == self.n - 1)
            def _():
                for step in range(self.n - 1):
                    self._copy(way, step).wait_recv()

            for step in range(self.n - 1):

                @pl.when((spot >= step) & (spot < self.n - 1))
                def _():
                    self._copy(way, step).wait_send()


class Spread:
    def __init__(self, place, home, send_sems, recv_sems):
        self.place, self.home, self.send, self.recv = place, home, send_sems, recv_sems
        self.half = home.shape[3] // 2
        self.copies = {"first": [], "second": [], "core": []}
        self.index = 0

    def _push(self, stage, block, to):
        spot = self.index
        self.index += 1
        self.copies[stage].append(push(block, block, self.send.at[spot], self.recv.at[spot], to))

    def first(self):
        p, half = self.place, self.half
        for step in range(1, p.side):
            own = self.home.at[p.y, p.x, p.core]
            self._push("first", own.at[pl.ds(0, half)], p.x_peer(step)[1])
            self._push("first", own.at[pl.ds(half, half)], p.y_peer(step)[1])

    def second(self):
        p, half = self.place, self.half
        for copy in self.copies["first"]:
            copy.wait_recv()
        for step in range(1, p.side):
            self._push(
                "second", self.home.at[p.y, :, p.core, pl.ds(0, half)], p.y_peer(step)[1]
            )
            self._push(
                "second", self.home.at[:, p.x, p.core, pl.ds(half, half)], p.x_peer(step)[1]
            )

    def core(self):
        for copy in self.copies["second"]:
            copy.wait_recv()
        self._push("core", self.home.at[:, :, self.place.core], self.place.sibling())

    def finish(self):
        for copy in self.copies["core"] or self.copies["second"] or self.copies["first"]:
            copy.wait_recv()
        for stage in self.copies.values():
            for copy in stage:
                copy.wait_send()

    @staticmethod
    def sems(side):
        return pltpu.SemaphoreType.DMA((4 * (side - 1) + 1,))


class Reduce:
    def __init__(self, place, sources, scratch):
        self.place, self.sources = place, sources
        self.keep, self.first_a, self.first_b, *rest = scratch
        *rest, self.local, self.send, self.recv = rest
        if rest:
            self.second_a, self.second_b = rest
        self.half = self.keep.shape[2] // 2
        self.copies = {"core": [], "first": [], "second": []}
        self.index = 0

    @staticmethod
    def scratch(side, rows, columns, sources, second=True):
        low, dma = jnp.bfloat16, pltpu.SemaphoreType.DMA
        block = pltpu.VMEM((side, side, rows, columns), low)
        first = pltpu.VMEM((side - 1, side, rows // 2, columns), low)
        rest = pltpu.VMEM((side - 1, rows // 2, columns), low)
        count = sources + 4 * (side - 1)
        seconds = [rest, rest] if second else []
        return [
            block, first, first, *seconds, dma((2, sources)), dma((count,)), dma((count,)),
        ]

    def _push(self, stage, source, target, to, begin=True):
        copy = pltpu.make_async_remote_copy(
            source, target, self.send.at[self.index], self.recv.at[self.index],
            device_id=to, device_id_type=MESH,
        )
        self.index += 1
        self.copies[stage].append(copy)
        if begin:
            copy.start()

    def core_start(self, begin=True):
        p, column = self.place, 0
        self.index, self.copies["core"] = 0, []
        for source in self.sources:
            cols = pl.ds(column, source.shape[4])
            column += source.shape[4]
            self._push(
                "core", source.at[:, :, 1 - p.core], self.keep.at[:, :, :, cols], p.sibling(), begin
            )

    def _load(self, stage, index):
        y, x = index // self.place.side, index % self.place.side
        column, loads = 0, []
        for spot, source in enumerate(self.sources):
            cols = pl.ds(column, source.shape[4])
            column += source.shape[4]
            loads.append(
                pltpu.make_async_copy(
                    source.at[y, x, self.place.core], stage.at[index % 2, :, cols],
                    self.local.at[index % 2, spot],
                )
            )
        return loads

    def core_finish(self, stage):
        side, keep, columns = self.place.side, self.keep, self.keep.shape[3]
        for load in self._load(stage, 0):
            load.start()
        for copy in self.copies["core"]:
            copy.wait_recv()
        for index in range(side * side):
            if index + 1 < side * side:
                for load in self._load(stage, index + 1):
                    load.start()
            for load in self._load(stage, index):
                load.wait()
            y, x = index // side, index % side
            keep[y, x] = bf16(f32(keep[y, x]) + f32(stage[index % 2, :, :columns]))

    def first_start(self, begin=True):
        p, half = self.place, self.half
        self.index, self.copies["first"] = len(self.sources), []
        top, bottom = pl.ds(0, half), pl.ds(half, half)
        for step in range(1, p.side):
            other, to = p.x_peer(step)
            self._push("first", self.keep.at[:, other, top], self.first_a.at[step - 1], to, begin)
            other, to = p.y_peer(step)
            self._push("first", self.keep.at[other, :, bottom], self.first_b.at[step - 1], to, begin)

    def first_finish(self):
        p, half, keep = self.place, self.half, self.keep
        for copy in self.copies["first"]:
            copy.wait_recv()

        def add(index, carry):
            total = f32(keep[index, p.x, :half, :])
            for step in range(p.side - 1):
                total = total + f32(self.first_a[step, index])
            keep[index, p.x, :half, :] = bf16(total)
            total = f32(keep[p.y, index, half:, :])
            for step in range(p.side - 1):
                total = total + f32(self.first_b[step, index])
            keep[p.y, index, half:, :] = bf16(total)
            return carry

        lax.fori_loop(0, p.side, add, 0)

    def halves(self, out_a, out_b):
        p, half, keep = self.place, self.half, self.keep
        for index in range(p.side):
            out_a[index] = keep[index, p.x, :half, :]
            out_b[index] = keep[p.y, index, half:, :]

    def second_start(self):
        p, half = self.place, self.half
        top, bottom = pl.ds(0, half), pl.ds(half, half)
        for step in range(1, p.side):
            other, to = p.y_peer(step)
            self._push("second", self.keep.at[other, p.x, top], self.second_a.at[step - 1], to)
            other, to = p.x_peer(step)
            self._push("second", self.keep.at[p.y, other, bottom], self.second_b.at[step - 1], to)

    def second_wait(self):
        for copy in self.copies["second"]:
            copy.wait_recv()

    def total(self, cols):
        p, half = self.place, self.half
        top, bottom = f32(self.keep[p.y, p.x, :half, cols]), f32(self.keep[p.y, p.x, half:, cols])
        for step in range(p.side - 1):
            top = top + f32(self.second_a[step, :, cols])
            bottom = bottom + f32(self.second_b[step, :, cols])
        return jnp.concatenate([top, bottom], axis=0)

    def finish(self):
        for stage in self.copies.values():
            for copy in stage:
                copy.wait_send()


class Halves:
    def __init__(self, place, part_a, part_b, scratch):
        self.place, self.parts = place, (part_a, part_b)
        self.landed, (self.send, self.recv) = scratch[:2], scratch[2:]

    @staticmethod
    def scratch(side, half, columns):
        dma = pltpu.SemaphoreType.DMA((2 * (side - 1),))
        return [pltpu.VMEM((side - 1, half, columns), jnp.bfloat16)] * 2 + [dma, dma]

    def start(self):
        p = self.place
        self.copies = []
        for step in range(1, p.side):
            for index, (other, to) in enumerate((p.y_peer(step), p.x_peer(step))):
                spot = 2 * (step - 1) + index
                self.copies.append(
                    push(
                        self.parts[index].at[other], self.landed[index].at[step - 1],
                        self.send.at[spot], self.recv.at[spot], to,
                    )
                )

    def total(self):
        for copy in self.copies:
            copy.wait()
        sums = []
        for index, mine in enumerate((self.place.y, self.place.x)):
            total = f32(self.parts[index][mine])
            for step in range(self.place.side - 1):
                total = total + f32(self.landed[index][step])
            sums.append(total)
        return jnp.concatenate(sums, axis=0)


def forward_rows(masked, start, block, prefix_ref, q_ref, k_ref, v_ref, mixed_ref, sums_ref):
    width = q_ref.shape[1]
    keys = k_ref.shape[0]
    if masked:
        keys = max(keys // 2, start + block)
    lane = lax.broadcasted_iota(jnp.int32, (block, width), 1) // HEAD
    span = slice(start, start + block)
    query = q_ref[span, :] * jnp.bfloat16(HEAD**-0.5)
    key_rows, value_rows = k_ref[:keys, :], v_ref[:keys, :]
    if masked:
        query_ids = start + lax.broadcasted_iota(jnp.int32, (block, keys), 0)
        key_ids = lax.broadcasted_iota(jnp.int32, (block, keys), 1)
        allowed = (key_ids <= query_ids) | (key_ids < prefix_ref[0])
    mixed = jnp.zeros((block, width), jnp.float32)
    slot = lax.broadcasted_iota(jnp.int32, (block, 128), 1)
    table = jnp.zeros((block, 128), jnp.float32)
    for head in range(width // HEAD):
        scores = dot(jnp.where(lane == head, query, jnp.bfloat16(0)), key_rows, NT)
        if masked:
            scores = jnp.where(allowed, scores, mask_fill)
        row_max = jnp.max(scores, axis=1, keepdims=True)
        powered = jnp.exp(scores - row_max)
        totals = jnp.sum(powered, axis=1, keepdims=True)
        part = dot(bf16(powered), value_rows) * (1.0 / totals)
        mixed = jnp.where(lane == head, part, mixed)
        table = jnp.where(slot == head, row_max + jnp.log(totals), table)
    mixed_ref[span, :] = bf16(mixed)
    sums_ref[:, span] = table.T[:8, :]


def backward_delta(do_ref, o_ref, delta):
    width = do_ref.shape[1]
    product = f32(do_ref[...]) * f32(o_ref[...])
    row = lax.broadcasted_iota(jnp.int32, (8, width), 0)
    col = lax.broadcasted_iota(jnp.int32, (8, width), 1) // HEAD
    pick = jnp.where(row == col, 1.0, 0.0).astype(jnp.float32)
    delta[...] = lax.dot_general(
        pick, product, NT, precision=lax.Precision.HIGHEST, preferred_element_type=jnp.float32
    )


def backward_block(
    masked, block, index, heads, prefix_ref, q_ref, k_ref, v_ref, do_ref, sums_ref, delta, acc, dk_ref, dv_ref
):
    total, width = q_ref.shape
    factor = HEAD**-0.5
    rows = slice(index * block, (index + 1) * block)
    first = index * block if masked and index * block >= total // 2 else 0
    count = total - first
    lane = lax.broadcasted_iota(jnp.int32, (block, width), 1) // HEAD
    query, grad_rows = q_ref[first:, :], do_ref[first:, :]
    scaled_keys = k_ref[rows, :] * jnp.bfloat16(factor)
    value_rows = v_ref[rows, :]
    if masked:
        query_ids = first + lax.broadcasted_iota(jnp.int32, (block, count), 1)
        key_ids = index * block + lax.broadcasted_iota(jnp.int32, (block, count), 0)
        allowed = (key_ids <= query_ids) | (key_ids < prefix_ref[0])
    key_grad = jnp.zeros((block, width), jnp.float32)
    value_grad = jnp.zeros((block, width), jnp.float32)
    query_grad = jnp.zeros((count, width), jnp.float32)
    for head in heads:
        own_keys = jnp.where(lane == head, scaled_keys, jnp.bfloat16(0))
        scores = dot(own_keys, query, NT)
        if masked:
            scores = jnp.where(allowed, scores, mask_fill)
        probs = jnp.exp(scores - sums_ref[head : head + 1, first:])
        prob_grad = dot(jnp.where(lane == head, value_rows, jnp.bfloat16(0)), grad_rows, NT)
        score_grad = bf16(probs * (prob_grad - delta[head : head + 1, first:]))
        value_grad = jnp.where(lane == head, dot(bf16(probs), grad_rows), value_grad)
        key_grad = jnp.where(lane == head, dot(score_grad, query), key_grad)
        query_grad = query_grad + dot(score_grad, own_keys, TN)
    acc[first:, :] += query_grad
    mine = (lane >= heads[0]) & (lane <= heads[-1])
    key_grad, value_grad = bf16(key_grad * factor), bf16(value_grad)
    if heads[0] > 0:
        key_grad = jnp.where(mine, key_grad, dk_ref[rows, :])
        value_grad = jnp.where(mine, value_grad, dv_ref[rows, :])
    dk_ref[rows, :] = key_grad
    dv_ref[rows, :] = value_grad


def cross_backward_kernel(
    n, side, prefix_ref, q_ref, k_ref, v_ref, do_ref, o_ref, sums_ref, mine_ref, states_ref,
    shrink_ref, expand_ref, dq_ref, dk_ref, dv_ref, all_ref, source_ref, half_a_ref, half_b_ref,
    acc, delta, source, stage, own_sem, *scratch,
):
    p = Place(n, side)
    give = Give(p, all_ref, scratch[:4])
    feed_sum = Reduce(p, [shrink_ref, expand_ref], scratch[4:])
    width = q_ref.shape[1]
    step = pl.program_id(0)
    steps = pl.num_programs(0)

    @pl.when(step == 0)
    def _():
        own = pltpu.make_async_copy(mine_ref, all_ref.at[give.me], own_sem)
        own.start()
        greet(p.line() + p.plane())
        feed_sum.core_start()
        own.wait()
        give.step(0)
        backward_delta(do_ref, o_ref, delta)
        acc[...] = jnp.zeros_like(acc)
        source[...] = jnp.zeros_like(source)

    for later in range(1, n - 1):

        @pl.when(step == (later + 1) * steps // n)
        def _():
            give.step(later)

    @pl.when(step == 1)
    def _():
        feed_sum.core_start(False)
        feed_sum.core_finish(stage)
        feed_sum.first_start()

    backward_block(
        False, k_ref.shape[0], 0, tuple(range(width // HEAD)),
        prefix_ref, q_ref, k_ref, v_ref, do_ref, sums_ref, delta, acc, dk_ref, dv_ref,
    )
    source[:, :width] += dot(states_ref[...], dk_ref[...], TN)
    source[:, width:] += dot(states_ref[...], dv_ref[...], TN)

    @pl.when(step == steps - 1)
    def _():
        dq_ref[...] = bf16(acc[...])
        source_ref[...] = bf16(source[...])
        feed_sum.core_start(False)
        feed_sum.first_start(False)
        feed_sum.first_finish()
        feed_sum.halves(half_a_ref, half_b_ref)
        feed_sum.finish()
        give.finish()


def cross_backward(
    n_dp, n, query, key_rows, value_rows, grad_out, mixed, sums, prefix, mine, states, shrink, expand, block=512
):
    total, width = query.shape
    keys, model = states.shape
    side = round((n_dp // 2) ** 0.5)
    rows, columns = model // n_dp, shrink.shape[1] + expand.shape[1]
    half = (side, rows // 2, columns)
    by_place = lambda values: values.reshape(side, side, 2, rows, values.shape[1])
    low, wide = jnp.bfloat16, jnp.float32
    shape = jax.ShapeDtypeStruct
    whole = pl.BlockSpec((total, width), lambda i, p: (0, 0))
    part = pl.BlockSpec((block, width), lambda i, p: (i, 0))
    return pl.pallas_call(
        partial(cross_backward_kernel, n, side),
        grid_spec=pltpu.PrefetchScalarGridSpec(
            num_scalar_prefetch=1,
            grid=(keys // block,),
            in_specs=[
                whole, part, part, whole, whole,
                pl.BlockSpec((8, total), lambda i, p: (0, 0)),
                pl.BlockSpec(mine.shape, lambda i, p: (0, 0)),
                pl.BlockSpec((block, model), lambda i, p: (i, 0)),
                ANYWHERE, ANYWHERE,
            ],
            out_specs=[
                whole, part, part, ANYWHERE, pl.BlockSpec((model, 2 * width), lambda i, p: (0, 0)),
                pl.BlockSpec(half, lambda i, p: (0, 0, 0)), pl.BlockSpec(half, lambda i, p: (0, 0, 0)),
            ],
            scratch_shapes=[
                pltpu.VMEM((total, width), wide),
                pltpu.VMEM((8, total), wide),
                pltpu.VMEM((model, 2 * width), wide),
                pltpu.VMEM((2, rows, columns), low),
                pltpu.SemaphoreType.DMA,
                *Give.sems(n),
                *Reduce.scratch(side, rows, columns, 2, second=False),
            ],
        ),
        out_shape=[
            shape((total, width), low),
            shape((keys, width), low),
            shape((keys, width), low),
            shape((n,) + mine.shape, low),
            shape((model, 2 * width), low),
            shape(half, low),
            shape(half, low),
        ],
        compiler_params=pltpu.CompilerParams(
            vmem_limit_bytes=VMEM_LIMIT, collective_id=6, has_side_effects=True
        ),
        cost_estimate=pl.CostEstimate(
            flops=40 * total * keys * width, bytes_accessed=4 * keys * width, transcendentals=0
        ),
        name="cross_backward",
    )(
        prefix, query, key_rows, value_rows, grad_out, mixed, sums, mine, states,
        by_place(shrink), by_place(expand),
    )


def front_kernel(
    n, side, prefix_ref, inner_ref, outer_ref, norm_ref, expand_ref, shrink_ref, x_ref,
    near_ref, home_ref, later_ref, feed_ref, q_ref, k_ref, v_ref, mixed_ref, sums_ref,
    block_near, block_line, block_norm, own_sems, near_send, near_recv, home_send, home_recv,
    line_send, line_recv, far_send, far_recv,
):
    p = Place(n, side)
    width = inner_ref.shape[3]
    units = expand_ref.shape[1]
    for index in range(3):
        block_near[:, index * width : (index + 1) * width] = bf16(inner_ref[0, index])
    block_line[:, :width] = bf16(inner_ref[1, 0])
    block_line[:, width : 2 * width] = outer_ref[0]
    block_norm[...] = norm_ref[...]
    line_cols = pl.ds(pl.multiple_of(2 * width * p.z, 2 * width), 2 * width)
    later_cols = pl.ds(pl.multiple_of(width * p.z, width), width)
    spot = home_ref.at[p.y, p.x, p.core]
    near_ref[p.y, p.x, p.core] = block_near[...]
    own = [
        pltpu.make_async_copy(block_line, spot.at[:, line_cols], own_sems.at[0]),
        pltpu.make_async_copy(
            block_norm, spot.at[:, pl.ds(2 * n * width, block_norm.shape[1])], own_sems.at[1]
        ),
    ]
    for copy in own:
        copy.start()
    later_ref[:, later_cols] = outer_ref[1]
    for index in range(2):
        start = (n + index) * width
        later_ref[:, start : start + width] = bf16(inner_ref[1, index + 1])
    feed_ref[:, :units] = bf16(expand_ref[...])
    feed_ref[:, 2 * units : 3 * units] = shrink_ref[...]
    greet(p.line() + p.plane())
    near = Spread(p, near_ref, near_send, near_recv)
    rest = Spread(p, home_ref, home_send, home_recv)
    near.first()
    line = [
        push(block_line, spot.at[:, line_cols], line_send.at[index], line_recv.at[index], other)
        for index, other in enumerate(p.line())
    ]
    later = [
        push(
            later_ref.at[:, later_cols], later_ref.at[:, later_cols],
            line_send.at[n - 1 + index], line_recv.at[n - 1 + index], other,
        )
        for index, other in enumerate(p.line())
    ]
    far = {"mp": lax.rem(p.z + n // 2, n)}
    later += [
        push(
            feed_ref.at[:, pl.ds(2 * index * units, units)],
            feed_ref.at[:, pl.ds((2 * index + 1) * units, units)],
            far_send.at[index], far_recv.at[index], far,
        )
        for index in range(2)
    ]
    near.second()
    near.core()
    for copy in own:
        copy.wait()
    for copy in line:
        copy.wait_recv()
    rest.first()
    near.finish()
    model = x_ref.shape[1]
    weights = near_ref[...].reshape(model, 3 * width)
    for start in range(0, x_ref.shape[0], 256):
        rows = slice(start, start + 256)
        made = bf16(dot(x_ref[rows, :], weights))
        for index, target in enumerate((q_ref, k_ref, v_ref)):
            target[rows, :] = made[:, index * width : (index + 1) * width]
    rest.second()
    block = x_ref.shape[0] // 4
    for index in range(4):
        forward_rows(
            True, index * block, block, prefix_ref, q_ref, k_ref, v_ref, mixed_ref, sums_ref
        )
        if index == 2:
            rest.core()
    rest.finish()
    for copy in line:
        copy.wait_send()
    for copy in later:
        copy.wait()


def front(n_dp, n_mp, prefix, inner, outer_t, norm_t, expand, shrink_t, tokens):
    rows, width = inner.shape[2:]
    total = tokens.shape[0]
    side = round((n_dp // 2) ** 0.5)
    line = 2 * width
    columns = n_mp * line + norm_t.shape[1]
    low = jnp.bfloat16
    dma = pltpu.SemaphoreType.DMA
    shape = jax.ShapeDtypeStruct
    return pl.pallas_call(
        partial(front_kernel, n_mp, side),
        out_shape=[
            shape((side, side, 2, rows, 3 * width), low),
            shape((side, side, 2, rows, columns), low),
            shape((rows, (n_mp + 2) * width), low),
            shape((rows, 4 * expand.shape[1]), low),
            *[shape((total, width), low)] * 4,
            shape((8, total), jnp.float32),
        ],
        in_specs=[pl.BlockSpec(memory_space=pltpu.SMEM)] + [IN_VMEM] * 6,
        out_specs=[IN_VMEM, ANYWHERE] + [IN_VMEM] * 7,
        scratch_shapes=[
            pltpu.VMEM((rows, 3 * width), low),
            pltpu.VMEM((rows, line), low),
            pltpu.VMEM((rows, norm_t.shape[1]), low),
            dma((2,)),
            Spread.sems(side), Spread.sems(side), Spread.sems(side), Spread.sems(side),
            dma((2 * n_mp - 2,)), dma((2 * n_mp - 2,)), dma((2,)), dma((2,)),
        ],
        compiler_params=pltpu.CompilerParams(
            collective_id=0, has_side_effects=True, vmem_limit_bytes=VMEM_LIMIT
        ),
        cost_estimate=pl.CostEstimate(flops=40 * 10**9, bytes_accessed=1 << 20, transcendentals=0),
        name="front",
    )(prefix, inner, outer_t, norm_t, expand, shrink_t, tokens)


def self_to_cross_kernel(
    n, side, mixed_ref, bundle_ref, x_ref, feed_ref, later_ref,
    hidden_ref, normed_ref, inverse_ref, slots_ref, norm_ref, q_ref, home_ref, rest_ref,
    wo, wq, norm_columns, x_rows, blocks, wo_sems, wq_sems, x_sem, own_sem, send_in, recv_in, send_out, recv_out,
    feed_block, later_block, block_sems, feed_send, feed_recv, later_send, later_recv, norm_sem,
):
    p = Place(n, side)
    me = p.z
    size = x_rows.shape[0]
    width = mixed_ref.shape[1]
    loads = [
        pltpu.make_async_copy(mixed_ref.at[rows_at(me, size)], slots_ref.at[me], own_sem),
        pltpu.make_async_copy(x_ref.at[rows_at(me, size)], x_rows, x_sem),
        pltpu.make_async_copy(
            bundle_ref.at[:, pl.ds(2 * n * width, norm_columns.shape[1])], norm_columns, norm_sem
        ),
        *load_groups(n, bundle_ref, 2 * width, width, width, wo, wo_sems),
        *load_groups(n, bundle_ref, 2 * width, 0, width, wq, wq_sems),
    ]
    sources, blocks_here, homes = (later_ref, feed_ref), (later_block, feed_block), (rest_ref, home_ref)
    block_loads = [
        pltpu.make_async_copy(source, block, block_sems.at[index])
        for index, (source, block) in enumerate(zip(sources, blocks_here))
    ]
    for load in block_loads + loads:
        load.start()
    greet(p.line() + p.plane())
    copies = heads_to_tokens(n, mixed_ref, slots_ref, send_in, recv_in)
    for load in block_loads:
        load.wait()
    stores = [
        pltpu.make_async_copy(block, home.at[p.y, p.x, p.core], block_sems.at[index])
        for index, (block, home) in enumerate(zip(blocks_here, homes))
    ]
    for store in stores:
        store.start()
    rest = Spread(p, rest_ref, later_send, later_recv)
    spread = Spread(p, home_ref, feed_send, feed_recv)
    for store in stores:
        store.wait()
    rest.first()
    spread.first()
    for load in loads:
        load.wait()
    norms = f32(norm_columns[...]).T[:8, :]
    norm_ref[...] = norms
    branch = merge_heads(
        n, slots_ref, copies, lambda part, group: dot(part, wo[group], NT), f32(x_rows[...])
    )
    rest.second()
    hidden, normed, inverse = layer_norm(branch, norms[0:1, :], norms[3:4, :])
    hidden_ref[...] = hidden
    normed_ref[...] = normed
    inverse_ref[...] = jnp.broadcast_to(inverse, inverse_ref.shape)
    low = bf16(hidden)
    sent = tokens_to_heads(
        n, lambda group: dot(low, wq[group]), blocks, q_ref, send_out, recv_out, own_sem
    )
    rest.core()
    for copy in sent:
        copy.wait()
    rest.finish()
    spread.finish()


def self_to_cross(n_dp, n, mixed, bundle, tokens, feed_block, later_block):
    side = round((n_dp // 2) ** 0.5)
    total, width = mixed.shape
    size, model = total // n, tokens.shape[1]
    shape = jax.ShapeDtypeStruct
    dma = pltpu.SemaphoreType.DMA
    return pl.pallas_call(
        partial(self_to_cross_kernel, n, side),
        out_shape=[
            shape((size, model), jnp.float32),
            shape((size, model), jnp.float32),
            shape((size, 128), jnp.float32),
            shape((n, size, width), jnp.bfloat16),
            shape((8, model), jnp.float32),
            shape((total, width), jnp.bfloat16),
            shape((side, side, 2) + feed_block.shape, jnp.bfloat16),
            shape((side, side, 2) + later_block.shape, jnp.bfloat16),
        ],
        in_specs=[ANYWHERE] * 5,
        out_specs=[IN_VMEM] * 5 + [ANYWHERE] * 3,
        scratch_shapes=[
            pltpu.VMEM((n, model, width), jnp.bfloat16),
            pltpu.VMEM((n, model, width), jnp.bfloat16),
            pltpu.VMEM((model, bundle.shape[1] - 2 * n * width), jnp.bfloat16),
            pltpu.VMEM((size, model), jnp.bfloat16),
            pltpu.VMEM((n, size, width), jnp.bfloat16),
            dma((n,)), dma((n,)), dma, dma,
            dma((n - 1,)), dma((n - 1,)), dma((n - 1,)), dma((n - 1,)),
            pltpu.VMEM(feed_block.shape, jnp.bfloat16),
            pltpu.VMEM(later_block.shape, jnp.bfloat16),
            dma((2,)), Spread.sems(side), Spread.sems(side), Spread.sems(side), Spread.sems(side), dma,
        ],
        compiler_params=pltpu.CompilerParams(
            collective_id=1, has_side_effects=True, vmem_limit_bytes=VMEM_LIMIT
        ),
        cost_estimate=pl.CostEstimate(
            flops=10**9, bytes_accessed=8 * total * width, transcendentals=0
        ),
        name="self_to_cross",
    )(mixed, bundle, tokens, feed_block, later_block)


def cross_forward_kernel(
    side, n, q_ref, states_ref, rest_ref, home_in_ref, k_ref, v_ref, mixed_ref, sums_ref, home_ref,
    weights, weight_sem, feed_send, feed_recv,
):
    p = Place(n, side)
    width = q_ref.shape[1]
    load = pltpu.make_async_copy(
        rest_ref.at[:, pl.ds(n * width, 2 * width)], weights, weight_sem
    )
    load.start()
    greet(p.plane())
    spread = Spread(p, home_ref, feed_send, feed_recv)
    spread.second()
    load.wait()
    for start in range(0, states_ref.shape[0], 512):
        rows = slice(start, start + 512)
        made = bf16(dot(states_ref[rows, :], weights[...]))
        k_ref[rows, :] = made[:, :width]
        v_ref[rows, :] = made[:, width:]
    block = q_ref.shape[0] // 2
    for start in range(0, q_ref.shape[0], block):
        forward_rows(False, start, block, None, q_ref, k_ref, v_ref, mixed_ref, sums_ref)
    spread.finish()


def cross_forward(n, query, states, rest, home):
    total, width = query.shape
    keys, model = states.shape
    side = home.shape[0]
    shape = jax.ShapeDtypeStruct
    low = jnp.bfloat16
    return pl.pallas_call(
        partial(cross_forward_kernel, side, n),
        out_shape=[
            shape((keys, width), low),
            shape((keys, width), low),
            shape((total, width), low),
            shape((8, total), jnp.float32),
            shape(home.shape, low),
        ],
        in_specs=[IN_VMEM] * 2 + [ANYWHERE] * 2,
        out_specs=[IN_VMEM] * 4 + [ANYWHERE],
        input_output_aliases={3: 4},
        scratch_shapes=[
            pltpu.VMEM((model, 2 * width), low),
            pltpu.SemaphoreType.DMA,
            Spread.sems(side), Spread.sems(side),
        ],
        compiler_params=pltpu.CompilerParams(
            collective_id=7, has_side_effects=True, vmem_limit_bytes=VMEM_LIMIT
        ),
        cost_estimate=pl.CostEstimate(flops=10**10, bytes_accessed=1 << 20, transcendentals=0),
        name="cross_forward",
    )(query, states, rest, home)


def feed_kernel(
    n, side, mixed_ref, rest_ref, home_ref, hidden_one_ref, cot_ref, norm_ref,
    out_ref, second_ref, dmix_ref, shrink_grad_ref, expand_grad_ref, wo_grad_ref, norm_grad_ref,
    wo, weights, slots, hidden_two, normed_two, low_two, low_three, act, slope,
    y_own, y_send, y_recv, d_send, d_recv, cot, blocks,
    load_sems, wo_sems, own_sem, send_in, recv_in, send_out, recv_out, pair_send, pair_recv,
    home_sems, home_send, home_recv,
):
    p = Place(n, side)
    me = p.z
    mate = {"mp": me + 1 - 2 * lax.rem(me, 2)}
    size = cot.shape[0]
    half = size // 2
    width = mixed_ref.shape[1]
    hidden_units = act.shape[1]
    chunk = min(512, hidden_units)
    loads = [
        pltpu.make_async_copy(mixed_ref.at[rows_at(me, size)], slots.at[me], load_sems.at[0]),
        *load_groups(n, rest_ref, width, 0, width, wo, wo_sems),
        pltpu.make_async_copy(cot_ref.at[rows_at(me, size)], cot, load_sems.at[1]),
    ]
    rows = home_ref.shape[3]
    places = [(y, x) for y in range(side) for x in range(side)]
    spots = [rows_at((y * side + x) * 2 + p.core, rows) for y, x in places]
    homes = [
        pltpu.make_async_copy(home_ref.at[y, x, p.core], weights.at[spot], home_sems.at[index])
        for index, ((y, x), spot) in enumerate(zip(places, spots))
    ]
    for load in loads + homes:
        load.start()
    greet(p.line() + [p.sibling()])
    copies = heads_to_tokens(n, mixed_ref, slots, send_in, recv_in)
    home_copies = [
        push(
            home_ref.at[y, x, p.core], weights.at[spot],
            home_send.at[index], home_recv.at[index], p.sibling(),
        )
        for index, ((y, x), spot) in enumerate(zip(places, spots))
    ]
    for load in loads[: n + 1]:
        load.wait()
    branch = merge_heads(
        n, slots, copies, lambda part, group: dot(part, wo[group], NT), hidden_one_ref[...]
    )
    hidden, normed, inverse_two = layer_norm(branch, norm_ref[1:2, :], norm_ref[4:5, :])
    hidden_two[...] = hidden
    normed_two[...] = normed
    low_two[:size, :] = bf16(hidden)
    own, other = pl.ds(0, size), pl.ds(size, size)
    pair = []

    def to_mate(source, target):
        index = len(pair)
        pair.append(push(source, target, pair_send.at[index], pair_recv.at[index], mate))
        return pair[-1]

    hidden_copy = to_mate(low_two.at[own], low_two.at[other])
    for copy in homes:
        copy.wait()
    for copy in home_copies:
        copy.wait_recv()
    expand = weights.at[:, pl.ds(0, hidden_units)]
    shrink = weights.at[:, pl.ds(hidden_units, hidden_units)]

    def expand_rows(start, count):
        rows = low_two[start : start + count, :]
        for first in range(0, hidden_units, chunk):
            pre = dot(rows, expand[:, first : first + chunk])
            cdf = 0.5 + 0.5 * lax.erf(pre * 0.7071067811865476)
            act[start : start + count, first : first + chunk] = bf16(pre * cdf)
            slope[start : start + count, first : first + chunk] = bf16(
                cdf + pre * jnp.exp(-0.5 * pre * pre) * 0.3989422804014327
            )

    expand_rows(0, size)
    hidden_copy.wait_recv()
    y_copies = []
    for start in (0, half):
        expand_rows(size + start, half)
        y_send[start : start + half, :] = bf16(
            dot(act[size + start : size + start + half, :], shrink[...], NT)
        )
        y_copies.append(to_mate(y_send.at[pl.ds(start, half)], y_recv.at[pl.ds(start, half)]))
    y_own[...] = dot(act[:size, :], shrink[...], NT)
    for copy in y_copies:
        copy.wait_recv()
    output, normed, inverse = layer_norm(
        hidden_two[...] + y_own[...] + f32(y_recv[...]), norm_ref[2:3, :], norm_ref[5:6, :]
    )
    out_ref[...] = bf16(output)
    loads[n + 1].wait()
    third, gain_three, bias_three = norm_back(f32(cot[...]), normed, inverse, norm_ref[2:3, :])
    low_three[:size, :] = bf16(third)
    grad_copy = to_mate(low_three.at[own], low_three.at[other])

    def back_rows(start, count):
        rows = low_three[start : start + count, :]
        for first in range(0, hidden_units, chunk):
            grad = dot(rows, shrink[:, first : first + chunk])
            spot = (slice(start, start + count), slice(first, first + chunk))
            slope[spot] = bf16(grad * f32(slope[spot]))

    back_rows(0, size)
    grad_copy.wait_recv()
    d_copies = []
    for start in (0, half):
        back_rows(size + start, half)
        d_send[start : start + half, :] = bf16(
            dot(slope[size + start : size + start + half, :], expand[...], NT)
        )
        d_copies.append(to_mate(d_send.at[pl.ds(start, half)], d_recv.at[pl.ds(start, half)]))
    y_own[...] = third + dot(slope[:size, :], expand[...], NT)
    for copy in d_copies:
        copy.wait_recv()
    second, gain_two, bias_two = norm_back(
        y_own[...] + f32(d_recv[...]), normed_two[...], inverse_two, norm_ref[1:2, :]
    )
    second_ref[...] = second
    low = bf16(second)
    sent = tokens_to_heads(
        n, lambda group: dot(low, wo[group]), blocks, dmix_ref, send_out, recv_out, own_sem
    )
    norm_grad_ref[...] = jnp.concatenate(
        [gain_two, gain_three, bias_two, bias_three, jnp.zeros((4, norm_grad_ref.shape[1]))], axis=0
    )
    for first in range(0, low_two.shape[1], 256):
        rows = slice(first, first + 256)
        shrink_grad_ref[rows, :] = bf16(dot(low_three[:, rows], act[...], TN))
        expand_grad_ref[rows, :] = bf16(dot(low_two[:, rows], slope[...], TN))
    for group in range(n):
        wo_grad_ref[:, group * width : (group + 1) * width] = bf16(dot(low, slots[group], TN))
    for copy in sent:
        copy.wait()
    for copy in pair + home_copies:
        copy.wait_send()


def feed(n, mixed, rest, home, hidden_one, cotangent, norms):
    total, width = mixed.shape
    side, model, units = home.shape[0], hidden_one.shape[1], home.shape[4] // 2
    size = total // n
    shape = jax.ShapeDtypeStruct
    dma = pltpu.SemaphoreType.DMA
    low, wide = jnp.bfloat16, jnp.float32
    return pl.pallas_call(
        partial(feed_kernel, n, side),
        out_shape=[
            shape((size, model), low),
            shape((size, model), wide),
            shape((total, width), low),
            shape((model, units), low),
            shape((model, units), low),
            shape((model, model), low),
            shape((8, model), wide),
        ],
        in_specs=[ANYWHERE] * 3 + [IN_VMEM, ANYWHERE, IN_VMEM],
        out_specs=[IN_VMEM] * 2 + [ANYWHERE] + [IN_VMEM] * 4,
        scratch_shapes=[
            pltpu.VMEM((n, model, width), low),
            pltpu.VMEM((model, 2 * units), low),
            pltpu.VMEM((n, size, width), low),
            pltpu.VMEM((size, model), wide),
            pltpu.VMEM((size, model), wide),
            pltpu.VMEM((2 * size, model), low),
            pltpu.VMEM((2 * size, model), low),
            pltpu.VMEM((2 * size, units), low),
            pltpu.VMEM((2 * size, units), low),
            pltpu.VMEM((size, model), wide),
            pltpu.VMEM((size, model), low),
            pltpu.VMEM((size, model), low),
            pltpu.VMEM((size, model), low),
            pltpu.VMEM((size, model), low),
            pltpu.VMEM((size, model), low),
            pltpu.VMEM((n, size, width), low),
            dma((2,)), dma((n,)), dma,
            dma((n - 1,)), dma((n - 1,)), dma((n - 1,)), dma((n - 1,)),
            dma((6,)), dma((6,)),
            dma((side * side,)), dma((side * side,)), dma((side * side,)),
        ],
        compiler_params=pltpu.CompilerParams(
            collective_id=2, has_side_effects=True, vmem_limit_bytes=VMEM_LIMIT
        ),
        cost_estimate=pl.CostEstimate(
            flops=80 * 10**9, bytes_accessed=8 * total * width, transcendentals=0
        ),
        name="feed",
    )(mixed, rest, home, hidden_one, cotangent, norms)


def cross_to_self_kernel(
    n, side, dq_ref, bundle_ref, second_ref, hidden_ref, normed_ref, inverse_ref, mixed_ref, gain_ref, norm_ref,
    half_a_ref, half_b_ref, first_ref, dmix_ref, weight_grad_ref, norm_grad_ref, feed_ref,
    wo, wq, slots, blocks, wo_sems, wq_sems, own_sem, send_in, recv_in, send_out, recv_out, *scratch,
):
    p = Place(n, side)
    halves = Halves(p, half_a_ref, half_b_ref, scratch)
    me = p.z
    size, model = second_ref.shape
    width = dq_ref.shape[1]
    loads = [
        pltpu.make_async_copy(dq_ref.at[rows_at(me, size)], slots.at[me], own_sem),
        *load_groups(n, bundle_ref, 2 * width, 0, width, wq, wq_sems),
        *load_groups(n, bundle_ref, 2 * width, width, width, wo, wo_sems),
    ]
    for load in loads:
        load.start()
    greet(p.line() + p.plane())
    copies = heads_to_tokens(n, dq_ref, slots, send_in, recv_in)
    halves.start()
    for load in loads:
        load.wait()
    upstream = merge_heads(
        n, slots, copies, lambda part, group: dot(part, wq[group], NT), second_ref[...]
    )
    first, gain_one, bias_one = norm_back(
        upstream, normed_ref[...], inverse_ref[:, 0:1], gain_ref[0:1, :]
    )
    first_ref[...] = first
    low = bf16(first)
    sent = tokens_to_heads(
        n, lambda group: dot(low, wo[group]), blocks, dmix_ref, send_out, recv_out, own_sem
    )
    hidden_low = bf16(hidden_ref[...])
    for group in range(n):
        cols = 2 * group * width
        weight_grad_ref[:, cols : cols + width] = bf16(dot(hidden_low, slots[group], TN))
        weight_grad_ref[:, cols + width : cols + 2 * width] = bf16(dot(low, mixed_ref[group], TN))
    rows = jnp.concatenate(
        [
            gain_one, norm_ref[0:2, :], bias_one, norm_ref[2:4, :],
            jnp.zeros((122, model), jnp.float32),
        ],
        axis=0,
    )
    norm_grad_ref[...] = bf16(rows.T)
    feed_ref[...] = bf16(halves.total())
    for copy in sent:
        copy.wait()


def cross_to_self(n_dp, n, dq, bundle, second, hidden, normed, inverse, slots, gains, norm_rows, halves):
    side = round((n_dp // 2) ** 0.5)
    half, columns = halves[0].shape[1:]
    total, width = dq.shape
    size, model = second.shape
    shape = jax.ShapeDtypeStruct
    dma = pltpu.SemaphoreType.DMA
    return pl.pallas_call(
        partial(cross_to_self_kernel, n, side),
        out_shape=[
            shape((size, model), jnp.float32),
            shape((total, width), jnp.bfloat16),
            shape((model, 2 * model), jnp.bfloat16),
            shape((model, 128), jnp.bfloat16),
            shape((2 * half, columns), jnp.bfloat16),
        ],
        in_specs=[ANYWHERE] * 2 + [IN_VMEM] * 9,
        out_specs=[IN_VMEM, ANYWHERE, IN_VMEM, IN_VMEM, IN_VMEM],
        scratch_shapes=[
            pltpu.VMEM((n, model, width), jnp.bfloat16),
            pltpu.VMEM((n, model, width), jnp.bfloat16),
            pltpu.VMEM((n, size, width), jnp.bfloat16),
            pltpu.VMEM((n, size, width), jnp.bfloat16),
            dma((n,)), dma((n,)), dma,
            dma((n - 1,)), dma((n - 1,)), dma((n - 1,)), dma((n - 1,)),
            *Halves.scratch(side, half, columns),
        ],
        compiler_params=pltpu.CompilerParams(
            collective_id=3, has_side_effects=True, vmem_limit_bytes=VMEM_LIMIT
        ),
        cost_estimate=pl.CostEstimate(
            flops=10**9, bytes_accessed=8 * total * width, transcendentals=0
        ),
        name="cross_to_self",
    )(dq, bundle, second, hidden, normed, inverse, slots, gains, norm_rows, *halves)


class Fold:
    def __init__(self, place, make, out, scratch, group, slack=2):
        self.n, self.me, self.make, self.out = place.n, place.z, make, out
        self.parts, self.held, self.down_send, self.down_recv, self.back_send, self.back_recv, self.own = scratch
        self.chunks = self.held.shape[1]
        self.ring = self.parts.shape[1]
        self.group, self.slack = group, slack
        self.ticks = self.chunks + slack * (2 * (self.n - 1) - 1)

    @staticmethod
    def scratch(chunks, rows, columns, ring=12):
        low, dma = jnp.bfloat16, pltpu.SemaphoreType.DMA((2, chunks))
        return [
            pltpu.VMEM((2, ring, rows, columns), low), pltpu.VMEM((2, chunks, rows, columns), low),
            dma, dma, dma, dma, dma,
        ]

    def _flows(self):
        n, me = self.n, self.me
        return (
            (0, me, lax.rem(me + 1, n), lax.rem(me + n - 1, n)),
            (1, n - 1 - me, lax.rem(me + n - 1, n), lax.rem(me + 1, n)),
        )

    def _down(self, flow, chunk, to, first):
        source = self.parts.at[flow, lax.rem(chunk, self.ring)] if first else self.held.at[flow, chunk]
        return pltpu.make_async_remote_copy(
            source, self.held.at[flow, chunk],
            self.down_send.at[flow, chunk], self.down_recv.at[flow, chunk],
            device_id={"mp": to}, device_id_type=MESH,
        )

    def _back(self, flow, chunk, to, first):
        source = (self.held if first else self.out).at[flow, chunk]
        return pltpu.make_async_remote_copy(
            source, self.out.at[flow, chunk],
            self.back_send.at[flow, chunk], self.back_recv.at[flow, chunk],
            device_id={"mp": to}, device_id_type=MESH,
        )

    def _keep(self, flow, chunk):
        return pltpu.make_async_copy(
            self.held.at[flow, chunk], self.out.at[flow, chunk], self.own.at[flow, chunk]
        )

    def tick(self, tick):
        last = self.n - 1
        for flow, spot, ahead, behind in self._flows():
            if tick < self.chunks:
                if tick % self.group == 0:
                    whole = bf16(self.make(flow, tick // self.group))
                    rows = whole.shape[0] // self.group
                    for index in range(self.group):
                        if tick + index >= self.ring:

                            @pl.when(spot == 0)
                            def _():
                                self._down(flow, tick + index - self.ring, ahead, True).wait_send()

                        self.parts[flow, (tick + index) % self.ring] = whole[
                            index * rows : (index + 1) * rows
                        ]

                @pl.when(spot == 0)
                def _():
                    self._down(flow, tick, ahead, True).start()

            chunk = tick - self.slack * spot

            @pl.when((spot > 0) & (chunk >= 0) & (chunk < self.chunks))
            def _():
                self._down(flow, chunk, ahead, False).wait_recv()
                self.held[flow, chunk] = bf16(
                    f32(self.held[flow, chunk]) + f32(self.parts[flow, lax.rem(chunk, self.ring)])
                )

                @pl.when(spot < last)
                def _():
                    self._down(flow, chunk, ahead, False).start()

                @pl.when(spot == last)
                def _():
                    self._back(flow, chunk, behind, True).start()
                    self._keep(flow, chunk).start()

            given = tick - self.slack * (2 * last - spot)

            @pl.when((spot > 0) & (spot < last) & (given >= 0) & (given < self.chunks))
            def _():
                self._back(flow, given, behind, False).wait_recv()
                self._back(flow, given, behind, False).start()

    def finish(self):
        last = self.n - 1
        for flow, spot, ahead, behind in self._flows():

            @pl.when(spot == 0)
            def _():
                def wait(chunk, carry):
                    self._back(flow, chunk, behind, False).wait_recv()
                    return carry

                lax.fori_loop(0, self.chunks, wait, 0)

                def sent(chunk, carry):
                    self._down(flow, chunk, ahead, True).wait_send()
                    return carry

                lax.fori_loop(max(self.chunks - self.ring, 0), self.chunks, sent, 0)

            @pl.when((spot > 0) & (spot < last))
            def _():
                def sent(chunk, carry):
                    self._down(flow, chunk, ahead, False).wait_send()
                    self._back(flow, chunk, behind, False).wait_send()
                    return carry

                lax.fori_loop(0, self.chunks, sent, 0)

            @pl.when(spot == last)
            def _():
                def sent(chunk, carry):
                    self._back(flow, chunk, behind, True).wait_send()
                    self._keep(flow, chunk).wait()
                    return carry

                lax.fori_loop(0, self.chunks, sent, 0)


class Everyone:
    def __init__(self, n_dp, n_mp, mine, slots, send_sems, recv_sems):
        self.n, self.n_mp = n_dp * n_mp, n_mp
        self.me = lax.axis_index("dp") * n_mp + lax.axis_index("mp")
        self.mine, self.slots, self.send, self.recv = mine, slots, send_sems, recv_sems

    def _to(self, distance):
        to = lax.rem(self.me + distance, self.n)
        return {"dp": to // self.n_mp, "mp": lax.rem(to, self.n_mp)}

    def _copy(self, distance):
        return pltpu.make_async_remote_copy(
            self.mine, self.slots.at[self.me], self.send.at[distance - 1], self.recv.at[distance - 1],
            device_id=self._to(distance), device_id_type=MESH,
        )

    def greet(self):
        barrier = pltpu.get_barrier_semaphore()

        def signal(distance, carry):
            pl.semaphore_signal(barrier, inc=1, device_id=self._to(distance), device_id_type=MESH)
            return carry

        lax.fori_loop(1, self.n, signal, 0)
        pl.semaphore_wait(barrier, self.n - 1)

    def start(self):
        def start(distance, carry):
            self._copy(distance).start()
            return carry

        self.slots[self.me] = self.mine[...]
        lax.fori_loop(1, self.n, start, 0)

    def finish(self):
        def wait(distance, carry):
            self._copy(distance).wait()
            return carry

        lax.fori_loop(1, self.n, wait, 0)
        return jnp.sum(self.slots[...], axis=0)


def moments(upstream, first_moment, second_moment, master, decay):
    first_new = first_decay * first_moment + (1.0 - first_decay) * upstream
    second_new = second_decay * second_moment + (1.0 - second_decay) * upstream * upstream
    direction = (
        first_new
        / (1.0 - first_decay**STEP)
        / (jnp.sqrt(second_new / (1.0 - second_decay**STEP)) + epsilon)
        + decay * master
    )
    return (first_new, second_new, direction)


def tensors(inner, outer, expand, shrink, norms):
    found = [inner.at[a, c] for a in range(2) for c in range(3)]
    found += [outer.at[0], outer.at[1], expand, shrink]
    found += [norms.at[pl.ds(row, 1)] for row in range(6)]
    return list(zip(found, [weight_decay] * 10 + [0.0] * 6))


def square_row(squares, share):
    lane = lax.broadcasted_iota(jnp.int32, (1, 128), 1)
    row = jnp.zeros((1, 128), jnp.float32)
    for index, values in enumerate(squares):
        total = jnp.sum(jnp.sum(values, axis=0, keepdims=True), axis=1, keepdims=True)
        row = jnp.where(lane == index, total * share if index >= 10 else total, row)
    return row


def update_kernel(split, *refs):
    (
        both_ref, layer_ref, sums_ref, grads, weights, firsts, seconds,
        states_ref, input_ref, output_ref, table_ref, new_weights, new_firsts, new_seconds,
        both, layer, wide, loads, stores,
    ) = (
        *refs[:3], refs[3:8], refs[8:13], refs[13:18], refs[18:23],
        *refs[23:27], refs[27:32], refs[32:37], refs[37:42], *refs[42:],
    )
    size, columns = both.shape[2], both.shape[3]
    chunks = both.shape[1]
    pieces, row = [], 0
    for source, held, first, count, target, start in (
        (both_ref.at[0], both.at[0], 0, split, states_ref, 0),
        (both_ref.at[1], both.at[1], 0, split, states_ref, split * size),
        (both_ref.at[0], both.at[0], split, chunks - split, input_ref, 0),
        (both_ref.at[1], both.at[1], split, chunks - split, input_ref, (chunks - split) * size),
        (layer_ref, layer, 0, layer_ref.shape[0], output_ref, 0),
    ):
        span = pl.ds(first, count)
        length = count * source.shape[1]
        load = pltpu.make_async_copy(source.at[span], held.at[span], loads.at[len(pieces)])
        store = pltpu.make_async_copy(
            wide.at[pl.ds(row, length)], target.at[pl.ds(start, length)], stores.at[len(pieces)]
        )
        pieces.append((load, store, held, first, count, row))
        row += length
    for piece in pieces:
        piece[0].start()
    for load, store, held, first, count, row in pieces:
        load.wait()
        length = held.shape[1]
        for index in range(count):
            wide[row + index * length : row + (index + 1) * length, :] = f32(held[first + index])
        store.start()
    lane = lax.broadcasted_iota(jnp.int32, (1, 128), 1)
    counts = jnp.where(lane < 8, float(D * D), jnp.where(lane < 10, float(D * FF), float(D)))
    weight_norm = jnp.sqrt(sums_ref[0:1, :] / counts)
    update_norm = jnp.sqrt(sums_ref[1:2, :] / counts)
    trust = weight_norm / (update_norm + epsilon)
    table_ref[...] = jnp.concatenate([weight_norm, update_norm, trust], axis=0)[:, :16]
    groups = [tensors(*group) for group in (grads, weights, firsts, seconds, new_weights, new_firsts, new_seconds)]
    for index, parts in enumerate(zip(*groups)):
        grad, weight, first, second, new_weight, new_first, new_second = [part[0] for part in parts]
        ratio = jnp.sum(jnp.where(lane == index, trust, 0.0), axis=1, keepdims=True)
        master = weight[...]
        first_new, second_new, direction = moments(
            grad[...], first[...], second[...], master, parts[0][1]
        )
        new_first[...] = first_new
        new_second[...] = second_new
        new_weight[...] = master - learn_rate * ratio * direction
    for piece in pieces:
        piece[1].wait()


def update(both, layer, source_rows, sums, grads, weights, firsts, seconds):
    shape = lambda values: jax.ShapeDtypeStruct(values.shape, jnp.float32)
    results = [shape(values) for values in weights]
    size, columns = both.shape[2:]
    split = source_rows // (2 * size)
    total = layer.shape[0] * layer.shape[1]
    wide = lambda rows: jax.ShapeDtypeStruct((rows, columns), jnp.float32)
    dma = pltpu.SemaphoreType.DMA((5,))
    return pl.pallas_call(
        partial(update_kernel, split),
        out_shape=[wide(source_rows), wide(total), wide(total)]
        + [jax.ShapeDtypeStruct((3, 16), jnp.float32)]
        + results * 3,
        in_specs=[ANYWHERE] * 2 + [IN_VMEM] * 21,
        out_specs=[ANYWHERE] * 3 + [IN_VMEM] * 16,
        scratch_shapes=[
            pltpu.VMEM(both.shape, jnp.bfloat16),
            pltpu.VMEM(layer.shape, jnp.bfloat16),
            pltpu.VMEM((source_rows + 2 * total, columns), jnp.float32),
            dma, dma,
        ],
        compiler_params=pltpu.CompilerParams(vmem_limit_bytes=VMEM_LIMIT),
        name="update",
    )(both, layer, sums, *grads, *weights, *firsts, *seconds)


def finish_kernel(
    n, side, units, width, prefix_ref, q_ref, k_ref, v_ref, do_ref, o_ref, row_sums_ref,
    near_ref, x_ref, first_ref, cross_dk_ref, cross_dv_ref, rest_ref,
    feed_ref, cross_wo_ref, weight_ref, norm_ref, source_grad_ref, *refs,
):
    states, refs = refs[:15], refs[15:]
    out_ref, sums_ref, grads, refs = refs[0], refs[1], refs[2:7], refs[7:]
    (
        source_ref, source_sem, dq_ref, dk_ref, dv_ref, query_acc, delta, master_sems, inner, stage, far_recv, group_send, group_recv,
        far_send_sem, far_recv_sem, group_send_sems, group_recv_sems,
        mine, slots, everyone_send, everyone_recv, *scratch,
    ) = refs
    n_dp = 2 * side * side
    p = Place(n, side)
    everyone = Everyone(n_dp, n, mine, slots, everyone_send, everyone_recv)

    me = p.z
    own_heads = (dq_ref, dk_ref, dv_ref)
    size, model = first_ref.shape
    rows = inner.shape[3]
    per_group = 4
    group_rows = per_group * out_ref.shape[2]
    source_groups = cross_dk_ref.shape[0] // (2 * group_rows)

    def make(flow, group):
        if group < source_groups:
            spot = pl.ds((flow * source_groups + group) * group_rows, group_rows)
            return dot(cross_dk_ref[spot, :], source_ref[:, :width], NT) + dot(
                cross_dv_ref[spot, :], source_ref[:, width:], NT
            )
        tokens = x_ref.shape[0]
        start = flow * (tokens // 2) + (group - source_groups) * group_rows
        spot = pl.ds(start, group_rows)
        total = jnp.zeros((group_rows, model), jnp.float32)
        for index, own in enumerate(own_heads):
            total = total + dot(own[spot, :], near_ref[:, index * width : (index + 1) * width], NT)
        here = first_ref[start % size : start % size + group_rows, :]
        return total + jnp.where(me == start // size, here, 0.0)

    fold = Fold(p, make, out_ref, scratch[:7], per_group)
    group_sum = Reduce(p, [cross_wo_ref, weight_ref, norm_ref, source_grad_ref], scratch[7:15])
    inner_sum = Reduce(p, [inner], scratch[15:23])

    source_load = pltpu.make_async_copy(
        rest_ref.at[:, pl.ds(n * width, 2 * width)], source_ref, source_sem
    )
    source_load.start()
    everyone.greet()
    group_sum.core_start()
    far = {"mp": lax.rem(me + n // 2, n)}
    far_copies = [
        push(
            feed_ref.at[:, pl.ds((2 * index + 1) * units, units)],
            far_recv.at[:, pl.ds(index * units, units)],
            far_send_sem.at[index], far_recv_sem.at[index], far,
        )
        for index in range(2)
    ]

    source_load.wait()
    ticks = iter(range(fold.ticks))

    def advance(count):
        for _ in range(count):
            fold.tick(next(ticks))

    advance(1)
    backward_delta(do_ref, o_ref, delta)
    query_acc[...] = jnp.zeros_like(query_acc)
    key_block = 256

    def self_backward(index, heads):
        backward_block(
            True, key_block, index, heads, prefix_ref, q_ref, k_ref, v_ref, do_ref, row_sums_ref, delta,
            query_acc, dk_ref, dv_ref,
        )

    advance(1)
    group_sum.core_finish(stage)
    group_sum.first_start()
    for index in range(x_ref.shape[0] // key_block):
        for heads in ((0, 1), (2, 3)):
            self_backward(index, heads)
            advance(1)
    dq_ref[...] = bf16(query_acc[...])

    per = 256
    for start in range(0, model, per):
        turned = x_ref[:, start : start + per]
        for index, own in enumerate(own_heads):
            block = bf16(dot(turned, own[...], TN))
            for row in range(0, per, rows):
                flat = (start + row) // rows
                y, x, core = flat // (2 * side), flat // 2 % side, flat % 2
                inner[y, x, core, :, index * width : (index + 1) * width] = block[row : row + rows]
    inner_sum.core_start()
    advance(1)
    inner_sum.core_finish(stage)
    inner_sum.first_start()
    advance(2)
    group_sum.first_finish()
    group_sum.second_start()
    advance(1)
    advance(1)
    inner_sum.first_finish()
    inner_sum.second_start()
    advance(1)
    group_sum.second_wait()
    whole = n * width
    for group in range(n):
        group_send[group, :, :width] = bf16(
            group_sum.total(slice(group * width, (group + 1) * width))
        )
        start = whole + 2 * group * width
        group_send[group, :, width : 3 * width] = bf16(
            group_sum.total(slice(start, start + 2 * width))
        )
        group_send[group, :, 3 * width :] = bf16(
            group_sum.total(slice(3 * whole, 3 * whole + norm_ref.shape[4]))
        )
    group_copies = []
    for distance in range(1, n):
        to = lax.rem(me + distance, n)
        group_copies.append(
            push(
                group_send.at[to], group_recv.at[distance - 1],
                group_send_sems.at[distance - 1], group_recv_sems.at[distance - 1], {"mp": to},
            )
        )
    advance(2)

    def optimizer_sums(*masters):
        master_loads = [
            pltpu.make_async_copy(source, target, master_sems.at[index])
            for index, (source, target) in enumerate(zip(states, masters))
        ]
        for load in master_loads:
            load.start()
        grad_inner, grad_outer, grad_expand, grad_shrink, grad_norms = grads
        inner_sum.second_wait()
        for index in range(3):
            grad_inner[0, index] = inner_sum.total(slice(index * width, (index + 1) * width))
        start = 3 * whole + norm_ref.shape[4]
        for index in range(2):
            grad_inner[1, index + 1] = group_sum.total(
                slice(start + index * width, start + (index + 1) * width)
            )
        for load in master_loads:
            load.wait()
        weights, firsts, seconds = (tensors(*masters[index : index + 5]) for index in (0, 5, 10))
        share = 1.0 / n
        mine[...] = jnp.zeros(mine.shape, jnp.float32)
        mine[0:1, :] = square_row([ref[...] * ref[...] for ref, _ in weights], share)
        advance(2)
        for copy in far_copies:
            copy.wait_recv()
        grad_shrink[...] = (f32(feed_ref[:, :units]) + f32(far_recv[:, :units])).T
        grad_expand[...] = f32(feed_ref[:, 2 * units : 3 * units]) + f32(far_recv[:, units:])
        advance(2)
        for distance in range(1, n):
            group_copies[distance - 1].wait_recv()
        received = lambda cols: sum(
            [f32(group_recv[distance - 1, :, cols]) for distance in range(1, n)],
            f32(group_send[me, :, cols]),
        )
        grad_outer[1] = received(slice(0, width)).T
        grad_inner[1, 0] = received(slice(width, 2 * width))
        grad_outer[0] = received(slice(2 * width, 3 * width)).T
        grad_norms[...] = received(slice(3 * width, 3 * width + norm_ref.shape[4])).T[:6, :]

        def direction_square(grad, first, second, weight):
            step = moments(grad[0][...], first[0][...], second[0][...], weight[0][...], weight[1])[2]
            return step * step

        mine[1:2, :] = square_row(
            [direction_square(*group) for group in zip(tensors(*grads), firsts, seconds, weights)], share
        )
        everyone.start()
        advance(4)
        sums_ref[...] = everyone.finish()

    pl.run_scoped(optimizer_sums, *[pltpu.VMEM(source.shape, jnp.float32) for source in states])
    for tick in ticks:
        fold.tick(tick)
    fold.finish()
    for copy in (*far_copies, *group_copies):
        copy.wait_send()
    for batch in (group_sum, inner_sum):
        batch.finish()


def finish(
    n_dp, n_mp, prefix, projections, grad_out, mixed, row_sums, near, tokens, first,
    source_heads, rest, feed_grad, cross_wo, weights, norms, source_grad, states,
):
    side = round((n_dp // 2) ** 0.5)
    total, width = mixed.shape
    size, model = first.shape
    units = feed_grad.shape[1] // 4
    rows = model // n_dp
    low, wide = jnp.bfloat16, jnp.float32
    shape = jax.ShapeDtypeStruct
    dma = pltpu.SemaphoreType.DMA
    by_place = lambda values: values.reshape(side, side, 2, rows, values.shape[1])
    early = [by_place(values) for values in (cross_wo, weights, norms, source_grad)]
    columns = sum(values.shape[4] for values in early)
    bundle = 3 * width + norms.shape[1]
    devices = n_dp * n_mp
    chunk_rows = 64
    chunks = (total + source_heads[0].shape[0]) // (2 * chunk_rows)
    both, sums, *grads = pl.pallas_call(
        partial(finish_kernel, n_mp, side, units, width),
        out_shape=[shape((2, chunks, chunk_rows, model), low), shape((8, 128), wide)]
        + [shape(values.shape, wide) for values in states[:5]],
        in_specs=[pl.BlockSpec(memory_space=pltpu.SMEM)]
        + [IN_VMEM] * 11
        + [ANYWHERE, IN_VMEM]
        + [ANYWHERE] * (4 + len(states)),
        out_specs=[ANYWHERE] + [IN_VMEM] * 6,
        scratch_shapes=[
            pltpu.VMEM((model, 2 * width), low),
            dma,
            *[pltpu.VMEM((total, width), low)] * 3,
            pltpu.VMEM((total, width), wide),
            pltpu.VMEM((8, total), wide),
            dma((len(states),)),
            pltpu.VMEM((side, side, 2, rows, 3 * width), low),
            pltpu.VMEM((2, rows, columns), low),
            pltpu.VMEM((rows, 2 * units), low),
            pltpu.VMEM((n_mp, rows, bundle), low),
            pltpu.VMEM((n_mp - 1, rows, bundle), low),
            dma((2,)), dma((2,)), dma((n_mp - 1,)), dma((n_mp - 1,)),
            pltpu.VMEM((8, 128), wide),
            pltpu.VMEM((devices, 8, 128), wide),
            dma((devices - 1,)), dma((devices - 1,)),
            *Fold.scratch(chunks, chunk_rows, model),
            *Reduce.scratch(side, rows, columns, 4),
            *Reduce.scratch(side, rows, 3 * width, 1),
        ],
        compiler_params=pltpu.CompilerParams(
            collective_id=5, has_side_effects=True, vmem_limit_bytes=VMEM_LIMIT
        ),
        cost_estimate=pl.CostEstimate(flops=10**9, bytes_accessed=1 << 20, transcendentals=0),
        name="finish",
    )(
        prefix, *projections, grad_out, mixed, row_sums, near, tokens, first, *source_heads,
        rest, feed_grad, *early, *states,
    )
    return both, sums, grads


def on_device(
    inputs,
    encoder,
    prefix,
    cotangent,
    inner_weights,
    inner_first,
    inner_second,
    outer_weights,
    outer_first,
    outer_second,
    expand_weights,
    expand_first,
    expand_second,
    shrink_weights,
    shrink_first,
    shrink_second,
    norm_params,
    norm_first,
    norm_second,
):
    n_dp, n_mp = lax.axis_size("dp"), lax.axis_size("mp")
    seq_count, seq_len, model = inputs.shape
    tokens = inputs.reshape(seq_len, model)
    states = encoder.reshape(-1, model)
    rows, width = inner_weights.shape[2:]
    units = expand_weights.shape[1]

    norm_t = jnp.pad(bf16(norm_params).reshape(6, rows).T, ((0, 0), (0, 122)))
    near, bundle, later_block, feed_block, self_q, self_k, self_v, self_mixed, self_sums = front(
        n_dp, n_mp, prefix, inner_weights, bf16(jnp.swapaxes(outer_weights, 1, 2)), norm_t,
        expand_weights, bf16(shrink_weights.T), tokens,
    )
    by_rows = lambda values: values.reshape(model, values.shape[-1])
    near, bundle = by_rows(near), by_rows(bundle)
    hidden_one, normed_one, inverse_one, self_slots, norms, cross_query, home, rest = self_to_cross(
        n_dp, n_mp, self_mixed, bundle, tokens, feed_block, later_block
    )
    rest = by_rows(rest)
    cross_k, cross_v, cross_mixed, cross_sums, home = cross_forward(
        n_mp, cross_query, states, rest, home
    )
    out_rows, grad_second, cross_dmix, shrink_grad, expand_grad, cross_wo_grad, norm_rows = feed(
        n_mp, cross_mixed, rest, home, hidden_one, cotangent.reshape(seq_len, model), norms,
    )
    cross_dq, cross_dk, cross_dv, layer_low, source_grad, *halves = cross_backward(
        n_dp, n_mp, cross_query, cross_k, cross_v, cross_dmix, cross_mixed, cross_sums, prefix, out_rows,
        states, shrink_grad, expand_grad,
    )
    grad_first, self_dmix, weight_grad, norm_grad, feed_grad = cross_to_self(
        n_dp, n_mp, cross_dq, bundle, grad_second, hidden_one, normed_one, inverse_one,
        self_slots, norms, norm_rows, halves,
    )
    flat = lambda values: values.reshape(6, rows)
    weights = [inner_weights, outer_weights, expand_weights, shrink_weights, flat(norm_params)]
    firsts = [inner_first, outer_first, expand_first, shrink_first, flat(norm_first)]
    seconds = [inner_second, outer_second, expand_second, shrink_second, flat(norm_second)]
    both, sums, grads = finish(
        n_dp, n_mp, prefix, (self_q, self_k, self_v), self_dmix, self_mixed, self_sums, near, tokens,
        grad_first, (cross_dk, cross_dv), rest,
        feed_grad, cross_wo_grad, weight_grad, norm_grad, source_grad,
        weights + firsts + seconds,
    )
    encoder_grad, input_grad, layer_out, table, *results = update(
        both, layer_low, states.shape[0], sums, grads, weights, firsts, seconds
    )
    for index in (4, 9, 14):
        results[index] = results[index].reshape(2, 3, rows)
    return (
        layer_out.reshape(seq_count, seq_len, model),
        input_grad.reshape(seq_count, seq_len, model),
        encoder_grad.reshape(seq_count, -1, model),
        *results,
        table,
    )


def solution(mesh):
    placed = (
        P("dp", None, None),
        P("dp", None, None),
        P("dp"),
        P("dp", None, None),
        P(None, None, "dp", "mp"),
        P(None, None, "dp", "mp"),
        P(None, None, "dp", "mp"),
        P(None, "mp", "dp"),
        P(None, "mp", "dp"),
        P(None, "mp", "dp"),
        P("dp", "mp"),
        P("dp", "mp"),
        P("dp", "mp"),
        P("mp", "dp"),
        P("mp", "dp"),
        P("mp", "dp"),
        P(None, None, "dp"),
        P(None, None, "dp"),
        P(None, None, "dp"),
    )
    return jax.shard_map(
        on_device,
        mesh=mesh,
        in_specs=placed,
        out_specs=(
            P("dp", None, None),
            P("dp", None, None),
            P("dp", None, None),
            P(None, None, "dp", "mp"),
            P(None, "mp", "dp"),
            P("dp", "mp"),
            P("mp", "dp"),
            P(None, None, "dp"),
            P(None, None, "dp", "mp"),
            P(None, "mp", "dp"),
            P("dp", "mp"),
            P("mp", "dp"),
            P(None, None, "dp"),
            P(None, None, "dp", "mp"),
            P(None, "mp", "dp"),
            P("dp", "mp"),
            P("mp", "dp"),
            P(None, None, "dp"),
            P(),
        ),
        check_vma=False,
    )
```

time: 594 us -> 517 us (0.87)
  Pallas kernels: 543 us -> 500 us
  local copies, waits for them, and re-layouts: 21.1 us -> 7.41 us
  other arithmetic: 11.1 us -> 0.69 us
  matrix products: 6.76 us -> 0 us
    pallas_call x1, Pallas kernels: 227 us -> 200 us  [finish(): pl.pallas_call(partial(finish_kernel, n_mp, side, units, width), out_shap...]
    pallas_call x1, Pallas kernels: 58.3 us -> 44.4 us  [self_to_cross(): pl.pallas_call(partial(self_to_cross_kernel, n, side), out_shape=[shape((...]
    slice x8 -> x0, local copies, waits for them, and re-layouts: 11.1 us -> none  [the longest x2 4.39 us: finish(): return (both[:, :split], both[:, split:], sums, grads)]
    reshape x3 -> x0, other arithmetic: 9.39 us -> none  [the longest x1 4.43 us: on_device(): f32(encoder_low).reshape(seq_count, -1, model)]
    dot_general x2 -> x0, matrix products: 6.76 us -> none  [dot(): lax.dot_general(left, right, dims, preferred_element_type=jnp.float32)]
    pallas_call x7 -> x5, Pallas kernels: 172 us -> 170 us  [the longest x1 49.7 us: front(): pl.pallas_call(partial(front_kernel, n_mp, side), out_shape=[shape((side,...]
where the time goes in v3:
time: 517 us; the launch traced here: 510 us
  Pallas kernels  500 us (97%)
  local copies, waits for them, and re-layouts  7.41 us (1%)
    pallas_call x1, Pallas kernels, finish(): pl.pallas_call(partial(finish_kernel, n_mp, side, units, width), out_shap...  200 us
    pallas_call x1, Pallas kernels, feed(): pl.pallas_call(partial(feed_kernel, n, side), out_shape=[shape((size, mod...  85.3 us
    pallas_call x1, Pallas kernels, front(): pl.pallas_call(partial(front_kernel, n_mp, side), out_shape=[shape((side,...  49.7 us
    pallas_call x1, Pallas kernels, cross_backward(): pl.pallas_call(partial(cross_backward_kernel, n, side), grid_spec=pltpu.P...  48 us
    pallas_call x1, Pallas kernels, self_to_cross(): pl.pallas_call(partial(self_to_cross_kernel, n, side), out_shape=[shape((...  44.4 us
    pallas_call x1, Pallas kernels, cross_forward(): pl.pallas_call(partial(cross_forward_kernel, side, n), out_shape=[shape((...  29.4 us
    pallas_call x1, Pallas kernels, cross_to_self(): pl.pallas_call(partial(cross_to_self_kernel, n, side), out_shape=[shape((...  29 us
    pallas_call x1, Pallas kernels, update(): pl.pallas_call(partial(update_kernel, split), out_shape=[wide(source_rows...  14 us

profile of v3, /device:TPU:0, one launch (start us, length us, event | category | flops | bytes accessed | tf_op | source)
XLA Modules:
  0.0 510.1 jit_solution(13926680210033403025)
XLA Ops:
  1.3 1.2 copy.51
  2.5 1.1 copy.48
  3.5 0.7 convert_element_type.17
  4.3 0.1 copy.50
  4.4 49.7 %front.1 = (bf16[2,2,2,128,768]{4,3,2,1,0:T(8,128)(2,1)}, bf16[2,2,2,128,2176]{4,3,2,1,0:T(8,128)(2,1)}, bf16[128,1536]{1,0:T(8,128)(2,1)S(1)}, bf16[128,4096]{1...) custom-call(s32[1]{0:T(128)S(6)} %copy.59.prefix_ref, ...), custom_call_target="tpu_custom_call" | custom-call | flops 40000000000 | bytes 1048576 | tf_op jit(solution)/shard_map/front/pallas_call | solution.py:731
  54.1 0.0 copy-start.3
  54.1 0.8 copy-done.3
  54.9 0.0 copy-start.4
  54.9 0.8 copy-done.4
  55.7 44.4 %self_to_cross.1 = (f32[256,1024]{1,0:T(8,128)}, f32[256,1024]{1,0:T(8,128)}, f32[256,128]{1,0:T(8,128)S(1)}, bf16[4,256,256]{2,1,0:T(8,128)(2,1)S(1)}, f32[8,10...) custom-call(bf16[1024,256]{1,0:T(8,128)(2,1)} %get-tuple-element.89., ...), custom_call_target="tpu_custom_call" | custom-call | flops 1000000000 | bytes 2097152 | tf_op jit(solution)/shard_map/self_to_cross/pallas_call | solution.py:830
  100.1 29.4 %cross_forward.1 = (bf16[2048,256]{1,0:T(8,128)(2,1)}, bf16[2048,256]{1,0:T(8,128)(2,1)}, bf16[1024,256]{1,0:T(8,128)(2,1)S(1)}, f32[8,1024]{1,0:T(8,128)S(1)}, bf16[2,2,2,128,4096]{4,3,2,1,0:T(8,128)(2,1)}) custom-call(bf16[1024,256]{1,0:T(8,128)(2,1)S(1)} %get-tuple-element.93.q_ref, bf16[2048,1024]{1,0:T(8,128)(2,1)} %bitcast.39, ...), custom_call_target="tpu_custom_call", output_to_operand_aliasing={{4}: (3, {})} | custom-call | flops 10000000000 | bytes 1048576 | tf_op jit(solution)/shard_map/cross_forward/pallas_call | solution.py:897
  129.6 0.0 copy-start.6
  129.6 85.3 %feed.1 = (bf16[256,1024]{1,0:T(8,128)(2,1)S(1)}, f32[256,1024]{1,0:T(8,128)}, bf16[1024,256]{1,0:T(8,128)(2,1)S(1)}, bf16[1024,2048]{1,0:T(8,128)(2,1)}, bf16[1...) custom-call(bf16[1024,256]{1,0:T(8,128)(2,1)S(1)} %get-tuple-element.98.mixed_ref.o_ref, ...), custom_call_target="tpu_custom_call" | custom-call | flops 80000000000 | bytes 2097152 | tf_op jit(solution)/shard_map/feed/pallas_call | solution.py:1066
  214.9 0.0 copy-done.6
  214.9 0.0 copy-start.7
  214.9 0.8 copy-done.7
  215.7 48.0 %cross_backward.1 = (bf16[1024,256]{1,0:T(8,128)(2,1)S(1)}, bf16[2048,256]{1,0:T(8,128)(2,1)}, bf16[2048,256]{1,0:T(8,128)(2,1)}, bf16[4,256,1024]{2,1,0:T(8,128...) custom-call(s32[1]{0:T(128)S(6)} %copy.59.prefix_ref, ...), custom_call_target="tpu_custom_call" | custom-call | flops 21474836480 | bytes 2097152 | tf_op jit(solution)/shard_map/cross_backward/pallas_call | solution.py:588
  263.7 0.0 copy-start.8
  263.7 0.0 copy-start.9
  263.7 0.0 copy-start.10
  263.7 0.0 copy-start
  263.7 0.0 copy-start.1
  263.7 0.0 copy-start.2
  263.7 29.0 %cross_to_self.1 = (f32[256,1024]{1,0:T(8,128)}, bf16[1024,256]{1,0:T(8,128)(2,1)S(1)}, bf16[1024,2048]{1,0:T(8,128)(2,1)}, bf16[1024,128]{1,0:T(8,128)(2,1)S(1)}, bf16[128,4096]{1,0:T(8,128)(2,1)}) custom-call(bf16[1024,256]{1,0:T(8,128)(2,1)S(1)} %get-tuple-element.107.dq_ref, bf16[1024,2176]{1,0:T(8,128)(2,1)} %bitcast.26, ...), custom_call_target="tpu_custom_call" | custom-call | flops 1000000000 | bytes 2097152 | tf_op jit(solution)/shard_map/cross_to_self/pallas_call | solution.py:1169
  292.7 0.0 copy-start.5
  292.8 0.8 copy-done.5
  293.5 0.0 copy-done.8
  293.6 0.0 copy-done.9
  293.6 0.0 copy-done.10
  293.6 0.0 copy-done
  293.6 0.0 copy-done.1
  293.6 0.0 copy-done.2
  293.6 200.5 %finish.1 = (bf16[2,24,64,1024]{3,2,1,0:T(8,128)(2,1)}, f32[8,128]{1,0:T(8,128)S(1)}, f32[2,3,128,256]{3,2,1,0:T(8,128)}, f32[2,256,128]{2,1,0:T(8,128)S(1)}, f3...) custom-call(s32[1]{0:T(128)S(6)} %copy.59.prefix_ref, bf16[1024,256]{1,0:T(8,128)(2,1)} %copy-done.3, ...), custom_call_target="tpu_custom_call" | custom-call | flops 1000000000 | bytes 1048576 | tf_op jit(solution)/shard_map/finish/pallas_call | solution.py:1691
  494.1 14.0 %update.1 = (f32[2048,1024]{1,0:T(8,128)}, f32[1024,1024]{1,0:T(8,128)}, f32[1024,1024]{1,0:T(8,128)}, f32[3,16]{1,0:T(4,128)}, f32[2,3,128,256]{3,2,1,0:T(8,128...) custom-call(bf16[2,24,64,1024]{3,2,1,0:T(8,128)(2,1)} %get-tuple-ele, ...), custom_call_target="tpu_custom_call" | custom-call | tf_op jit(solution)/shard_map/update/pallas_call | solution.py:1463
  508.1 0.6 copy.55
  508.7 0.6 copy.56
  509.3 0.6 copy.57
  (12 shorter events, 0.1 us)
Async XLA Ops:
  54.1 0.8 copy-start.3
  54.9 0.8 copy-start.4
  129.6 85.3 %copy-start.6 = (bf16[1024,256]{1,0:T(8,128)(2,1)}, bf16[1024,256]{1,0:T(8,128)(2,1)S(1)}, u32[]{:S(2)}) copy-start(bf16[1024,256]{1,0:T(8,128)(2,1)S(1)} %get-tuple-element.98.mixed_ref.o_ref) | copy-start | bytes 1572868
  214.9 0.8 copy-start.7
  263.7 29.9 %copy-start.8 = (f32[2,3,128]{2,0,1:T(2,128)S(1)}, f32[2,3,128]{2,0,1:T(2,128)}, u32[]{:S(2)}) copy-start(f32[2,3,128]{2,0,1:T(2,128)} %param.35) | copy-start | bytes 9220
  263.7 29.9 %copy-start.9 = (f32[2,3,128]{2,0,1:T(2,128)S(1)}, f32[2,3,128]{2,0,1:T(2,128)}, u32[]{:S(2)}) copy-start(f32[2,3,128]{2,0,1:T(2,128)} %param.36) | copy-start | bytes 9220
  263.7 29.9 %copy-start.10 = (f32[2,3,128]{2,0,1:T(2,128)S(1)}, f32[2,3,128]{2,0,1:T(2,128)}, u32[]{:S(2)}) copy-start(f32[2,3,128]{2,0,1:T(2,128)} %param.37) | copy-start | bytes 9220
  263.7 29.9 %copy-start = (f32[2,256,128]{2,1,0:T(8,128)S(1)}, f32[2,256,128]{2,1,0:T(8,128)}, u32[]{:S(2)}) copy-start(f32[2,256,128]{2,1,0:T(8,128)} %refs_9_.1) | copy-start | bytes 786436
  263.7 29.9 %copy-start.1 = (f32[2,256,128]{2,1,0:T(8,128)S(1)}, f32[2,256,128]{2,1,0:T(8,128)}, u32[]{:S(2)}) copy-start(f32[2,256,128]{2,1,0:T(8,128)} %refs_14_.1) | copy-start | bytes 786436
  263.7 29.9 %copy-start.2 = (f32[2,256,128]{2,1,0:T(8,128)S(1)}, f32[2,256,128]{2,1,0:T(8,128)}, u32[]{:S(2)}) copy-start(f32[2,256,128]{2,1,0:T(8,128)} %refs_19_.1) | copy-start | bytes 786436
  292.7 0.8 copy-start.5

commit v4 on v3

--- a/solution.py
+++ b/solution.py
@@ -26,7 +26,7 @@
 NN = (((1,), (0,)), ((), ()))
 NT = (((1,), (1,)), ((), ()))
 TN = (((0,), (0,)), ((), ()))
-VMEM_LIMIT = 52 << 20
+VMEM_LIMIT = 60 << 20
 
 
 def dot(left, right, dims=NN):
@@ -115,21 +115,6 @@
 
 def rows_at(index, size):
     return pl.ds(pl.multiple_of(index * size, size), size)
-
-
-def heads_to_tokens(n, source, slots, send_sems, recv_sems):
-    me = lax.axis_index("mp")
-    size = source.shape[0] // n
-    copies = []
-    for distance in range(1, n):
-        to = lax.rem(me + distance, n)
-        copies.append(
-            push(
-                source.at[rows_at(to, size)], slots.at[me],
-                send_sems.at[distance - 1], recv_sems.at[distance - 1], {"mp": to},
-            )
-        )
-    return copies
 
 
 def tokens_to_heads(n, make, blocks, target, send_sems, recv_sems, local_sem):
@@ -154,18 +139,6 @@
     return copies
 
 
-def merge_heads(n, slots, copies, part_of, start):
-    me = lax.axis_index("mp")
-    total = start + part_of(slots[me], me)
-    for distance in range(1, n):
-        origin = lax.rem(me + n - distance, n)
-        copies[distance - 1].wait_recv()
-        total = total + part_of(slots[origin], origin)
-    for copy in copies:
-        copy.wait_send()
-    return total
-
-
 def load_groups(n, bundle, stride, first, width, target, sems):
     return [
         pltpu.make_async_copy(
@@ -442,7 +415,7 @@
     if masked:
         keys = max(keys // 2, start + block)
     lane = lax.broadcasted_iota(jnp.int32, (block, width), 1) // HEAD
-    span = slice(start, start + block)
+    span = slice(start, start + block) if masked else rows_at(start, block)
     query = q_ref[span, :] * jnp.bfloat16(HEAD**-0.5)
     key_rows, value_rows = k_ref[:keys, :], v_ref[:keys, :]
     if masked:
@@ -518,63 +491,102 @@
 
 
 def cross_backward_kernel(
-    n, side, prefix_ref, q_ref, k_ref, v_ref, do_ref, o_ref, sums_ref, mine_ref, states_ref,
-    shrink_ref, expand_ref, dq_ref, dk_ref, dv_ref, all_ref, source_ref, half_a_ref, half_b_ref,
-    acc, delta, source, stage, own_sem, *scratch,
+    n, side, q_ref, k_ref, v_ref, do_ref, o_ref, sums_ref, mine_ref, states_ref, shrink_ref, expand_ref,
+    slots_ref, dk_ref, dv_ref, all_ref, source_ref, half_a_ref, half_b_ref,
+    scaled_keys, key_acc, value_acc, delta, blocks, stage, own_sem, dq_send, dq_recv, *scratch,
 ):
     p = Place(n, side)
     give = Give(p, all_ref, scratch[:4])
     feed_sum = Reduce(p, [shrink_ref, expand_ref], scratch[4:])
     width = q_ref.shape[1]
-    step = pl.program_id(0)
-    steps = pl.num_programs(0)
-
-    @pl.when(step == 0)
-    def _():
-        own = pltpu.make_async_copy(mine_ref, all_ref.at[give.me], own_sem)
-        own.start()
-        greet(p.line() + p.plane())
-        feed_sum.core_start()
-        own.wait()
-        give.step(0)
-        backward_delta(do_ref, o_ref, delta)
-        acc[...] = jnp.zeros_like(acc)
-        source[...] = jnp.zeros_like(source)
-
-    for later in range(1, n - 1):
-
-        @pl.when(step == (later + 1) * steps // n)
+    size = blocks.shape[1]
+    heads = range(width // HEAD)
+    factor = HEAD**-0.5
+    own = pltpu.make_async_copy(mine_ref, all_ref.at[p.z], own_sem)
+    own.start()
+    greet(p.line() + p.plane())
+    feed_sum.core_start()
+    own.wait()
+    give.step(0)
+    backward_delta(do_ref, o_ref, delta)
+    scaled_keys[...] = k_ref[...] * jnp.bfloat16(factor)
+    key_acc[...] = jnp.zeros_like(key_acc)
+    value_acc[...] = jnp.zeros_like(value_acc)
+    lane = lax.broadcasted_iota(jnp.int32, (size, width), 1) // HEAD
+    chunk = 512
+
+    def dq_copy(distance):
+        to = lax.rem(p.z + distance, n)
+        return pltpu.make_async_remote_copy(
+            blocks.at[to], slots_ref.at[p.z], dq_send.at[distance - 1], dq_recv.at[distance - 1],
+            device_id={"mp": to}, device_id_type=MESH,
+        )
+
+    def one_block(step, carry):
+        block = lax.rem(p.z + 1 + step, n)
+        span = rows_at(block, size)
+        query, grad_rows = q_ref[span, :], do_ref[span, :]
+        stacked = lambda values: jnp.concatenate(
+            [jnp.where(lane == head, values, jnp.bfloat16(0)) for head in heads], axis=0
+        )
+        across = lambda ref: jnp.concatenate([ref[head : head + 1, span] for head in heads], axis=1)
+        own_query, own_grad = stacked(query), stacked(grad_rows)
+        row_sums, row_delta = across(sums_ref), across(delta)
+        all_grads = jnp.zeros((len(heads) * size, width), jnp.float32)
+        for first in range(0, k_ref.shape[0], chunk):
+            rows = slice(first, first + chunk)
+            if first == chunk:
+
+                @pl.when(step == 0)
+                def _():
+                    feed_sum.core_start(False)
+                    feed_sum.core_finish(stage)
+                    feed_sum.first_start()
+
+            if first == 2 * chunk:
+
+                @pl.when(step == 2)
+                def _():
+                    give.step(1)
+
+            probs = jnp.exp(dot(scaled_keys[rows, :], own_query, NT) - row_sums)
+            prob_grad = dot(v_ref[rows, :], own_grad, NT)
+            score_grad = bf16(probs * (prob_grad - row_delta))
+            value_acc[rows, :] += dot(bf16(probs), own_grad)
+            key_acc[rows, :] += dot(score_grad, own_query)
+            all_grads = all_grads + dot(score_grad, scaled_keys[rows, :], TN)
+        query_grad = jnp.zeros((size, width), jnp.float32)
+        for head in heads:
+            query_grad = jnp.where(
+                lane == head, all_grads[head * size : (head + 1) * size], query_grad
+            )
+        blocks[block] = bf16(query_grad)
+
+        @pl.when(step < n - 1)
         def _():
-            give.step(later)
-
-    @pl.when(step == 1)
-    def _():
-        feed_sum.core_start(False)
-        feed_sum.core_finish(stage)
-        feed_sum.first_start()
-
-    backward_block(
-        False, k_ref.shape[0], 0, tuple(range(width // HEAD)),
-        prefix_ref, q_ref, k_ref, v_ref, do_ref, sums_ref, delta, acc, dk_ref, dv_ref,
-    )
-    source[:, :width] += dot(states_ref[...], dk_ref[...], TN)
-    source[:, width:] += dot(states_ref[...], dv_ref[...], TN)
-
-    @pl.when(step == steps - 1)
-    def _():
-        dq_ref[...] = bf16(acc[...])
-        source_ref[...] = bf16(source[...])
-        feed_sum.core_start(False)
-        feed_sum.first_start(False)
-        feed_sum.first_finish()
-        feed_sum.halves(half_a_ref, half_b_ref)
-        feed_sum.finish()
-        give.finish()
-
-
-def cross_backward(
-    n_dp, n, query, key_rows, value_rows, grad_out, mixed, sums, prefix, mine, states, shrink, expand, block=512
-):
+            dq_copy(step + 1).start()
+
+        return carry
+
+    lax.fori_loop(0, n, one_block, 0)
+    slots_ref[p.z] = blocks[p.z]
+    dk_ref[...] = bf16(key_acc[...] * factor)
+    dv_ref[...] = bf16(value_acc[...])
+    source_ref[:, :width] = bf16(dot(states_ref[...], dk_ref[...], TN))
+    source_ref[:, width:] = bf16(dot(states_ref[...], dv_ref[...], TN))
+    for later in range(2, n - 1):
+        give.step(later)
+    feed_sum.core_start(False)
+    feed_sum.first_start(False)
+    feed_sum.first_finish()
+    feed_sum.halves(half_a_ref, half_b_ref)
+    feed_sum.finish()
+    for distance in range(1, n):
+        dq_copy(distance).wait()
+    give.finish()
+
+
+def cross_backward(n_dp, n, query, key_rows, value_rows, grad_out, mixed, sums, mine, states, shrink, expand):
     total, width = query.shape
     keys, model = states.shape
     side = round((n_dp // 2) ** 0.5)
@@ -583,36 +595,11 @@
     by_place = lambda values: values.reshape(side, side, 2, rows, values.shape[1])
     low, wide = jnp.bfloat16, jnp.float32
     shape = jax.ShapeDtypeStruct
-    whole = pl.BlockSpec((total, width), lambda i, p: (0, 0))
-    part = pl.BlockSpec((block, width), lambda i, p: (i, 0))
+    dma = pltpu.SemaphoreType.DMA
     return pl.pallas_call(
         partial(cross_backward_kernel, n, side),
-        grid_spec=pltpu.PrefetchScalarGridSpec(
-            num_scalar_prefetch=1,
-            grid=(keys // block,),
-            in_specs=[
-                whole, part, part, whole, whole,
-                pl.BlockSpec((8, total), lambda i, p: (0, 0)),
-                pl.BlockSpec(mine.shape, lambda i, p: (0, 0)),
-                pl.BlockSpec((block, model), lambda i, p: (i, 0)),
-                ANYWHERE, ANYWHERE,
-            ],
-            out_specs=[
-                whole, part, part, ANYWHERE, pl.BlockSpec((model, 2 * width), lambda i, p: (0, 0)),
-                pl.BlockSpec(half, lambda i, p: (0, 0, 0)), pl.BlockSpec(half, lambda i, p: (0, 0, 0)),
-            ],
-            scratch_shapes=[
-                pltpu.VMEM((total, width), wide),
-                pltpu.VMEM((8, total), wide),
-                pltpu.VMEM((model, 2 * width), wide),
-                pltpu.VMEM((2, rows, columns), low),
-                pltpu.SemaphoreType.DMA,
-                *Give.sems(n),
-                *Reduce.scratch(side, rows, columns, 2, second=False),
-            ],
-        ),
         out_shape=[
-            shape((total, width), low),
+            shape((n, total // n, width), low),
             shape((keys, width), low),
             shape((keys, width), low),
             shape((n,) + mine.shape, low),
@@ -620,24 +607,35 @@
             shape(half, low),
             shape(half, low),
         ],
+        in_specs=[IN_VMEM] * 8 + [ANYWHERE] * 2,
+        out_specs=[IN_VMEM] * 3 + [ANYWHERE] + [IN_VMEM] * 3,
+        scratch_shapes=[
+            pltpu.VMEM((keys, width), low),
+            pltpu.VMEM((keys, width), wide),
+            pltpu.VMEM((keys, width), wide),
+            pltpu.VMEM((8, total), wide),
+            pltpu.VMEM((n, total // n, width), low),
+            pltpu.VMEM((2, rows, columns), low),
+            dma, dma((n - 1,)), dma((n - 1,)),
+            *Give.sems(n),
+            *Reduce.scratch(side, rows, columns, 2, second=False),
+        ],
         compiler_params=pltpu.CompilerParams(
             vmem_limit_bytes=VMEM_LIMIT, collective_id=6, has_side_effects=True
         ),
-        cost_estimate=pl.CostEstimate(
-            flops=40 * total * keys * width, bytes_accessed=4 * keys * width, transcendentals=0
-        ),
+        cost_estimate=pl.CostEstimate(flops=40 * total * keys * width, bytes_accessed=1 << 20, transcendentals=0),
         name="cross_backward",
     )(
-        prefix, query, key_rows, value_rows, grad_out, mixed, sums, mine, states,
-        by_place(shrink), by_place(expand),
+        query, key_rows, value_rows, grad_out, mixed, sums, mine, states, by_place(shrink), by_place(expand),
     )
 
 
 def front_kernel(
     n, side, prefix_ref, inner_ref, outer_ref, norm_ref, expand_ref, shrink_ref, x_ref,
-    near_ref, home_ref, later_ref, feed_ref, q_ref, k_ref, v_ref, mixed_ref, sums_ref,
-    block_near, block_line, block_norm, own_sems, near_send, near_recv, home_send, home_recv,
-    line_send, line_recv, far_send, far_recv,
+    near_ref, home_ref, feed_home_ref, q_ref, k_ref, v_ref, mixed_ref, sums_ref, slots_ref,
+    block_near, block_line, block_rest, own_sems, near_send, near_recv, home_send, home_recv,
+    line_send, line_recv, far_send, far_recv, mixed_send, mixed_recv,
+    block_feed, feed_send, feed_recv, rest_send, rest_recv,
 ):
     p = Place(n, side)
     width = inner_ref.shape[3]
@@ -646,57 +644,69 @@
         block_near[:, index * width : (index + 1) * width] = bf16(inner_ref[0, index])
     block_line[:, :width] = bf16(inner_ref[1, 0])
     block_line[:, width : 2 * width] = outer_ref[0]
-    block_norm[...] = norm_ref[...]
-    line_cols = pl.ds(pl.multiple_of(2 * width * p.z, 2 * width), 2 * width)
-    later_cols = pl.ds(pl.multiple_of(width * p.z, width), width)
+    for index in range(2):
+        block_rest[:, index * width : (index + 1) * width] = bf16(inner_ref[1, index + 1])
+    block_rest[:, 2 * width :] = norm_ref[...]
+    norms = block_rest.shape[1] - 2 * width
+    whole = n * width
+    later = whole + norms
+    out_cols = pl.ds(pl.multiple_of(p.z * width, width), width)
+    query_cols = pl.ds(pl.multiple_of(later + p.z * width, 128), width)
     spot = home_ref.at[p.y, p.x, p.core]
     near_ref[p.y, p.x, p.core] = block_near[...]
+    block_feed[:, :units] = bf16(expand_ref[...])
+    block_feed[:, units:] = shrink_ref[...]
+    feed_spot = feed_home_ref.at[p.y, p.x, p.core]
     own = [
-        pltpu.make_async_copy(block_line, spot.at[:, line_cols], own_sems.at[0]),
-        pltpu.make_async_copy(
-            block_norm, spot.at[:, pl.ds(2 * n * width, block_norm.shape[1])], own_sems.at[1]
-        ),
+        pltpu.make_async_copy(source, target, own_sems.at[index])
+        for index, (source, target) in enumerate(
+            (
+                (block_line.at[:, pl.ds(width, width)], spot.at[:, out_cols]),
+                (block_line.at[:, pl.ds(0, width)], spot.at[:, query_cols]),
+                (block_rest.at[:, pl.ds(2 * width, norms)], spot.at[:, pl.ds(whole, norms)]),
+                (block_rest.at[:, pl.ds(0, 2 * width)], spot.at[:, pl.ds(later + whole, 2 * width)]),
+                (block_feed, feed_spot.at[:, pl.ds(0, 2 * units)]),
+            )
+        )
     ]
     for copy in own:
         copy.start()
-    later_ref[:, later_cols] = outer_ref[1]
-    for index in range(2):
-        start = (n + index) * width
-        later_ref[:, start : start + width] = bf16(inner_ref[1, index + 1])
-    feed_ref[:, :units] = bf16(expand_ref[...])
-    feed_ref[:, 2 * units : 3 * units] = shrink_ref[...]
     greet(p.line() + p.plane())
     near = Spread(p, near_ref, near_send, near_recv)
-    rest = Spread(p, home_ref, home_send, home_recv)
+    first_rest = Spread(p, home_ref.at[:, :, :, :, pl.ds(0, later)], home_send, home_recv)
+    rest = Spread(
+        p, home_ref.at[:, :, :, :, pl.ds(later, whole + 2 * width)], rest_send, rest_recv
+    )
     near.first()
-    line = [
-        push(block_line, spot.at[:, line_cols], line_send.at[index], line_recv.at[index], other)
-        for index, other in enumerate(p.line())
+    lines = [
+        [
+            push(
+                block_line.at[:, pl.ds(first, width)], spot.at[:, cols],
+                line_send.at[part * (n - 1) + index], line_recv.at[part * (n - 1) + index], other,
+            )
+            for index, other in enumerate(p.line())
+        ]
+        for part, (first, cols) in enumerate(((width, out_cols), (0, query_cols)))
     ]
-    later = [
-        push(
-            later_ref.at[:, later_cols], later_ref.at[:, later_cols],
-            line_send.at[n - 1 + index], line_recv.at[n - 1 + index], other,
-        )
-        for index, other in enumerate(p.line())
-    ]
-    far = {"mp": lax.rem(p.z + n // 2, n)}
-    later += [
-        push(
-            feed_ref.at[:, pl.ds(2 * index * units, units)],
-            feed_ref.at[:, pl.ds((2 * index + 1) * units, units)],
-            far_send.at[index], far_recv.at[index], far,
-        )
-        for index in range(2)
-    ]
-    near.second()
-    near.core()
+    far = push(
+        block_feed.at[:, pl.ds(0, units)], feed_spot.at[:, pl.ds(2 * units, units)], far_send, far_recv,
+        {"mp": lax.rem(p.z + n // 2, n)},
+    )
     for copy in own:
         copy.wait()
-    for copy in line:
+    near.second()
+    feed_spread = Spread(
+        p, feed_home_ref.at[:, :, :, :, pl.ds(0, 2 * units)], feed_send, feed_recv
+    )
+    for copy in lines[0]:
+        copy.wait_recv()
+    first_rest.first()
+    near.core()
+    for copy in lines[1]:
         copy.wait_recv()
     rest.first()
     near.finish()
+    first_rest.second()
     model = x_ref.shape[1]
     weights = near_ref[...].reshape(model, 3 * width)
     for start in range(0, x_ref.shape[0], 256):
@@ -705,18 +715,45 @@
         for index, target in enumerate((q_ref, k_ref, v_ref)):
             target[rows, :] = made[:, index * width : (index + 1) * width]
     rest.second()
-    block = x_ref.shape[0] // 4
-    for index in range(4):
-        forward_rows(
-            True, index * block, block, prefix_ref, q_ref, k_ref, v_ref, mixed_ref, sums_ref
-        )
-        if index == 2:
-            rest.core()
+    feed_spread.first()
+    size = x_ref.shape[0] // n
+
+    def mixed_copy(distance):
+        to = lax.rem(p.z + distance, n)
+        return pltpu.make_async_remote_copy(
+            mixed_ref.at[rows_at(to, size)], slots_ref.at[p.z],
+            mixed_send.at[distance - 1], mixed_recv.at[distance - 1],
+            device_id={"mp": to}, device_id_type=MESH,
+        )
+
+    def attend(step, carry):
+        block = lax.rem(p.z + 1 + step, n)
+        for index in range(n):
+
+            @pl.when(block == index)
+            def _():
+                forward_rows(
+                    True, index * size, size, prefix_ref, q_ref, k_ref, v_ref, mixed_ref, sums_ref
+                )
+
+        @pl.when(step < n - 1)
+        def _():
+            mixed_copy(step + 1).start()
+
+        return carry
+
+    lax.fori_loop(0, n, attend, 0)
+    slots_ref[p.z] = mixed_ref[rows_at(p.z, size), :]
+    first_rest.core()
+    rest.core()
+    first_rest.finish()
     rest.finish()
-    for copy in line:
+    for distance in range(1, n):
+        mixed_copy(distance).wait()
+    for copy in (*lines[0], *lines[1]):
         copy.wait_send()
-    for copy in later:
-        copy.wait()
+    far.wait()
+    feed_spread.finish()
 
 
 def front(n_dp, n_mp, prefix, inner, outer_t, norm_t, expand, shrink_t, tokens):
@@ -724,7 +761,8 @@
     total = tokens.shape[0]
     side = round((n_dp // 2) ** 0.5)
     line = 2 * width
-    columns = n_mp * line + norm_t.shape[1]
+    columns = n_mp * line + 2 * width + norm_t.shape[1]
+    units = expand.shape[1]
     low = jnp.bfloat16
     dma = pltpu.SemaphoreType.DMA
     shape = jax.ShapeDtypeStruct
@@ -733,20 +771,23 @@
         out_shape=[
             shape((side, side, 2, rows, 3 * width), low),
             shape((side, side, 2, rows, columns), low),
-            shape((rows, (n_mp + 2) * width), low),
-            shape((rows, 4 * expand.shape[1]), low),
+            shape((side, side, 2, rows, 4 * units), low),
             *[shape((total, width), low)] * 4,
             shape((8, total), jnp.float32),
+            shape((n_mp, total // n_mp, width), low),
         ],
         in_specs=[pl.BlockSpec(memory_space=pltpu.SMEM)] + [IN_VMEM] * 6,
-        out_specs=[IN_VMEM, ANYWHERE] + [IN_VMEM] * 7,
+        out_specs=[IN_VMEM, ANYWHERE, ANYWHERE] + [IN_VMEM] * 6,
         scratch_shapes=[
             pltpu.VMEM((rows, 3 * width), low),
             pltpu.VMEM((rows, line), low),
-            pltpu.VMEM((rows, norm_t.shape[1]), low),
-            dma((2,)),
+            pltpu.VMEM((rows, 2 * width + norm_t.shape[1]), low),
+            dma((5,)),
             Spread.sems(side), Spread.sems(side), Spread.sems(side), Spread.sems(side),
-            dma((2 * n_mp - 2,)), dma((2 * n_mp - 2,)), dma((2,)), dma((2,)),
+            dma((2 * n_mp - 2,)), dma((2 * n_mp - 2,)), dma, dma,
+            dma((n_mp - 1,)), dma((n_mp - 1,)),
+            pltpu.VMEM((rows, 2 * units), low),
+            Spread.sems(side), Spread.sems(side), Spread.sems(side), Spread.sems(side),
         ],
         compiler_params=pltpu.CompilerParams(
             collective_id=0, has_side_effects=True, vmem_limit_bytes=VMEM_LIMIT
@@ -756,175 +797,176 @@
     )(prefix, inner, outer_t, norm_t, expand, shrink_t, tokens)
 
 
-def self_to_cross_kernel(
-    n, side, mixed_ref, bundle_ref, x_ref, feed_ref, later_ref,
-    hidden_ref, normed_ref, inverse_ref, slots_ref, norm_ref, q_ref, home_ref, rest_ref,
-    wo, wq, norm_columns, x_rows, blocks, wo_sems, wq_sems, x_sem, own_sem, send_in, recv_in, send_out, recv_out,
-    feed_block, later_block, block_sems, feed_send, feed_recv, later_send, later_recv, norm_sem,
+def middle_kernel(
+    n, side, slots_ref, bundle_ref, x_ref, home_in_ref, shrink_ref, outer_ref, states_ref,
+    hidden_ref, normed_ref, inverse_ref, norm_ref, q_ref, k_ref, v_ref, mixed_ref, sums_ref, cross_slots_ref,
+    home_ref, rest_ref,
+    wo, wq, norm_columns, source, x_rows, blocks,
+    wo_sems, wq_sems, load_sems, q_send, q_recv, mixed_send, mixed_recv, far_send, far_recv,
+    feed_send, feed_recv, later_send, later_recv, line_send, line_recv,
+    expand_send, expand_recv, shrink_send, shrink_recv,
 ):
     p = Place(n, side)
     me = p.z
     size = x_rows.shape[0]
-    width = mixed_ref.shape[1]
+    width = slots_ref.shape[2]
+    whole = n * width
+    norms = norm_columns.shape[1]
+    later = whole + norms
     loads = [
-        pltpu.make_async_copy(mixed_ref.at[rows_at(me, size)], slots_ref.at[me], own_sem),
-        pltpu.make_async_copy(x_ref.at[rows_at(me, size)], x_rows, x_sem),
+        pltpu.make_async_copy(x_ref.at[rows_at(me, size)], x_rows, load_sems.at[0]),
+        pltpu.make_async_copy(bundle_ref.at[:, pl.ds(whole, norms)], norm_columns, load_sems.at[1]),
         pltpu.make_async_copy(
-            bundle_ref.at[:, pl.ds(2 * n * width, norm_columns.shape[1])], norm_columns, norm_sem
+            bundle_ref.at[:, pl.ds(later + whole, 2 * width)], source, load_sems.at[2]
         ),
-        *load_groups(n, bundle_ref, 2 * width, width, width, wo, wo_sems),
-        *load_groups(n, bundle_ref, 2 * width, 0, width, wq, wq_sems),
+        *load_groups(n, bundle_ref, width, 0, width, wo, wo_sems),
+        *load_groups(n, bundle_ref, width, later, width, wq, wq_sems),
     ]
-    sources, blocks_here, homes = (later_ref, feed_ref), (later_block, feed_block), (rest_ref, home_ref)
-    block_loads = [
-        pltpu.make_async_copy(source, block, block_sems.at[index])
-        for index, (source, block) in enumerate(zip(sources, blocks_here))
+    for load in loads:
+        load.start()
+    units = home_ref.shape[4] // 4
+    spot = rest_ref.at[p.y, p.x, p.core, :, pl.ds(pl.multiple_of(width * me, width), width)]
+    greet(p.line() + p.plane())
+    store = pltpu.make_async_copy(outer_ref.at[1], spot, load_sems.at[3])
+    store.start()
+    line = [
+        push(outer_ref.at[1], spot, line_send.at[index], line_recv.at[index], other)
+        for index, other in enumerate(p.line())
     ]
-    for load in block_loads + loads:
-        load.start()
-    greet(p.line() + p.plane())
-    copies = heads_to_tokens(n, mixed_ref, slots_ref, send_in, recv_in)
-    for load in block_loads:
-        load.wait()
-    stores = [
-        pltpu.make_async_copy(block, home.at[p.y, p.x, p.core], block_sems.at[index])
-        for index, (block, home) in enumerate(zip(blocks_here, homes))
-    ]
-    for store in stores:
-        store.start()
+    part = lambda first, count: home_ref.at[:, :, :, :, pl.ds(first * units, count * units)]
     rest = Spread(p, rest_ref, later_send, later_recv)
-    spread = Spread(p, home_ref, feed_send, feed_recv)
-    for store in stores:
-        store.wait()
-    rest.first()
-    spread.first()
+    own_units = Spread(p, part(0, 2), feed_send, feed_recv)
+    far_expand = Spread(p, part(2, 1), expand_send, expand_recv)
+    far_shrink = Spread(p, part(3, 1), shrink_send, shrink_recv)
+    own_units.second()
+    far_expand.first()
+    store.wait()
     for load in loads:
         load.wait()
     norms = f32(norm_columns[...]).T[:8, :]
     norm_ref[...] = norms
-    branch = merge_heads(
-        n, slots_ref, copies, lambda part, group: dot(part, wo[group], NT), f32(x_rows[...])
-    )
-    rest.second()
+    branch = f32(x_rows[...])
+    for group in range(n):
+        branch = branch + dot(slots_ref[group], wo[group], NT)
     hidden, normed, inverse = layer_norm(branch, norms[0:1, :], norms[3:4, :])
     hidden_ref[...] = hidden
     normed_ref[...] = normed
     inverse_ref[...] = jnp.broadcast_to(inverse, inverse_ref.shape)
     low = bf16(hidden)
-    sent = tokens_to_heads(
-        n, lambda group: dot(low, wq[group]), blocks, q_ref, send_out, recv_out, own_sem
-    )
+
+    def q_copy(distance):
+        to = lax.rem(me + distance, n)
+        return pltpu.make_async_remote_copy(
+            blocks.at[to], q_ref.at[rows_at(me, size)], q_send.at[distance - 1], q_recv.at[distance - 1],
+            device_id={"mp": to}, device_id_type=MESH,
+        )
+
+    for distance in range(1, n):
+        to = lax.rem(me + distance, n)
+        blocks[to] = bf16(dot(low, wq[to]))
+        q_copy(distance).start()
+    far = push(
+        shrink_ref, home_ref.at[p.y, p.x, p.core, :, pl.ds(3 * units, units)], far_send, far_recv,
+        {"mp": lax.rem(me + n // 2, n)},
+    )
+    q_ref[rows_at(me, size), :] = bf16(dot(low, wq[me]))
+    for copy in line:
+        copy.wait_recv()
+    rest.first()
+    for start in range(0, states_ref.shape[0], 512):
+        rows = slice(start, start + 512)
+        made = bf16(dot(states_ref[rows, :], source[...]))
+        k_ref[rows, :] = made[:, :width]
+        v_ref[rows, :] = made[:, width:]
+    far_expand.second()
+
+    def mixed_copy(distance):
+        to = lax.rem(me + distance, n)
+        return pltpu.make_async_remote_copy(
+            mixed_ref.at[rows_at(to, size)], cross_slots_ref.at[me],
+            mixed_send.at[distance - 1], mixed_recv.at[distance - 1],
+            device_id={"mp": to}, device_id_type=MESH,
+        )
+
+    for step in range(n):
+        if step > 0:
+            q_copy(n - step).wait_recv()
+        forward_rows(
+            False, lax.rem(me + step, n), size, None, q_ref, k_ref, v_ref, mixed_ref, sums_ref
+        )
+        if step > 0:
+            mixed_copy(step).start()
+        if step == 0:
+            rest.second()
+    cross_slots_ref[me] = mixed_ref[rows_at(me, size), :]
+    far.wait_recv()
+    far_shrink.first()
     rest.core()
-    for copy in sent:
-        copy.wait()
-    rest.finish()
-    spread.finish()
-
-
-def self_to_cross(n_dp, n, mixed, bundle, tokens, feed_block, later_block):
+    far_shrink.second()
+    for distance in range(1, n):
+        q_copy(distance).wait_send()
+        mixed_copy(distance).wait()
+    for copy in line:
+        copy.wait_send()
+    far.wait_send()
+    for spread in (rest, own_units, far_expand, far_shrink):
+        spread.finish()
+
+
+def middle(n_dp, n, slots, bundle, tokens, home, shrink_t, outer_t, states):
     side = round((n_dp // 2) ** 0.5)
-    total, width = mixed.shape
-    size, model = total // n, tokens.shape[1]
+    _, size, width = slots.shape
+    total, model = tokens.shape
+    keys = states.shape[0]
     shape = jax.ShapeDtypeStruct
     dma = pltpu.SemaphoreType.DMA
+    low, wide = jnp.bfloat16, jnp.float32
     return pl.pallas_call(
-        partial(self_to_cross_kernel, n, side),
+        partial(middle_kernel, n, side),
         out_shape=[
-            shape((size, model), jnp.float32),
-            shape((size, model), jnp.float32),
-            shape((size, 128), jnp.float32),
-            shape((n, size, width), jnp.bfloat16),
-            shape((8, model), jnp.float32),
-            shape((total, width), jnp.bfloat16),
-            shape((side, side, 2) + feed_block.shape, jnp.bfloat16),
-            shape((side, side, 2) + later_block.shape, jnp.bfloat16),
+            shape((size, model), wide),
+            shape((size, model), wide),
+            shape((size, 128), wide),
+            shape((8, model), wide),
+            shape((total, width), low),
+            shape((keys, width), low),
+            shape((keys, width), low),
+            shape((total, width), low),
+            shape((8, total), wide),
+            shape((n, size, width), low),
+            shape(home.shape, low),
+            shape((side, side, 2, outer_t.shape[1], n * width), low),
         ],
-        in_specs=[ANYWHERE] * 5,
-        out_specs=[IN_VMEM] * 5 + [ANYWHERE] * 3,
+        in_specs=[IN_VMEM] + [ANYWHERE] * 3 + [IN_VMEM] * 3,
+        out_specs=[IN_VMEM] * 10 + [ANYWHERE] * 2,
+        input_output_aliases={3: 10},
         scratch_shapes=[
-            pltpu.VMEM((n, model, width), jnp.bfloat16),
-            pltpu.VMEM((n, model, width), jnp.bfloat16),
-            pltpu.VMEM((model, bundle.shape[1] - 2 * n * width), jnp.bfloat16),
-            pltpu.VMEM((size, model), jnp.bfloat16),
-            pltpu.VMEM((n, size, width), jnp.bfloat16),
-            dma((n,)), dma((n,)), dma, dma,
-            dma((n - 1,)), dma((n - 1,)), dma((n - 1,)), dma((n - 1,)),
-            pltpu.VMEM(feed_block.shape, jnp.bfloat16),
-            pltpu.VMEM(later_block.shape, jnp.bfloat16),
-            dma((2,)), Spread.sems(side), Spread.sems(side), Spread.sems(side), Spread.sems(side), dma,
+            pltpu.VMEM((n, model, width), low),
+            pltpu.VMEM((n, model, width), low),
+            pltpu.VMEM((model, bundle.shape[1] - 2 * n * width - 2 * width), low),
+            pltpu.VMEM((model, 2 * width), low),
+            pltpu.VMEM((size, model), low),
+            pltpu.VMEM((n, size, width), low),
+            dma((n,)), dma((n,)), dma((4,)),
+            dma((n - 1,)), dma((n - 1,)), dma((n - 1,)), dma((n - 1,)), dma, dma,
+            Spread.sems(side), Spread.sems(side), Spread.sems(side), Spread.sems(side),
+            dma((n - 1,)), dma((n - 1,)),
+            Spread.sems(side), Spread.sems(side), Spread.sems(side), Spread.sems(side),
         ],
         compiler_params=pltpu.CompilerParams(
             collective_id=1, has_side_effects=True, vmem_limit_bytes=VMEM_LIMIT
         ),
-        cost_estimate=pl.CostEstimate(
-            flops=10**9, bytes_accessed=8 * total * width, transcendentals=0
-        ),
-        name="self_to_cross",
-    )(mixed, bundle, tokens, feed_block, later_block)
-
-
-def cross_forward_kernel(
-    side, n, q_ref, states_ref, rest_ref, home_in_ref, k_ref, v_ref, mixed_ref, sums_ref, home_ref,
-    weights, weight_sem, feed_send, feed_recv,
-):
-    p = Place(n, side)
-    width = q_ref.shape[1]
-    load = pltpu.make_async_copy(
-        rest_ref.at[:, pl.ds(n * width, 2 * width)], weights, weight_sem
-    )
-    load.start()
-    greet(p.plane())
-    spread = Spread(p, home_ref, feed_send, feed_recv)
-    spread.second()
-    load.wait()
-    for start in range(0, states_ref.shape[0], 512):
-        rows = slice(start, start + 512)
-        made = bf16(dot(states_ref[rows, :], weights[...]))
-        k_ref[rows, :] = made[:, :width]
-        v_ref[rows, :] = made[:, width:]
-    block = q_ref.shape[0] // 2
-    for start in range(0, q_ref.shape[0], block):
-        forward_rows(False, start, block, None, q_ref, k_ref, v_ref, mixed_ref, sums_ref)
-    spread.finish()
-
-
-def cross_forward(n, query, states, rest, home):
-    total, width = query.shape
-    keys, model = states.shape
-    side = home.shape[0]
-    shape = jax.ShapeDtypeStruct
-    low = jnp.bfloat16
-    return pl.pallas_call(
-        partial(cross_forward_kernel, side, n),
-        out_shape=[
-            shape((keys, width), low),
-            shape((keys, width), low),
-            shape((total, width), low),
-            shape((8, total), jnp.float32),
-            shape(home.shape, low),
-        ],
-        in_specs=[IN_VMEM] * 2 + [ANYWHERE] * 2,
-        out_specs=[IN_VMEM] * 4 + [ANYWHERE],
-        input_output_aliases={3: 4},
-        scratch_shapes=[
-            pltpu.VMEM((model, 2 * width), low),
-            pltpu.SemaphoreType.DMA,
-            Spread.sems(side), Spread.sems(side),
-        ],
-        compiler_params=pltpu.CompilerParams(
-            collective_id=7, has_side_effects=True, vmem_limit_bytes=VMEM_LIMIT
-        ),
         cost_estimate=pl.CostEstimate(flops=10**10, bytes_accessed=1 << 20, transcendentals=0),
-        name="cross_forward",
-    )(query, states, rest, home)
+        name="middle",
+    )(slots, bundle, tokens, home, shrink_t, outer_t, states)
 
 
 def feed_kernel(
-    n, side, mixed_ref, rest_ref, home_ref, hidden_one_ref, cot_ref, norm_ref,
+    n, side, slots, rest_ref, home_ref, hidden_one_ref, cot_ref, norm_ref,
     out_ref, second_ref, dmix_ref, shrink_grad_ref, expand_grad_ref, wo_grad_ref, norm_grad_ref,
-    wo, weights, slots, hidden_two, normed_two, low_two, low_three, act, slope,
+    wo, weights, hidden_two, normed_two, low_two, low_three, act, slope,
     y_own, y_send, y_recv, d_send, d_recv, cot, blocks,
-    load_sems, wo_sems, own_sem, send_in, recv_in, send_out, recv_out, pair_send, pair_recv,
+    load_sem, wo_sems, own_sem, send_out, recv_out, pair_send, pair_recv,
     home_sems, home_send, home_recv,
 ):
     p = Place(n, side)
@@ -932,13 +974,12 @@
     mate = {"mp": me + 1 - 2 * lax.rem(me, 2)}
     size = cot.shape[0]
     half = size // 2
-    width = mixed_ref.shape[1]
+    width = slots.shape[2]
     hidden_units = act.shape[1]
     chunk = min(512, hidden_units)
     loads = [
-        pltpu.make_async_copy(mixed_ref.at[rows_at(me, size)], slots.at[me], load_sems.at[0]),
         *load_groups(n, rest_ref, width, 0, width, wo, wo_sems),
-        pltpu.make_async_copy(cot_ref.at[rows_at(me, size)], cot, load_sems.at[1]),
+        pltpu.make_async_copy(cot_ref.at[rows_at(me, size)], cot, load_sem),
     ]
     rows = home_ref.shape[3]
     places = [(y, x) for y in range(side) for x in range(side)]
@@ -950,7 +991,6 @@
     for load in loads + homes:
         load.start()
     greet(p.line() + [p.sibling()])
-    copies = heads_to_tokens(n, mixed_ref, slots, send_in, recv_in)
     home_copies = [
         push(
             home_ref.at[y, x, p.core], weights.at[spot],
@@ -958,16 +998,15 @@
         )
         for index, ((y, x), spot) in enumerate(zip(places, spots))
     ]
-    for load in loads[: n + 1]:
+    for load in loads[:n]:
         load.wait()
-    branch = merge_heads(
-        n, slots, copies, lambda part, group: dot(part, wo[group], NT), hidden_one_ref[...]
-    )
+    branch = hidden_one_ref[...]
+    for group in range(n):
+        branch = branch + dot(slots[group], wo[group], NT)
     hidden, normed, inverse_two = layer_norm(branch, norm_ref[1:2, :], norm_ref[4:5, :])
     hidden_two[...] = hidden
     normed_two[...] = normed
     low_two[:size, :] = bf16(hidden)
-    own, other = pl.ds(0, size), pl.ds(size, size)
     pair = []
 
     def to_mate(source, target):
@@ -975,18 +1014,40 @@
         pair.append(push(source, target, pair_send.at[index], pair_recv.at[index], mate))
         return pair[-1]
 
-    hidden_copy = to_mate(low_two.at[own], low_two.at[other])
+    hidden_copies = [
+        to_mate(low_two.at[pl.ds(start, half)], low_two.at[pl.ds(size + start, half)])
+        for start in (0, half)
+    ]
     for copy in homes:
         copy.wait()
     for copy in home_copies:
         copy.wait_recv()
-    expand = weights.at[:, pl.ds(0, hidden_units)]
-    shrink = weights.at[:, pl.ds(hidden_units, hidden_units)]
+    units = hidden_units // 2
+
+    def expand_cols(first, count):
+        first += first // units * units
+        return slice(first, first + count)
+
+    def shrink_cols(first, count):
+        first += (first // units + 1) * units
+        return slice(first, first + count)
+
+    def shrink_sum(rows):
+        return sum(
+            dot(act[rows, first : first + units], weights[:, shrink_cols(first, units)], NT)
+            for first in (0, units)
+        )
+
+    def expand_sum(rows):
+        return sum(
+            dot(slope[rows, first : first + units], weights[:, expand_cols(first, units)], NT)
+            for first in (0, units)
+        )
 
     def expand_rows(start, count):
         rows = low_two[start : start + count, :]
         for first in range(0, hidden_units, chunk):
-            pre = dot(rows, expand[:, first : first + chunk])
+            pre = dot(rows, weights[:, expand_cols(first, chunk)])
             cdf = 0.5 + 0.5 * lax.erf(pre * 0.7071067811865476)
             act[start : start + count, first : first + chunk] = bf16(pre * cdf)
             slope[start : start + count, first : first + chunk] = bf16(
@@ -994,43 +1055,42 @@
             )
 
     expand_rows(0, size)
-    hidden_copy.wait_recv()
     y_copies = []
-    for start in (0, half):
+    for index, start in enumerate((0, half)):
+        hidden_copies[index].wait_recv()
         expand_rows(size + start, half)
-        y_send[start : start + half, :] = bf16(
-            dot(act[size + start : size + start + half, :], shrink[...], NT)
-        )
+        y_send[start : start + half, :] = bf16(shrink_sum(slice(size + start, size + start + half)))
         y_copies.append(to_mate(y_send.at[pl.ds(start, half)], y_recv.at[pl.ds(start, half)]))
-    y_own[...] = dot(act[:size, :], shrink[...], NT)
+    y_own[...] = shrink_sum(slice(0, size))
     for copy in y_copies:
         copy.wait_recv()
     output, normed, inverse = layer_norm(
         hidden_two[...] + y_own[...] + f32(y_recv[...]), norm_ref[2:3, :], norm_ref[5:6, :]
     )
     out_ref[...] = bf16(output)
-    loads[n + 1].wait()
+    loads[n].wait()
     third, gain_three, bias_three = norm_back(f32(cot[...]), normed, inverse, norm_ref[2:3, :])
     low_three[:size, :] = bf16(third)
-    grad_copy = to_mate(low_three.at[own], low_three.at[other])
+    grad_copies = [
+        to_mate(low_three.at[pl.ds(start, half)], low_three.at[pl.ds(size + start, half)])
+        for start in (0, half)
+    ]
 
     def back_rows(start, count):
         rows = low_three[start : start + count, :]
         for first in range(0, hidden_units, chunk):
-            grad = dot(rows, shrink[:, first : first + chunk])
+            grad = dot(rows, weights[:, shrink_cols(first, chunk)])
             spot = (slice(start, start + count), slice(first, first + chunk))
             slope[spot] = bf16(grad * f32(slope[spot]))
 
     back_rows(0, size)
-    grad_copy.wait_recv()
     d_copies = []
-    for start in (0, half):
+    for index, start in enumerate((0, half)):
+        grad_copies[index].wait_recv()
         back_rows(size + start, half)
-        d_send[start : start + half, :] = bf16(
-            dot(slope[size + start : size + start + half, :], expand[...], NT)
-        )
+        d_send[start : start + half, :] = bf16(expand_sum(slice(size + start, size + start + half)))
         d_copies.append(to_mate(d_send.at[pl.ds(start, half)], d_recv.at[pl.ds(start, half)]))
-    y_own[...] = third + dot(slope[:size, :], expand[...], NT)
+    y_own[...] = third + expand_sum(slice(0, size))
     for copy in d_copies:
         copy.wait_recv()
     second, gain_two, bias_two = norm_back(
@@ -1056,8 +1116,9 @@
         copy.wait_send()
 
 
-def feed(n, mixed, rest, home, hidden_one, cotangent, norms):
-    total, width = mixed.shape
+def feed(n, slots, rest, home, hidden_one, cotangent, norms):
+    width = slots.shape[2]
+    total = cotangent.shape[0]
     side, model, units = home.shape[0], hidden_one.shape[1], home.shape[4] // 2
     size = total // n
     shape = jax.ShapeDtypeStruct
@@ -1074,12 +1135,11 @@
             shape((model, model), low),
             shape((8, model), wide),
         ],
-        in_specs=[ANYWHERE] * 3 + [IN_VMEM, ANYWHERE, IN_VMEM],
+        in_specs=[IN_VMEM, ANYWHERE, ANYWHERE, IN_VMEM, ANYWHERE, IN_VMEM],
         out_specs=[IN_VMEM] * 2 + [ANYWHERE] + [IN_VMEM] * 4,
         scratch_shapes=[
             pltpu.VMEM((n, model, width), low),
             pltpu.VMEM((model, 2 * units), low),
-            pltpu.VMEM((n, size, width), low),
             pltpu.VMEM((size, model), wide),
             pltpu.VMEM((size, model), wide),
             pltpu.VMEM((2 * size, model), low),
@@ -1093,9 +1153,9 @@
             pltpu.VMEM((size, model), low),
             pltpu.VMEM((size, model), low),
             pltpu.VMEM((n, size, width), low),
-            dma((2,)), dma((n,)), dma,
-            dma((n - 1,)), dma((n - 1,)), dma((n - 1,)), dma((n - 1,)),
-            dma((6,)), dma((6,)),
+            dma, dma((n,)), dma,
+            dma((n - 1,)), dma((n - 1,)),
+            dma((8,)), dma((8,)),
             dma((side * side,)), dma((side * side,)), dma((side * side,)),
         ],
         compiler_params=pltpu.CompilerParams(
@@ -1105,95 +1165,68 @@
             flops=80 * 10**9, bytes_accessed=8 * total * width, transcendentals=0
         ),
         name="feed",
-    )(mixed, rest, home, hidden_one, cotangent, norms)
-
-
-def cross_to_self_kernel(
-    n, side, dq_ref, bundle_ref, second_ref, hidden_ref, normed_ref, inverse_ref, mixed_ref, gain_ref, norm_ref,
-    half_a_ref, half_b_ref, first_ref, dmix_ref, weight_grad_ref, norm_grad_ref, feed_ref,
-    wo, wq, slots, blocks, wo_sems, wq_sems, own_sem, send_in, recv_in, send_out, recv_out, *scratch,
-):
-    p = Place(n, side)
-    halves = Halves(p, half_a_ref, half_b_ref, scratch)
-    me = p.z
-    size, model = second_ref.shape
-    width = dq_ref.shape[1]
-    loads = [
-        pltpu.make_async_copy(dq_ref.at[rows_at(me, size)], slots.at[me], own_sem),
-        *load_groups(n, bundle_ref, 2 * width, 0, width, wq, wq_sems),
-        *load_groups(n, bundle_ref, 2 * width, width, width, wo, wo_sems),
-    ]
-    for load in loads:
-        load.start()
-    greet(p.line() + p.plane())
-    copies = heads_to_tokens(n, dq_ref, slots, send_in, recv_in)
-    halves.start()
-    for load in loads:
-        load.wait()
-    upstream = merge_heads(
-        n, slots, copies, lambda part, group: dot(part, wq[group], NT), second_ref[...]
-    )
-    first, gain_one, bias_one = norm_back(
-        upstream, normed_ref[...], inverse_ref[:, 0:1], gain_ref[0:1, :]
-    )
-    first_ref[...] = first
-    low = bf16(first)
-    sent = tokens_to_heads(
-        n, lambda group: dot(low, wo[group]), blocks, dmix_ref, send_out, recv_out, own_sem
-    )
-    hidden_low = bf16(hidden_ref[...])
-    for group in range(n):
-        cols = 2 * group * width
-        weight_grad_ref[:, cols : cols + width] = bf16(dot(hidden_low, slots[group], TN))
-        weight_grad_ref[:, cols + width : cols + 2 * width] = bf16(dot(low, mixed_ref[group], TN))
-    rows = jnp.concatenate(
-        [
-            gain_one, norm_ref[0:2, :], bias_one, norm_ref[2:4, :],
-            jnp.zeros((122, model), jnp.float32),
-        ],
-        axis=0,
-    )
-    norm_grad_ref[...] = bf16(rows.T)
-    feed_ref[...] = bf16(halves.total())
-    for copy in sent:
-        copy.wait()
-
-
-def cross_to_self(n_dp, n, dq, bundle, second, hidden, normed, inverse, slots, gains, norm_rows, halves):
-    side = round((n_dp // 2) ** 0.5)
-    half, columns = halves[0].shape[1:]
-    total, width = dq.shape
-    size, model = second.shape
-    shape = jax.ShapeDtypeStruct
-    dma = pltpu.SemaphoreType.DMA
-    return pl.pallas_call(
-        partial(cross_to_self_kernel, n, side),
-        out_shape=[
-            shape((size, model), jnp.float32),
-            shape((total, width), jnp.bfloat16),
-            shape((model, 2 * model), jnp.bfloat16),
-            shape((model, 128), jnp.bfloat16),
-            shape((2 * half, columns), jnp.bfloat16),
-        ],
-        in_specs=[ANYWHERE] * 2 + [IN_VMEM] * 9,
-        out_specs=[IN_VMEM, ANYWHERE, IN_VMEM, IN_VMEM, IN_VMEM],
-        scratch_shapes=[
-            pltpu.VMEM((n, model, width), jnp.bfloat16),
-            pltpu.VMEM((n, model, width), jnp.bfloat16),
-            pltpu.VMEM((n, size, width), jnp.bfloat16),
-            pltpu.VMEM((n, size, width), jnp.bfloat16),
-            dma((n,)), dma((n,)), dma,
-            dma((n - 1,)), dma((n - 1,)), dma((n - 1,)), dma((n - 1,)),
-            *Halves.scratch(side, half, columns),
-        ],
-        compiler_params=pltpu.CompilerParams(
-            collective_id=3, has_side_effects=True, vmem_limit_bytes=VMEM_LIMIT
-        ),
-        cost_estimate=pl.CostEstimate(
-            flops=10**9, bytes_accessed=8 * total * width, transcendentals=0
-        ),
-        name="cross_to_self",
-    )(dq, bundle, second, hidden, normed, inverse, slots, gains, norm_rows, *halves)
+    )(slots, rest, home, hidden_one, cotangent, norms)
+
+
+class Line:
+    def __init__(self, place, parts, scratch):
+        self.n, self.me, self.parts = place.n, place.z, parts
+        self.landed = {"right": scratch[0], "left": scratch[1]}
+        self.sems = {"right": scratch[2:4], "left": scratch[4:6]}
+
+    @staticmethod
+    def scratch(n, rows, columns):
+        return [pltpu.VMEM((n - 1, rows, columns), jnp.bfloat16)] * 2 + [
+            pltpu.SemaphoreType.DMA((n - 1,))
+        ] * 4
+
+    def _spots(self):
+        return (("right", self.me, self.me + 1), ("left", self.n - 1 - self.me, self.me - 1))
+
+    def _copy(self, way, spot, to, step):
+        n = self.n
+        chunk = n - 1 - step + spot if way == "right" else step - spot
+        return pltpu.make_async_remote_copy(
+            self.parts.at[lax.rem(chunk + n, n)], self.landed[way].at[step],
+            self.sems[way][0].at[step], self.sems[way][1].at[step],
+            device_id={"mp": lax.rem(to + n, n)}, device_id_type=MESH,
+        )
+
+    def step(self, step):
+        n = self.n
+        for way, spot, to in self._spots():
+            chunk = n - 1 - step + spot if way == "right" else step - spot
+            chunk = lax.rem(chunk + n, n)
+
+            if step > 0:
+
+                @pl.when((spot > 0) & (spot <= step) & (spot < n - 1))
+                def _():
+                    self._copy(way, spot, to, step - 1).wait_recv()
+                    self.parts[chunk] = bf16(
+                        f32(self.parts[chunk]) + f32(self.landed[way][step - 1])
+                    )
+
+            @pl.when((spot <= step) & (spot < n - 1))
+            def _():
+                self._copy(way, spot, to, step).start()
+
+    def finish(self):
+        last = self.n - 2
+        for way, spot, to in self._spots():
+
+            @pl.when(spot > 0)
+            def _():
+                self._copy(way, spot, to, last).wait_recv()
+                self.parts[self.me] = bf16(
+                    f32(self.parts[self.me]) + f32(self.landed[way][last])
+                )
+
+            for step in range(self.n - 1):
+
+                @pl.when((spot <= step) & (spot < self.n - 1))
+                def _():
+                    self._copy(way, spot, to, step).wait_send()
 
 
 class Fold:
@@ -1479,16 +1512,16 @@
 
 
 def finish_kernel(
-    n, side, units, width, prefix_ref, q_ref, k_ref, v_ref, do_ref, o_ref, row_sums_ref,
-    near_ref, x_ref, first_ref, cross_dk_ref, cross_dv_ref, rest_ref,
-    feed_ref, cross_wo_ref, weight_ref, norm_ref, source_grad_ref, *refs,
+    n, side, units, width, prefix_ref, q_ref, k_ref, v_ref, o_ref, row_sums_ref,
+    near_ref, x_ref, cross_dk_ref, cross_dv_ref, dq_slots_ref, mixed_slots_ref, inverse_ref, norms_ref, norm_rows_ref,
+    half_a_ref, half_b_ref, bundle_ref, second_hbm, hidden_hbm, normed_hbm, cross_wo_ref, source_grad_ref, *refs,
 ):
     states, refs = refs[:15], refs[15:]
     out_ref, sums_ref, grads, refs = refs[0], refs[1], refs[2:7], refs[7:]
     (
-        source_ref, source_sem, dq_ref, dk_ref, dv_ref, query_acc, delta, master_sems, inner, stage, far_recv, group_send, group_recv,
-        far_send_sem, far_recv_sem, group_send_sems, group_recv_sems,
-        mine, slots, everyone_send, everyone_recv, *scratch,
+        source_ref, source_sem, do_ref, first_ref, feed_ref, weight_ref, blocks, early_sems, group_sem,
+        own_sem, send_out, recv_out, dq_ref, dk_ref, dv_ref, query_acc, delta, master_sems, inner, stage, far_recv, group_send,
+        far_send_sem, far_recv_sem, mine, slots, everyone_send, everyone_recv, *scratch,
     ) = refs
     n_dp = 2 * side * side
     p = Place(n, side)
@@ -1505,8 +1538,9 @@
     def make(flow, group):
         if group < source_groups:
             spot = pl.ds((flow * source_groups + group) * group_rows, group_rows)
-            return dot(cross_dk_ref[spot, :], source_ref[:, :width], NT) + dot(
-                cross_dv_ref[spot, :], source_ref[:, width:], NT
+            made = source_ref[...].reshape(model, 2 * width)
+            return dot(cross_dk_ref[spot, :], made[:, :width], NT) + dot(
+                cross_dv_ref[spot, :], made[:, width:], NT
             )
         tokens = x_ref.shape[0]
         start = flow * (tokens // 2) + (group - source_groups) * group_rows
@@ -1518,15 +1552,93 @@
         return total + jnp.where(me == start // size, here, 0.0)
 
     fold = Fold(p, make, out_ref, scratch[:7], per_group)
-    group_sum = Reduce(p, [cross_wo_ref, weight_ref, norm_ref, source_grad_ref], scratch[7:15])
-    inner_sum = Reduce(p, [inner], scratch[15:23])
+    group_sum = Reduce(p, [cross_wo_ref, source_grad_ref], scratch[7:15])
+    weight_sum = Reduce(p, [weight_ref], scratch[15:23])
+    inner_sum = Reduce(p, [inner], scratch[23:31])
+    halves = Halves(p, half_a_ref, half_b_ref, scratch[31:35])
+    line = Line(p, group_send, scratch[35:])
 
     source_load = pltpu.make_async_copy(
-        rest_ref.at[:, pl.ds(n * width, 2 * width)], source_ref, source_sem
+        bundle_ref.at[:, :, :, :, pl.ds(2 * n * width + 128, 2 * width)], source_ref, source_sem
     )
     source_load.start()
+    weight_loads = [
+        pltpu.make_async_copy(
+            bundle_ref.at[:, :, :, :, pl.ds(start, n * width)],
+            weight_ref.at[:, :, :, :, pl.ds(index * n * width, n * width)], group_sem.at[index],
+        )
+        for index, start in enumerate((n * width + 128, 0))
+    ]
+    for load in weight_loads:
+        load.start()
     everyone.greet()
     group_sum.core_start()
+    halves.start()
+    source_load.wait()
+    ticks = iter(range(fold.ticks))
+
+    def advance(count):
+        for _ in range(count):
+            fold.tick(next(ticks))
+
+    advance(2)
+
+    def store_by_place(target, first, columns, value, start):
+        for row in range(0, value.shape[0], rows):
+            flat = (start + row) // rows
+            y, x, core = flat // (2 * side), flat // 2 % side, flat % 2
+            target[y, x, core, :, first : first + columns] = value[row : row + rows]
+
+    def held_weight(group, second):
+        cols = pl.ds(pl.multiple_of((n * second + group) * width, width), width)
+        return weight_ref[:, :, :, :, cols].reshape(model, width)
+
+    def cross_to_self(rows_f32):
+        second_load = pltpu.make_async_copy(second_hbm, first_ref, early_sems.at[0])
+        normed_load = pltpu.make_async_copy(normed_hbm, rows_f32, early_sems.at[1])
+        hidden_load = pltpu.make_async_copy(hidden_hbm, rows_f32, early_sems.at[2])
+        second_load.start()
+        normed_load.start()
+        second_load.wait()
+        for load in weight_loads:
+            load.wait()
+        upstream = first_ref[...]
+        for group in range(n):
+            upstream = upstream + dot(dq_slots_ref[group], held_weight(group, 0), NT)
+        normed_load.wait()
+        first, gain_one, bias_one = norm_back(
+            upstream, rows_f32[...], inverse_ref[:, 0:1], norms_ref[0:1, :]
+        )
+        hidden_load.start()
+        first_ref[...] = first
+        low = bf16(first)
+        sent = tokens_to_heads(
+            n, lambda group: dot(low, held_weight(group, 1)), blocks, do_ref, send_out, recv_out, own_sem
+        )
+        advance(1)
+        hidden_load.wait()
+        hidden_low = bf16(rows_f32[...])
+        for group in range(n):
+            at = 2 * group * width
+            store_by_place(weight_ref, at, width, bf16(dot(hidden_low, dq_slots_ref[group], TN)), 0)
+            store_by_place(
+                weight_ref, at + width, width, bf16(dot(low, mixed_slots_ref[group], TN)), 0
+            )
+        rows_all = jnp.concatenate(
+            [
+                gain_one, norm_rows_ref[0:2, :], bias_one, norm_rows_ref[2:4, :],
+                jnp.zeros((122, model), jnp.float32),
+            ],
+            axis=0,
+        )
+        store_by_place(weight_ref, 2 * n * width, 128, bf16(rows_all.T), 0)
+        advance(1)
+        for copy in sent:
+            copy.wait()
+
+    pl.run_scoped(cross_to_self, pltpu.VMEM((size, model), jnp.float32))
+    weight_sum.core_start()
+    feed_ref[...] = bf16(halves.total())
     far = {"mp": lax.rem(me + n // 2, n)}
     far_copies = [
         push(
@@ -1536,15 +1648,11 @@
         )
         for index in range(2)
     ]
-
-    source_load.wait()
-    ticks = iter(range(fold.ticks))
-
-    def advance(count):
-        for _ in range(count):
-            fold.tick(next(ticks))
-
+    group_sum.core_finish(stage)
+    group_sum.first_start()
     advance(1)
+    weight_sum.core_finish(stage)
+    weight_sum.first_start()
     backward_delta(do_ref, o_ref, delta)
     query_acc[...] = jnp.zeros_like(query_acc)
     key_block = 256
@@ -1555,9 +1663,6 @@
             query_acc, dk_ref, dv_ref,
         )
 
-    advance(1)
-    group_sum.core_finish(stage)
-    group_sum.first_start()
     for index in range(x_ref.shape[0] // key_block):
         for heads in ((0, 1), (2, 3)):
             self_backward(index, heads)
@@ -1568,11 +1673,7 @@
     for start in range(0, model, per):
         turned = x_ref[:, start : start + per]
         for index, own in enumerate(own_heads):
-            block = bf16(dot(turned, own[...], TN))
-            for row in range(0, per, rows):
-                flat = (start + row) // rows
-                y, x, core = flat // (2 * side), flat // 2 % side, flat % 2
-                inner[y, x, core, :, index * width : (index + 1) * width] = block[row : row + rows]
+            store_by_place(inner, index * width, width, bf16(dot(turned, own[...], TN)), start)
     inner_sum.core_start()
     advance(1)
     inner_sum.core_finish(stage)
@@ -1580,33 +1681,28 @@
     advance(2)
     group_sum.first_finish()
     group_sum.second_start()
+    weight_sum.first_finish()
+    weight_sum.second_start()
     advance(1)
     advance(1)
     inner_sum.first_finish()
     inner_sum.second_start()
     advance(1)
     group_sum.second_wait()
+    weight_sum.second_wait()
     whole = n * width
     for group in range(n):
         group_send[group, :, :width] = bf16(
             group_sum.total(slice(group * width, (group + 1) * width))
         )
-        start = whole + 2 * group * width
+        start = 2 * group * width
         group_send[group, :, width : 3 * width] = bf16(
-            group_sum.total(slice(start, start + 2 * width))
+            weight_sum.total(slice(start, start + 2 * width))
         )
         group_send[group, :, 3 * width :] = bf16(
-            group_sum.total(slice(3 * whole, 3 * whole + norm_ref.shape[4]))
-        )
-    group_copies = []
-    for distance in range(1, n):
-        to = lax.rem(me + distance, n)
-        group_copies.append(
-            push(
-                group_send.at[to], group_recv.at[distance - 1],
-                group_send_sems.at[distance - 1], group_recv_sems.at[distance - 1], {"mp": to},
-            )
-        )
+            weight_sum.total(slice(2 * whole, 2 * whole + 128))
+        )
+    line.step(0)
     advance(2)
 
     def optimizer_sums(*masters):
@@ -1620,11 +1716,12 @@
         inner_sum.second_wait()
         for index in range(3):
             grad_inner[0, index] = inner_sum.total(slice(index * width, (index + 1) * width))
-        start = 3 * whole + norm_ref.shape[4]
+        start = whole
         for index in range(2):
             grad_inner[1, index + 1] = group_sum.total(
                 slice(start + index * width, start + (index + 1) * width)
             )
+        line.step(1)
         for load in master_loads:
             load.wait()
         weights, firsts, seconds = (tensors(*masters[index : index + 5]) for index in (0, 5, 10))
@@ -1632,21 +1729,18 @@
         mine[...] = jnp.zeros(mine.shape, jnp.float32)
         mine[0:1, :] = square_row([ref[...] * ref[...] for ref, _ in weights], share)
         advance(2)
+        line.step(2)
         for copy in far_copies:
             copy.wait_recv()
         grad_shrink[...] = (f32(feed_ref[:, :units]) + f32(far_recv[:, :units])).T
         grad_expand[...] = f32(feed_ref[:, 2 * units : 3 * units]) + f32(far_recv[:, units:])
         advance(2)
-        for distance in range(1, n):
-            group_copies[distance - 1].wait_recv()
-        received = lambda cols: sum(
-            [f32(group_recv[distance - 1, :, cols]) for distance in range(1, n)],
-            f32(group_send[me, :, cols]),
-        )
+        line.finish()
+        received = lambda cols: f32(group_send[me, :, cols])
         grad_outer[1] = received(slice(0, width)).T
         grad_inner[1, 0] = received(slice(width, 2 * width))
         grad_outer[0] = received(slice(2 * width, 3 * width)).T
-        grad_norms[...] = received(slice(3 * width, 3 * width + norm_ref.shape[4])).T[:6, :]
+        grad_norms[...] = received(slice(3 * width, 3 * width + 128)).T[:6, :]
 
         def direction_square(grad, first, second, weight):
             step = moments(grad[0][...], first[0][...], second[0][...], weight[0][...], weight[1])[2]
@@ -1663,68 +1757,77 @@
     for tick in ticks:
         fold.tick(tick)
     fold.finish()
-    for copy in (*far_copies, *group_copies):
+    for copy in far_copies:
         copy.wait_send()
-    for batch in (group_sum, inner_sum):
+    for batch in (group_sum, weight_sum, inner_sum):
         batch.finish()
 
 
 def finish(
-    n_dp, n_mp, prefix, projections, grad_out, mixed, row_sums, near, tokens, first,
-    source_heads, rest, feed_grad, cross_wo, weights, norms, source_grad, states,
+    n_dp, n_mp, prefix, projections, mixed, row_sums, near, tokens, source_heads, dq_slots, mixed_slots,
+    inverse, norms, norm_rows, halves, bundle, second, hidden, normed, cross_wo, source_grad, states,
 ):
     side = round((n_dp // 2) ** 0.5)
     total, width = mixed.shape
-    size, model = first.shape
-    units = feed_grad.shape[1] // 4
+    size, model = second.shape
     rows = model // n_dp
+    half, feed_columns = halves[0].shape[1:]
+    units = feed_columns // 4
     low, wide = jnp.bfloat16, jnp.float32
     shape = jax.ShapeDtypeStruct
     dma = pltpu.SemaphoreType.DMA
     by_place = lambda values: values.reshape(side, side, 2, rows, values.shape[1])
-    early = [by_place(values) for values in (cross_wo, weights, norms, source_grad)]
+    early = [by_place(values) for values in (cross_wo, source_grad)]
     columns = sum(values.shape[4] for values in early)
-    bundle = 3 * width + norms.shape[1]
+    group_bundle = 3 * width + 128
     devices = n_dp * n_mp
     chunk_rows = 64
     chunks = (total + source_heads[0].shape[0]) // (2 * chunk_rows)
+    weight_columns = 2 * n_mp * width + 128
     both, sums, *grads = pl.pallas_call(
         partial(finish_kernel, n_mp, side, units, width),
         out_shape=[shape((2, chunks, chunk_rows, model), low), shape((8, 128), wide)]
         + [shape(values.shape, wide) for values in states[:5]],
         in_specs=[pl.BlockSpec(memory_space=pltpu.SMEM)]
-        + [IN_VMEM] * 11
-        + [ANYWHERE, IN_VMEM]
-        + [ANYWHERE] * (4 + len(states)),
+        + [IN_VMEM] * 16
+        + [ANYWHERE] * (6 + len(states)),
         out_specs=[ANYWHERE] + [IN_VMEM] * 6,
         scratch_shapes=[
-            pltpu.VMEM((model, 2 * width), low),
+            pltpu.VMEM((side, side, 2, rows, 2 * width), low),
             dma,
+            pltpu.VMEM((total, width), low),
+            pltpu.VMEM((size, model), wide),
+            pltpu.VMEM((rows, feed_columns), low),
+            pltpu.VMEM((side, side, 2, rows, weight_columns), low),
+            pltpu.VMEM((n_mp, size, width), low),
+            dma((3,)), dma((2,)), dma, dma((n_mp - 1,)), dma((n_mp - 1,)),
             *[pltpu.VMEM((total, width), low)] * 3,
             pltpu.VMEM((total, width), wide),
             pltpu.VMEM((8, total), wide),
             dma((len(states),)),
             pltpu.VMEM((side, side, 2, rows, 3 * width), low),
-            pltpu.VMEM((2, rows, columns), low),
+            pltpu.VMEM((2, rows, max(columns, weight_columns)), low),
             pltpu.VMEM((rows, 2 * units), low),
-            pltpu.VMEM((n_mp, rows, bundle), low),
-            pltpu.VMEM((n_mp - 1, rows, bundle), low),
-            dma((2,)), dma((2,)), dma((n_mp - 1,)), dma((n_mp - 1,)),
+            pltpu.VMEM((n_mp, rows, group_bundle), low),
+            dma((2,)), dma((2,)),
             pltpu.VMEM((8, 128), wide),
             pltpu.VMEM((devices, 8, 128), wide),
             dma((devices - 1,)), dma((devices - 1,)),
             *Fold.scratch(chunks, chunk_rows, model),
-            *Reduce.scratch(side, rows, columns, 4),
+            *Reduce.scratch(side, rows, columns, 2),
+            *Reduce.scratch(side, rows, weight_columns, 1),
             *Reduce.scratch(side, rows, 3 * width, 1),
+            *Halves.scratch(side, half, feed_columns),
+            *Line.scratch(n_mp, rows, group_bundle),
         ],
         compiler_params=pltpu.CompilerParams(
             collective_id=5, has_side_effects=True, vmem_limit_bytes=VMEM_LIMIT
         ),
-        cost_estimate=pl.CostEstimate(flops=10**9, bytes_accessed=1 << 20, transcendentals=0),
+        cost_estimate=pl.CostEstimate(flops=10**10, bytes_accessed=1 << 20, transcendentals=0),
         name="finish",
     )(
-        prefix, *projections, grad_out, mixed, row_sums, near, tokens, first, *source_heads,
-        rest, feed_grad, *early, *states,
+        prefix, *projections, mixed, row_sums, near, tokens, *source_heads, dq_slots, mixed_slots, inverse,
+        norms, norm_rows, *halves, by_place(bundle), second, hidden, normed, *early, *states,
     )
     return both, sums, grads
 
@@ -1758,39 +1861,33 @@
     units = expand_weights.shape[1]
 
     norm_t = jnp.pad(bf16(norm_params).reshape(6, rows).T, ((0, 0), (0, 122)))
-    near, bundle, later_block, feed_block, self_q, self_k, self_v, self_mixed, self_sums = front(
-        n_dp, n_mp, prefix, inner_weights, bf16(jnp.swapaxes(outer_weights, 1, 2)), norm_t,
-        expand_weights, bf16(shrink_weights.T), tokens,
+    outer_t = bf16(jnp.swapaxes(outer_weights, 1, 2))
+    shrink_t = bf16(shrink_weights.T)
+    near, bundle, home, self_q, self_k, self_v, self_mixed, self_sums, self_slots = front(
+        n_dp, n_mp, prefix, inner_weights, outer_t, norm_t, expand_weights, shrink_t, tokens
     )
     by_rows = lambda values: values.reshape(model, values.shape[-1])
     near, bundle = by_rows(near), by_rows(bundle)
-    hidden_one, normed_one, inverse_one, self_slots, norms, cross_query, home, rest = self_to_cross(
-        n_dp, n_mp, self_mixed, bundle, tokens, feed_block, later_block
-    )
+    (
+        hidden_one, normed_one, inverse_one, norms, cross_query, cross_k, cross_v, cross_mixed,
+        cross_sums, cross_slots, home, rest,
+    ) = middle(n_dp, n_mp, self_slots, bundle, tokens, home, shrink_t, outer_t, states)
     rest = by_rows(rest)
-    cross_k, cross_v, cross_mixed, cross_sums, home = cross_forward(
-        n_mp, cross_query, states, rest, home
-    )
     out_rows, grad_second, cross_dmix, shrink_grad, expand_grad, cross_wo_grad, norm_rows = feed(
-        n_mp, cross_mixed, rest, home, hidden_one, cotangent.reshape(seq_len, model), norms,
-    )
-    cross_dq, cross_dk, cross_dv, layer_low, source_grad, *halves = cross_backward(
-        n_dp, n_mp, cross_query, cross_k, cross_v, cross_dmix, cross_mixed, cross_sums, prefix, out_rows,
-        states, shrink_grad, expand_grad,
-    )
-    grad_first, self_dmix, weight_grad, norm_grad, feed_grad = cross_to_self(
-        n_dp, n_mp, cross_dq, bundle, grad_second, hidden_one, normed_one, inverse_one,
-        self_slots, norms, norm_rows, halves,
+        n_mp, cross_slots, rest, home, hidden_one, cotangent.reshape(seq_len, model), norms,
+    )
+    dq_slots, cross_dk, cross_dv, layer_low, source_grad, *halves = cross_backward(
+        n_dp, n_mp, cross_query, cross_k, cross_v, cross_dmix, cross_mixed, cross_sums, out_rows, states,
+        shrink_grad, expand_grad,
     )
     flat = lambda values: values.reshape(6, rows)
     weights = [inner_weights, outer_weights, expand_weights, shrink_weights, flat(norm_params)]
     firsts = [inner_first, outer_first, expand_first, shrink_first, flat(norm_first)]
     seconds = [inner_second, outer_second, expand_second, shrink_second, flat(norm_second)]
     both, sums, grads = finish(
-        n_dp, n_mp, prefix, (self_q, self_k, self_v), self_dmix, self_mixed, self_sums, near, tokens,
-        grad_first, (cross_dk, cross_dv), rest,
-        feed_grad, cross_wo_grad, weight_grad, norm_grad, source_grad,
-        weights + firsts + seconds,
+        n_dp, n_mp, prefix, (self_q, self_k, self_v), self_mixed, self_sums, near, tokens,
+        (cross_dk, cross_dv), dq_slots, self_slots, inverse_one, norms, norm_rows, halves, bundle,
+        grad_second, hidden_one, normed_one, cross_wo_grad, source_grad, weights + firsts + seconds,
     )
     encoder_grad, input_grad, layer_out, table, *results = update(
         both, layer_low, states.shape[0], sums, grads, weights, firsts, seconds

time: 517 us -> 481 us (0.930)
  Pallas kernels: 500 us -> 464 us
    pallas_call x4 -> x2, Pallas kernels: 151 us -> 120 us  [the longest x1 61 us: cross_backward(): pl.pallas_call(partial(cross_backward_kernel, n, side), out_shape=[shape(...]
    pallas_call x1, Pallas kernels: 85.3 us -> 70.5 us  [feed(): pl.pallas_call(partial(feed_kernel, n, side), out_shape=[shape((size, mod...]
    pallas_call x1, Pallas kernels: 200 us -> 208 us  [finish(): pl.pallas_call(partial(finish_kernel, n_mp, side, units, width), out_shap...]
where the time goes in v4:
time: 481 us; the launch traced here: 476 us
  Pallas kernels  464 us (96%)
  local copies, waits for them, and re-layouts  10 us (2%)
    pallas_call x1, Pallas kernels, finish(): pl.pallas_call(partial(finish_kernel, n_mp, side, units, width), out_shap...  208 us
    pallas_call x1, Pallas kernels, feed(): pl.pallas_call(partial(feed_kernel, n, side), out_shape=[shape((size, mod...  70.5 us
    pallas_call x1, Pallas kernels, cross_backward(): pl.pallas_call(partial(cross_backward_kernel, n, side), out_shape=[shape(...  61 us
    pallas_call x1, Pallas kernels, middle(): pl.pallas_call(partial(middle_kernel, n, side), out_shape=[shape((size, m...  59.2 us
    pallas_call x1, Pallas kernels, front(): pl.pallas_call(partial(front_kernel, n_mp, side), out_shape=[shape((side,...  50.2 us
    pallas_call x1, Pallas kernels, update(): pl.pallas_call(partial(update_kernel, split), out_shape=[wide(source_rows...  14.5 us

profile of v4, /device:TPU:0, one launch (start us, length us, event | category | flops | bytes accessed | tf_op | source)
XLA Modules:
  0.0 476.4 jit_solution(12579355435833631448)
XLA Ops:
  1.3 1.7 copy.48
  3.0 0.7 convert_element_type.17
  3.7 0.1 copy.50
  3.9 0.6 pad.4.norm_ref
  4.5 1.9 copy.51
  6.4 50.2 %front.1 = (bf16[2,2,2,128,768]{4,3,2,1,0:T(8,128)(2,1)}, bf16[2,2,2,128,2688]{4,3,2,1,0:T(8,128)(2,1)}, bf16[2,2,2,128,4096]{4,3,2,1,0:T(8,128)(2,1)}, bf16[102...) custom-call(s32[1]{0:T(128)S(6)} %copy.59.prefix_ref, ...), custom_call_target="tpu_custom_call" | custom-call | flops 40000000000 | bytes 1048576 | tf_op jit(solution)/shard_map/front/pallas_call | solution.py:769
  56.6 59.2 %middle.1 = (f32[256,1024]{1,0:T(8,128)}, f32[256,1024]{1,0:T(8,128)}, f32[256,128]{1,0:T(8,128)}, f32[8,1024]{1,0:T(8,128)}, bf16[1024,256]{1,0:T(8,128)(2,1)},...) custom-call(bf16[4,256,256]{2,1,0:T(8,128)(2,1)} %get-tuple-element., ...), custom_call_target="tpu_custom_call", output_to_operand_aliasing={{10}: (3, {})} | custom-call | flops 10000000000 | bytes 1048576 | tf_op jit(solution)/shard_map/middle/pallas_call | solution.py:924
  115.8 70.5 %feed.1 = (bf16[256,1024]{1,0:T(8,128)(2,1)}, f32[256,1024]{1,0:T(8,128)}, bf16[1024,256]{1,0:T(8,128)(2,1)}, bf16[1024,2048]{1,0:T(8,128)(2,1)}, bf16[1024,2048...) custom-call(bf16[4,256,256]{2,1,0:T(8,128)(2,1)} %get-tuple-element.92.slots, ...), custom_call_target="tpu_custom_call" | custom-call | flops 80000000000 | bytes 2097152 | tf_op jit(solution)/shard_map/feed/pallas_call | solution.py:1127
  186.3 0.0 copy-start
  186.3 0.0 copy-start.1
  186.3 0.0 copy-start.2
  186.3 61.0 %cross_backward.1 = (bf16[4,256,256]{2,1,0:T(8,128)(2,1)}, bf16[2048,256]{1,0:T(8,128)(2,1)}, bf16[2048,256]{1,0:T(8,128)(2,1)}, bf16[4,256,1024]{2,1,0:T(8,128)...) custom-call(bf16[1024,256]{1,0:T(8,128)(2,1)} %get-tuple-element.89.q_ref, ...), custom_call_target="tpu_custom_call" | custom-call | flops 21474836480 | bytes 1048576 | tf_op jit(solution)/shard_map/cross_backward/pallas_call | solution.py:599
  247.3 0.0 copy-done
  247.3 0.6 reshape.109.refs_4_.refs_12_
  247.9 0.0 copy-done.1
  247.9 0.6 reshape.110.refs_9_.refs_17_
  248.6 0.0 copy-done.2
  248.6 0.6 reshape.111.refs_14_.refs_22_
  249.2 208.5 %finish.1 = (bf16[2,24,64,1024]{3,2,1,0:T(8,128)(2,1)}, f32[8,128]{1,0:T(8,128)}, f32[2,3,128,256]{3,2,1,0:T(8,128)}, f32[2,256,128]{2,1,0:T(8,128)}, f32[128,10...) custom-call(s32[1]{0:T(128)S(6)} %copy.59.prefix_ref, bf16[1024,256]{1,0:T(8,128)(2,1)} %get-tuple-element.80.q_ref, ...), custom_call_target="tpu_custom_call" | custom-call | flops 10000000000 | bytes 1048576 | tf_op jit(solution)/shard_map/finish/pallas_call | solution.py:1787
  457.6 14.5 %update.1 = (f32[2048,1024]{1,0:T(8,128)}, f32[1024,1024]{1,0:T(8,128)}, f32[1024,1024]{1,0:T(8,128)}, f32[3,16]{1,0:T(4,128)}, f32[2,3,128,256]{3,2,1,0:T(8,128...) custom-call(bf16[2,24,64,1024]{3,2,1,0:T(8,128)(2,1)} %get-tuple-ele, ...), custom_call_target="tpu_custom_call" | custom-call | tf_op jit(solution)/shard_map/update/pallas_call | solution.py:1496
  472.1 0.7 reshape.115
  472.8 0.6 copy.55
  473.4 0.7 reshape.116
  474.1 0.6 copy.56
  474.6 0.7 reshape.117
  475.3 0.6 copy.57
  (5 shorter events, 0.0 us)
Async XLA Ops:
  186.3 61.1 %copy-start = (f32[2,3,128]{2,0,1:T(2,128)S(1)}, f32[2,3,128]{2,0,1:T(2,128)}, u32[]{:S(2)}) copy-start(f32[2,3,128]{2,0,1:T(2,128)} %param.35) | copy-start | bytes 9220
  186.3 61.7 %copy-start.1 = (f32[2,3,128]{2,0,1:T(2,128)S(1)}, f32[2,3,128]{2,0,1:T(2,128)}, u32[]{:S(2)}) copy-start(f32[2,3,128]{2,0,1:T(2,128)} %param.36) | copy-start | bytes 9220
  186.3 62.3 %copy-start.2 = (f32[2,3,128]{2,0,1:T(2,128)S(1)}, f32[2,3,128]{2,0,1:T(2,128)}, u32[]{:S(2)}) copy-start(f32[2,3,128]{2,0,1:T(2,128)} %param.37) | copy-start | bytes 9220

commit v5 on v4

--- a/solution.py
+++ b/solution.py
@@ -151,46 +151,48 @@
 class Give:
     def __init__(self, place, out, sems):
         self.place, self.n, self.me, self.out = place, place.n, place.z, out
+        self.half = out.shape[1] // 2
         self.sems = {"right": sems[0:2], "left": sems[2:4]}
 
     @staticmethod
     def sems(n):
-        return [pltpu.SemaphoreType.DMA((max(n - 1, 1),))] * 4
-
-    def _copy(self, way, step):
+        return [pltpu.SemaphoreType.DMA((2 * (n - 1),))] * 4
+
+    def _copy(self, way, step, part):
         ahead = 1 if way == "right" else -1
         chunk = lax.rem(self.me - ahead * step + self.n, self.n)
+        block = self.out.at[chunk, pl.ds(part * self.half, self.half)]
         return pltpu.make_async_remote_copy(
-            self.out.at[chunk], self.out.at[chunk],
-            self.sems[way][0].at[step], self.sems[way][1].at[step],
+            block, block, self.sems[way][0].at[2 * step + part], self.sems[way][1].at[2 * step + part],
             device_id={"mp": lax.rem(self.me + ahead + self.n, self.n)}, device_id_type=MESH,
         )
 
     def _spots(self):
         return (("right", self.me), ("left", self.n - 1 - self.me))
 
-    def step(self, step):
+    def step(self, step, part):
         for way, spot in self._spots():
 
             @pl.when((spot >= step) & (spot < self.n - 1))
             def _():
                 if step > 0:
-                    self._copy(way, step - 1).wait_recv()
-                self._copy(way, step).start()
+                    self._copy(way, step - 1, part).wait_recv()
+                self._copy(way, step, part).start()
 
     def finish(self):
+        every = [(step, part) for step in range(self.n - 1) for part in range(2)]
         for way, spot in self._spots():
 
             @pl.when(spot == self.n - 1)
             def _():
-                for step in range(self.n - 1):
-                    self._copy(way, step).wait_recv()
-
-            for step in range(self.n - 1):
+                for step, part in every:
+                    self._copy(way, step, part).wait_recv()
+
+            for step, part in every:
 
                 @pl.when((spot >= step) & (spot < self.n - 1))
                 def _():
-                    self._copy(way, step).wait_send()
+                    self._copy(way, step, part).wait_send()
 
 
 class Spread:
@@ -491,9 +493,9 @@
 
 
 def cross_backward_kernel(
-    n, side, q_ref, k_ref, v_ref, do_ref, o_ref, sums_ref, mine_ref, states_ref, shrink_ref, expand_ref,
+    n, side, q_ref, k_ref, v_ref, do_ref, o_ref, sums_ref, mine_ref, states_hbm, shrink_ref, expand_ref,
     slots_ref, dk_ref, dv_ref, all_ref, source_ref, half_a_ref, half_b_ref,
-    scaled_keys, key_acc, value_acc, delta, blocks, stage, own_sem, dq_send, dq_recv, *scratch,
+    scaled_keys, key_acc, value_acc, delta, blocks, stage, states_ref, states_sem, own_sem, dq_send, dq_recv, *scratch,
 ):
     p = Place(n, side)
     give = Give(p, all_ref, scratch[:4])
@@ -504,10 +506,13 @@
     factor = HEAD**-0.5
     own = pltpu.make_async_copy(mine_ref, all_ref.at[p.z], own_sem)
     own.start()
+    states_load = pltpu.make_async_copy(states_hbm, states_ref, states_sem)
+    states_load.start()
     greet(p.line() + p.plane())
     feed_sum.core_start()
     own.wait()
-    give.step(0)
+    give.step(0, 0)
+    give.step(0, 1)
     backward_delta(do_ref, o_ref, delta)
     scaled_keys[...] = k_ref[...] * jnp.bfloat16(factor)
     key_acc[...] = jnp.zeros_like(key_acc)
@@ -535,7 +540,16 @@
         all_grads = jnp.zeros((len(heads) * size, width), jnp.float32)
         for first in range(0, k_ref.shape[0], chunk):
             rows = slice(first, first + chunk)
-            if first == chunk:
+            if first == 0:
+                for later in range(1, n):
+                    hop = divmod(later + 1, 2)
+                    if hop[0] < n - 1:
+
+                        @pl.when(step == later)
+                        def _():
+                            give.step(*hop)
+
+            if first == 2 * chunk:
 
                 @pl.when(step == 0)
                 def _():
@@ -543,11 +557,6 @@
                     feed_sum.core_finish(stage)
                     feed_sum.first_start()
 
-            if first == 2 * chunk:
-
-                @pl.when(step == 2)
-                def _():
-                    give.step(1)
 
             probs = jnp.exp(dot(scaled_keys[rows, :], own_query, NT) - row_sums)
             prob_grad = dot(v_ref[rows, :], own_grad, NT)
@@ -569,13 +578,14 @@
         return carry
 
     lax.fori_loop(0, n, one_block, 0)
+    for later in range(n + 1, 2 * (n - 1)):
+        give.step(*divmod(later, 2))
     slots_ref[p.z] = blocks[p.z]
     dk_ref[...] = bf16(key_acc[...] * factor)
     dv_ref[...] = bf16(value_acc[...])
+    states_load.wait()
     source_ref[:, :width] = bf16(dot(states_ref[...], dk_ref[...], TN))
     source_ref[:, width:] = bf16(dot(states_ref[...], dv_ref[...], TN))
-    for later in range(2, n - 1):
-        give.step(later)
     feed_sum.core_start(False)
     feed_sum.first_start(False)
     feed_sum.first_finish()
@@ -607,7 +617,7 @@
             shape(half, low),
             shape(half, low),
         ],
-        in_specs=[IN_VMEM] * 8 + [ANYWHERE] * 2,
+        in_specs=[IN_VMEM] * 7 + [ANYWHERE] * 3,
         out_specs=[IN_VMEM] * 3 + [ANYWHERE] + [IN_VMEM] * 3,
         scratch_shapes=[
             pltpu.VMEM((keys, width), low),
@@ -616,7 +626,8 @@
             pltpu.VMEM((8, total), wide),
             pltpu.VMEM((n, total // n, width), low),
             pltpu.VMEM((2, rows, columns), low),
-            dma, dma((n - 1,)), dma((n - 1,)),
+            pltpu.VMEM((keys, model), low),
+            dma, dma, dma((n - 1,)), dma((n - 1,)),
             *Give.sems(n),
             *Reduce.scratch(side, rows, columns, 2, second=False),
         ],
@@ -631,7 +642,7 @@
 
 
 def front_kernel(
-    n, side, prefix_ref, inner_ref, outer_ref, norm_ref, expand_ref, shrink_ref, x_ref,
+    n, side, prefix_ref, inner_ref, outer_in_ref, norm_in_ref, expand_ref, shrink_in_ref, x_ref, outer_ref, shrink_ref,
     near_ref, home_ref, feed_home_ref, q_ref, k_ref, v_ref, mixed_ref, sums_ref, slots_ref,
     block_near, block_line, block_rest, own_sems, near_send, near_recv, home_send, home_recv,
     line_send, line_recv, far_send, far_recv, mixed_send, mixed_recv,
@@ -640,13 +651,24 @@
     p = Place(n, side)
     width = inner_ref.shape[3]
     units = expand_ref.shape[1]
+    if outer_in_ref.shape[1] == width:
+        for index in range(2):
+            outer_ref[index] = bf16(outer_in_ref[index].T)
+        shrink_ref[...] = bf16(shrink_in_ref[...].T)
+        norm_row = jnp.concatenate(
+            [norm_in_ref[...], jnp.zeros((122, norm_in_ref.shape[1]), jnp.float32)], axis=0
+        ).T
+    else:
+        outer_ref[...] = bf16(outer_in_ref[...])
+        shrink_ref[...] = bf16(shrink_in_ref[...])
+        norm_row = norm_in_ref[...]
     for index in range(3):
         block_near[:, index * width : (index + 1) * width] = bf16(inner_ref[0, index])
     block_line[:, :width] = bf16(inner_ref[1, 0])
     block_line[:, width : 2 * width] = outer_ref[0]
     for index in range(2):
         block_rest[:, index * width : (index + 1) * width] = bf16(inner_ref[1, index + 1])
-    block_rest[:, 2 * width :] = norm_ref[...]
+    block_rest[:, 2 * width :] = bf16(norm_row)
     norms = block_rest.shape[1] - 2 * width
     whole = n * width
     later = whole + norms
@@ -756,12 +778,16 @@
     feed_spread.finish()
 
 
-def front(n_dp, n_mp, prefix, inner, outer_t, norm_t, expand, shrink_t, tokens):
+def front(n_dp, n_mp, prefix, inner, outer, norms, expand, shrink, tokens):
     rows, width = inner.shape[2:]
+    norm_columns = 128
+    if rows % 128:
+        outer, shrink = jnp.swapaxes(outer, 1, 2), shrink.T
+        norms = jnp.pad(norms.T, ((0, 0), (0, norm_columns - 6)))
     total = tokens.shape[0]
     side = round((n_dp // 2) ** 0.5)
     line = 2 * width
-    columns = n_mp * line + 2 * width + norm_t.shape[1]
+    columns = n_mp * line + 2 * width + norm_columns
     units = expand.shape[1]
     low = jnp.bfloat16
     dma = pltpu.SemaphoreType.DMA
@@ -769,6 +795,8 @@
     return pl.pallas_call(
         partial(front_kernel, n_mp, side),
         out_shape=[
+            shape((2, rows, width), low),
+            shape((rows, units), low),
             shape((side, side, 2, rows, 3 * width), low),
             shape((side, side, 2, rows, columns), low),
             shape((side, side, 2, rows, 4 * units), low),
@@ -777,11 +805,11 @@
             shape((n_mp, total // n_mp, width), low),
         ],
         in_specs=[pl.BlockSpec(memory_space=pltpu.SMEM)] + [IN_VMEM] * 6,
-        out_specs=[IN_VMEM, ANYWHERE, ANYWHERE] + [IN_VMEM] * 6,
+        out_specs=[IN_VMEM] * 3 + [ANYWHERE, ANYWHERE] + [IN_VMEM] * 6,
         scratch_shapes=[
             pltpu.VMEM((rows, 3 * width), low),
             pltpu.VMEM((rows, line), low),
-            pltpu.VMEM((rows, 2 * width + norm_t.shape[1]), low),
+            pltpu.VMEM((rows, 2 * width + norm_columns), low),
             dma((5,)),
             Spread.sems(side), Spread.sems(side), Spread.sems(side), Spread.sems(side),
             dma((2 * n_mp - 2,)), dma((2 * n_mp - 2,)), dma, dma,
@@ -794,17 +822,17 @@
         ),
         cost_estimate=pl.CostEstimate(flops=40 * 10**9, bytes_accessed=1 << 20, transcendentals=0),
         name="front",
-    )(prefix, inner, outer_t, norm_t, expand, shrink_t, tokens)
+    )(prefix, inner, outer, norms, expand, shrink, tokens)
 
 
 def middle_kernel(
-    n, side, slots_ref, bundle_ref, x_ref, home_in_ref, shrink_ref, outer_ref, states_ref,
+    n, side, slots_ref, bundle_ref, x_ref, home_in_ref, states_hbm, shrink_ref, outer_ref,
     hidden_ref, normed_ref, inverse_ref, norm_ref, q_ref, k_ref, v_ref, mixed_ref, sums_ref, cross_slots_ref,
     home_ref, rest_ref,
     wo, wq, norm_columns, source, x_rows, blocks,
     wo_sems, wq_sems, load_sems, q_send, q_recv, mixed_send, mixed_recv, far_send, far_recv,
     feed_send, feed_recv, later_send, later_recv, line_send, line_recv,
-    expand_send, expand_recv, shrink_send, shrink_recv,
+    expand_send, expand_recv, shrink_send, shrink_recv, states_ref, states_sem,
 ):
     p = Place(n, side)
     me = p.z
@@ -824,6 +852,8 @@
     ]
     for load in loads:
         load.start()
+    states_load = pltpu.make_async_copy(states_hbm, states_ref, states_sem)
+    states_load.start()
     units = home_ref.shape[4] // 4
     spot = rest_ref.at[p.y, p.x, p.core, :, pl.ds(pl.multiple_of(width * me, width), width)]
     greet(p.line() + p.plane())
@@ -873,6 +903,7 @@
     for copy in line:
         copy.wait_recv()
     rest.first()
+    states_load.wait()
     for start in range(0, states_ref.shape[0], 512):
         rows = slice(start, start + 512)
         made = bf16(dot(states_ref[rows, :], source[...]))
@@ -937,7 +968,7 @@
             shape(home.shape, low),
             shape((side, side, 2, outer_t.shape[1], n * width), low),
         ],
-        in_specs=[IN_VMEM] + [ANYWHERE] * 3 + [IN_VMEM] * 3,
+        in_specs=[IN_VMEM] + [ANYWHERE] * 4 + [IN_VMEM] * 2,
         out_specs=[IN_VMEM] * 10 + [ANYWHERE] * 2,
         input_output_aliases={3: 10},
         scratch_shapes=[
@@ -952,22 +983,23 @@
             Spread.sems(side), Spread.sems(side), Spread.sems(side), Spread.sems(side),
             dma((n - 1,)), dma((n - 1,)),
             Spread.sems(side), Spread.sems(side), Spread.sems(side), Spread.sems(side),
+            pltpu.VMEM((keys, model), low), dma,
         ],
         compiler_params=pltpu.CompilerParams(
             collective_id=1, has_side_effects=True, vmem_limit_bytes=VMEM_LIMIT
         ),
         cost_estimate=pl.CostEstimate(flops=10**10, bytes_accessed=1 << 20, transcendentals=0),
         name="middle",
-    )(slots, bundle, tokens, home, shrink_t, outer_t, states)
+    )(slots, bundle, tokens, home, states, shrink_t, outer_t)
 
 
 def feed_kernel(
     n, side, slots, rest_ref, home_ref, hidden_one_ref, cot_ref, norm_ref,
-    out_ref, second_ref, dmix_ref, shrink_grad_ref, expand_grad_ref, wo_grad_ref, norm_grad_ref,
+    out_ref, second_ref, dmix_ref, shrink_grad_hbm, expand_grad_hbm, wo_grad_ref, norm_grad_ref,
     wo, weights, hidden_two, normed_two, low_two, low_three, act, slope,
     y_own, y_send, y_recv, d_send, d_recv, cot, blocks,
     load_sem, wo_sems, own_sem, send_out, recv_out, pair_send, pair_recv,
-    home_sems, home_send, home_recv,
+    home_sems, home_send, home_recv, shrink_grad_ref, expand_grad_ref, grad_sems,
 ):
     p = Place(n, side)
     me = p.z
@@ -1104,16 +1136,27 @@
     norm_grad_ref[...] = jnp.concatenate(
         [gain_two, gain_three, bias_two, bias_three, jnp.zeros((4, norm_grad_ref.shape[1]))], axis=0
     )
+    stores = []
     for first in range(0, low_two.shape[1], 256):
         rows = slice(first, first + 256)
         shrink_grad_ref[rows, :] = bf16(dot(low_three[:, rows], act[...], TN))
         expand_grad_ref[rows, :] = bf16(dot(low_two[:, rows], slope[...], TN))
+        for index, (made, target) in enumerate(
+            ((shrink_grad_ref, shrink_grad_hbm), (expand_grad_ref, expand_grad_hbm))
+        ):
+            span = pl.ds(first, 256)
+            stores.append(
+                pltpu.make_async_copy(made.at[span], target.at[span], grad_sems.at[index, first // 256])
+            )
+            stores[-1].start()
     for group in range(n):
         wo_grad_ref[:, group * width : (group + 1) * width] = bf16(dot(low, slots[group], TN))
     for copy in sent:
         copy.wait()
     for copy in pair + home_copies:
         copy.wait_send()
+    for store in stores:
+        store.wait()
 
 
 def feed(n, slots, rest, home, hidden_one, cotangent, norms):
@@ -1136,7 +1179,7 @@
             shape((8, model), wide),
         ],
         in_specs=[IN_VMEM, ANYWHERE, ANYWHERE, IN_VMEM, ANYWHERE, IN_VMEM],
-        out_specs=[IN_VMEM] * 2 + [ANYWHERE] + [IN_VMEM] * 4,
+        out_specs=[IN_VMEM] * 2 + [ANYWHERE] * 3 + [IN_VMEM] * 2,
         scratch_shapes=[
             pltpu.VMEM((n, model, width), low),
             pltpu.VMEM((model, 2 * units), low),
@@ -1157,6 +1200,7 @@
             dma((n - 1,)), dma((n - 1,)),
             dma((8,)), dma((8,)),
             dma((side * side,)), dma((side * side,)), dma((side * side,)),
+            pltpu.VMEM((model, units), low), pltpu.VMEM((model, units), low), dma((2, model // 256)),
         ],
         compiler_params=pltpu.CompilerParams(
             collective_id=2, has_side_effects=True, vmem_limit_bytes=VMEM_LIMIT
@@ -1512,14 +1556,14 @@
 
 
 def finish_kernel(
-    n, side, units, width, prefix_ref, q_ref, k_ref, v_ref, o_ref, row_sums_ref,
-    near_ref, x_ref, cross_dk_ref, cross_dv_ref, dq_slots_ref, mixed_slots_ref, inverse_ref, norms_ref, norm_rows_ref,
+    n, side, units, width, prefix_ref, q_hbm, k_hbm, v_hbm, o_hbm, row_sums_ref,
+    near_hbm, x_hbm, cross_dk_ref, cross_dv_ref, dq_slots_ref, mixed_slots_ref, inverse_ref, norms_ref, norm_rows_ref,
     half_a_ref, half_b_ref, bundle_ref, second_hbm, hidden_hbm, normed_hbm, cross_wo_ref, source_grad_ref, *refs,
 ):
     states, refs = refs[:15], refs[15:]
     out_ref, sums_ref, grads, refs = refs[0], refs[1], refs[2:7], refs[7:]
     (
-        source_ref, source_sem, do_ref, first_ref, feed_ref, weight_ref, blocks, early_sems, group_sem,
+        q_ref, k_ref, v_ref, o_ref, near_ref, x_ref, late_sems, source_ref, source_sem, do_ref, first_ref, feed_ref, weight_ref, blocks, early_sems, group_sem,
         own_sem, send_out, recv_out, dq_ref, dk_ref, dv_ref, query_acc, delta, master_sems, inner, stage, far_recv, group_send,
         far_send_sem, far_recv_sem, mine, slots, everyone_send, everyone_recv, *scratch,
     ) = refs
@@ -1562,6 +1606,14 @@
         bundle_ref.at[:, :, :, :, pl.ds(2 * n * width + 128, 2 * width)], source_ref, source_sem
     )
     source_load.start()
+    late_loads = [
+        pltpu.make_async_copy(source, target, late_sems.at[index])
+        for index, (source, target) in enumerate(
+            zip((q_hbm, k_hbm, v_hbm, o_hbm, near_hbm, x_hbm), (q_ref, k_ref, v_ref, o_ref, near_ref, x_ref))
+        )
+    ]
+    for load in late_loads:
+        load.start()
     weight_loads = [
         pltpu.make_async_copy(
             bundle_ref.at[:, :, :, :, pl.ds(start, n * width)],
@@ -1653,6 +1705,8 @@
     advance(1)
     weight_sum.core_finish(stage)
     weight_sum.first_start()
+    for load in late_loads:
+        load.wait()
     backward_delta(do_ref, o_ref, delta)
     query_acc[...] = jnp.zeros_like(query_acc)
     key_block = 256
@@ -1789,10 +1843,17 @@
         out_shape=[shape((2, chunks, chunk_rows, model), low), shape((8, 128), wide)]
         + [shape(values.shape, wide) for values in states[:5]],
         in_specs=[pl.BlockSpec(memory_space=pltpu.SMEM)]
-        + [IN_VMEM] * 16
+        + [ANYWHERE] * 4
+        + [IN_VMEM]
+        + [ANYWHERE] * 2
+        + [IN_VMEM] * 9
         + [ANYWHERE] * (6 + len(states)),
         out_specs=[ANYWHERE] + [IN_VMEM] * 6,
         scratch_shapes=[
+            *[pltpu.VMEM((total, width), low)] * 4,
+            pltpu.VMEM(near.shape, low),
+            pltpu.VMEM(tokens.shape, low),
+            dma((6,)),
             pltpu.VMEM((side, side, 2, rows, 2 * width), low),
             dma,
             pltpu.VMEM((total, width), low),
@@ -1860,11 +1921,9 @@
     rows, width = inner_weights.shape[2:]
     units = expand_weights.shape[1]
 
-    norm_t = jnp.pad(bf16(norm_params).reshape(6, rows).T, ((0, 0), (0, 122)))
-    outer_t = bf16(jnp.swapaxes(outer_weights, 1, 2))
-    shrink_t = bf16(shrink_weights.T)
-    near, bundle, home, self_q, self_k, self_v, self_mixed, self_sums, self_slots = front(
-        n_dp, n_mp, prefix, inner_weights, outer_t, norm_t, expand_weights, shrink_t, tokens
+    flat = lambda values: values.reshape(6, rows)
+    outer_t, shrink_t, near, bundle, home, self_q, self_k, self_v, self_mixed, self_sums, self_slots = front(
+        n_dp, n_mp, prefix, inner_weights, outer_weights, flat(norm_params), expand_weights, shrink_weights, tokens
     )
     by_rows = lambda values: values.reshape(model, values.shape[-1])
     near, bundle = by_rows(near), by_rows(bundle)
@@ -1880,7 +1939,6 @@
         n_dp, n_mp, cross_query, cross_k, cross_v, cross_dmix, cross_mixed, cross_sums, out_rows, states,
         shrink_grad, expand_grad,
     )
-    flat = lambda values: values.reshape(6, rows)
     weights = [inner_weights, outer_weights, expand_weights, shrink_weights, flat(norm_params)]
     firsts = [inner_first, outer_first, expand_first, shrink_first, flat(norm_first)]
     seconds = [inner_second, outer_second, expand_second, shrink_second, flat(norm_second)]

time: 481 us -> 461 us (0.958)
  Pallas kernels: 464 us -> 448 us
    pallas_call x1, Pallas kernels: 61 us -> 54.4 us  [cross_backward(): pl.pallas_call(partial(cross_backward_kernel, n, side), out_shape=[shape(...]
    pallas_call x1, Pallas kernels: 208 us -> 203 us  [finish(): pl.pallas_call(partial(finish_kernel, n_mp, side, units, width), out_shap...]
where the time goes in v5:
time: 461 us; the launch traced here: 456 us
  Pallas kernels  448 us (97%)
  local copies, waits for them, and re-layouts  6.3 us (1%)
    pallas_call x1, Pallas kernels, finish(): pl.pallas_call(partial(finish_kernel, n_mp, side, units, width), out_shap...  203 us
    pallas_call x1, Pallas kernels, feed(): pl.pallas_call(partial(feed_kernel, n, side), out_shape=[shape((size, mod...  67.8 us
    pallas_call x1, Pallas kernels, middle(): pl.pallas_call(partial(middle_kernel, n, side), out_shape=[shape((size, m...  57.9 us
    pallas_call x1, Pallas kernels, cross_backward(): pl.pallas_call(partial(cross_backward_kernel, n, side), out_shape=[shape(...  54.4 us
    pallas_call x1, Pallas kernels, front(): pl.pallas_call(partial(front_kernel, n_mp, side), out_shape=[shape((2, ro...  50.5 us
    pallas_call x1, Pallas kernels, update(): pl.pallas_call(partial(update_kernel, split), out_shape=[wide(source_rows...  14.5 us

profile of v5, /device:TPU:0, one launch (start us, length us, event | category | flops | bytes accessed | tf_op | source)
XLA Modules:
  0.0 456.3 jit_solution(429888881581648781)
XLA Ops:
  1.3 0.7 copy.45
  2.0 0.6 reshape.96.norm_in_ref.refs_4_.refs_12_
  2.6 50.5 %front.1 = (bf16[2,128,256]{2,1,0:T(8,128)(2,1)}, bf16[128,1024]{1,0:T(8,128)(2,1)}, bf16[2,2,2,128,768]{4,3,2,1,0:T(8,128)(2,1)}, bf16[2,2,2,128,2688]{4,3,2,1,...) custom-call(s32[1]{0:T(128)S(6)} %copy.52.prefix_ref, ...), custom_call_target="tpu_custom_call" | custom-call | flops 40000000000 | bytes 1048576 | tf_op jit(solution)/shard_map/front/pallas_call | solution.py:795
  53.1 57.9 %middle.1 = (f32[256,1024]{1,0:T(8,128)}, f32[256,1024]{1,0:T(8,128)}, f32[256,128]{1,0:T(8,128)}, f32[8,1024]{1,0:T(8,128)}, bf16[1024,256]{1,0:T(8,128)(2,1)},...) custom-call(bf16[4,256,256]{2,1,0:T(8,128)(2,1)} %get-tuple-element., ...), custom_call_target="tpu_custom_call", output_to_operand_aliasing={{10}: (3, {})} | custom-call | flops 10000000000 | bytes 1048576 | tf_op jit(solution)/shard_map/middle/pallas_call | solution.py:955
  111.0 67.8 %feed.1 = (bf16[256,1024]{1,0:T(8,128)(2,1)}, f32[256,1024]{1,0:T(8,128)}, bf16[1024,256]{1,0:T(8,128)(2,1)}, bf16[1024,2048]{1,0:T(8,128)(2,1)}, bf16[1024,2048...) custom-call(bf16[4,256,256]{2,1,0:T(8,128)(2,1)} %get-tuple-element.96.slots, ...), custom_call_target="tpu_custom_call" | custom-call | flops 80000000000 | bytes 2097152 | tf_op jit(solution)/shard_map/feed/pallas_call | solution.py:1170
  178.9 0.0 copy-start
  178.9 0.0 copy-start.1
  178.9 54.4 %cross_backward.1 = (bf16[4,256,256]{2,1,0:T(8,128)(2,1)}, bf16[2048,256]{1,0:T(8,128)(2,1)}, bf16[2048,256]{1,0:T(8,128)(2,1)}, bf16[4,256,1024]{2,1,0:T(8,128)...) custom-call(bf16[1024,256]{1,0:T(8,128)(2,1)} %get-tuple-element.93.q_ref, ...), custom_call_target="tpu_custom_call" | custom-call | flops 21474836480 | bytes 1048576 | tf_op jit(solution)/shard_map/cross_backward/pallas_call | solution.py:609
  233.3 0.0 copy-done
  233.3 0.6 reshape.107.refs_9_.refs_17_
  233.9 0.0 copy-done.1
  233.9 0.6 reshape.108.refs_14_.refs_22_
  234.5 203.0 %finish.1 = (bf16[2,24,64,1024]{3,2,1,0:T(8,128)(2,1)}, f32[8,128]{1,0:T(8,128)}, f32[2,3,128,256]{3,2,1,0:T(8,128)}, f32[2,256,128]{2,1,0:T(8,128)}, f32[128,10...) custom-call(s32[1]{0:T(128)S(6)} %copy.52.prefix_ref, bf16[1024,256]{1,0:T(8,128)(2,1)} %get-tuple-element.82.q_hbm, ...), custom_call_target="tpu_custom_call" | custom-call | flops 10000000000 | bytes 1048576 | tf_op jit(solution)/shard_map/finish/pallas_call | solution.py:1841
  437.5 14.5 %update.1 = (f32[2048,1024]{1,0:T(8,128)}, f32[1024,1024]{1,0:T(8,128)}, f32[1024,1024]{1,0:T(8,128)}, f32[3,16]{1,0:T(4,128)}, f32[2,3,128,256]{3,2,1,0:T(8,128...) custom-call(bf16[2,24,64,1024]{3,2,1,0:T(8,128)(2,1)} %get-tuple-ele, ...), custom_call_target="tpu_custom_call" | custom-call | tf_op jit(solution)/shard_map/update/pallas_call | solution.py:1540
  452.0 0.7 reshape.112
  452.7 0.6 copy.48
  453.3 0.7 reshape.113
  454.0 0.6 copy.49
  454.5 0.7 reshape.114
  455.2 0.6 copy.50
  (2 shorter events, 0.0 us)
Async XLA Ops:
  178.9 54.4 %copy-start = (f32[2,3,128]{2,0,1:T(2,128)S(1)}, f32[2,3,128]{2,0,1:T(2,128)}, u32[]{:S(2)}) copy-start(f32[2,3,128]{2,0,1:T(2,128)} %param.36) | copy-start | bytes 9220
  178.9 55.0 %copy-start.1 = (f32[2,3,128]{2,0,1:T(2,128)S(1)}, f32[2,3,128]{2,0,1:T(2,128)}, u32[]{:S(2)}) copy-start(f32[2,3,128]{2,0,1:T(2,128)} %param.37) | copy-start | bytes 9220

commit v6 on v5

--- a/solution.py
+++ b/solution.py
@@ -549,7 +549,7 @@
                         def _():
                             give.step(*hop)
 
-            if first == 2 * chunk:
+            if first == 3 * chunk:
 
                 @pl.when(step == 0)
                 def _():

time: 461 us -> 460 us (level)
  no operation moved by 1% of the time
where the time goes in v6:
time: 460 us; the launch traced here: 456 us
  Pallas kernels  448 us (97%)
  local copies, waits for them, and re-layouts  6.3 us (1%)
    pallas_call x1, Pallas kernels, finish(): pl.pallas_call(partial(finish_kernel, n_mp, side, units, width), out_shap...  203 us
    pallas_call x1, Pallas kernels, feed(): pl.pallas_call(partial(feed_kernel, n, side), out_shape=[shape((size, mod...  67.8 us
    pallas_call x1, Pallas kernels, middle(): pl.pallas_call(partial(middle_kernel, n, side), out_shape=[shape((size, m...  57.9 us
    pallas_call x1, Pallas kernels, cross_backward(): pl.pallas_call(partial(cross_backward_kernel, n, side), out_shape=[shape(...  54.6 us
    pallas_call x1, Pallas kernels, front(): pl.pallas_call(partial(front_kernel, n_mp, side), out_shape=[shape((2, ro...  50.5 us
    pallas_call x1, Pallas kernels, update(): pl.pallas_call(partial(update_kernel, split), out_shape=[wide(source_rows...  14.5 us

profile of v6, /device:TPU:0, one launch (start us, length us, event | category | flops | bytes accessed | tf_op | source)
XLA Modules:
  0.0 456.2 jit_solution(5753676318874921577)
XLA Ops:
  1.3 0.7 copy.45
  2.0 0.6 reshape.96.norm_in_ref.refs_4_.refs_12_
  2.6 50.5 %front.1 = (bf16[2,128,256]{2,1,0:T(8,128)(2,1)}, bf16[128,1024]{1,0:T(8,128)(2,1)}, bf16[2,2,2,128,768]{4,3,2,1,0:T(8,128)(2,1)}, bf16[2,2,2,128,2688]{4,3,2,1,...) custom-call(s32[1]{0:T(128)S(6)} %copy.52.prefix_ref, ...), custom_call_target="tpu_custom_call" | custom-call | flops 40000000000 | bytes 1048576 | tf_op jit(solution)/shard_map/front/pallas_call | solution.py:795
  53.1 57.9 %middle.1 = (f32[256,1024]{1,0:T(8,128)}, f32[256,1024]{1,0:T(8,128)}, f32[256,128]{1,0:T(8,128)}, f32[8,1024]{1,0:T(8,128)}, bf16[1024,256]{1,0:T(8,128)(2,1)},...) custom-call(bf16[4,256,256]{2,1,0:T(8,128)(2,1)} %get-tuple-element., ...), custom_call_target="tpu_custom_call", output_to_operand_aliasing={{10}: (3, {})} | custom-call | flops 10000000000 | bytes 1048576 | tf_op jit(solution)/shard_map/middle/pallas_call | solution.py:955
  111.0 67.8 %feed.1 = (bf16[256,1024]{1,0:T(8,128)(2,1)}, f32[256,1024]{1,0:T(8,128)}, bf16[1024,256]{1,0:T(8,128)(2,1)}, bf16[1024,2048]{1,0:T(8,128)(2,1)}, bf16[1024,2048...) custom-call(bf16[4,256,256]{2,1,0:T(8,128)(2,1)} %get-tuple-element.96.slots, ...), custom_call_target="tpu_custom_call" | custom-call | flops 80000000000 | bytes 2097152 | tf_op jit(solution)/shard_map/feed/pallas_call | solution.py:1170
  178.9 0.0 copy-start
  178.9 0.0 copy-start.1
  178.9 54.6 %cross_backward.1 = (bf16[4,256,256]{2,1,0:T(8,128)(2,1)}, bf16[2048,256]{1,0:T(8,128)(2,1)}, bf16[2048,256]{1,0:T(8,128)(2,1)}, bf16[4,256,1024]{2,1,0:T(8,128)...) custom-call(bf16[1024,256]{1,0:T(8,128)(2,1)} %get-tuple-element.93.q_ref, ...), custom_call_target="tpu_custom_call" | custom-call | flops 21474836480 | bytes 1048576 | tf_op jit(solution)/shard_map/cross_backward/pallas_call | solution.py:609
  233.5 0.0 copy-done
  233.5 0.6 reshape.107.refs_9_.refs_17_
  234.1 0.0 copy-done.1
  234.1 0.6 reshape.108.refs_14_.refs_22_
  234.7 202.7 %finish.1 = (bf16[2,24,64,1024]{3,2,1,0:T(8,128)(2,1)}, f32[8,128]{1,0:T(8,128)}, f32[2,3,128,256]{3,2,1,0:T(8,128)}, f32[2,256,128]{2,1,0:T(8,128)}, f32[128,10...) custom-call(s32[1]{0:T(128)S(6)} %copy.52.prefix_ref, bf16[1024,256]{1,0:T(8,128)(2,1)} %get-tuple-element.82.q_hbm, ...), custom_call_target="tpu_custom_call" | custom-call | flops 10000000000 | bytes 1048576 | tf_op jit(solution)/shard_map/finish/pallas_call | solution.py:1841
  437.4 14.5 %update.1 = (f32[2048,1024]{1,0:T(8,128)}, f32[1024,1024]{1,0:T(8,128)}, f32[1024,1024]{1,0:T(8,128)}, f32[3,16]{1,0:T(4,128)}, f32[2,3,128,256]{3,2,1,0:T(8,128...) custom-call(bf16[2,24,64,1024]{3,2,1,0:T(8,128)(2,1)} %get-tuple-ele, ...), custom_call_target="tpu_custom_call" | custom-call | tf_op jit(solution)/shard_map/update/pallas_call | solution.py:1540
  451.9 0.7 reshape.112
  452.6 0.6 copy.48
  453.1 0.7 reshape.113
  453.8 0.6 copy.49
  454.4 0.7 reshape.114
  455.1 0.6 copy.50
  (2 shorter events, 0.0 us)
Async XLA Ops:
  178.9 54.7 %copy-start = (f32[2,3,128]{2,0,1:T(2,128)S(1)}, f32[2,3,128]{2,0,1:T(2,128)}, u32[]{:S(2)}) copy-start(f32[2,3,128]{2,0,1:T(2,128)} %param.36) | copy-start | bytes 9220
  178.9 55.3 %copy-start.1 = (f32[2,3,128]{2,0,1:T(2,128)S(1)}, f32[2,3,128]{2,0,1:T(2,128)}, u32[]{:S(2)}) copy-start(f32[2,3,128]{2,0,1:T(2,128)} %param.37) | copy-start | bytes 9220
